TPU v7x, 32 devices: a whole 2x2x4 slice. The times are simulated.
32 devices in a mesh: seq: 16 (over z, y, x), head: 2 (over core).
Axes of the slice: x: 2, y: 2, z: 4, core: 2. Of those that a mesh axis runs over, the one named last changes fastest.
Arguments:
- act: bfloat16 [8192, 4608], P('seq', 'head'), may hold values from -6 to 6
- query_rows: bfloat16 [8192, 2048], P('seq', 'head'), may hold values from -6 to 6
- key_rows: bfloat16 [8192, 1024], P('seq', 'head'), may hold values from -6 to 6
- out_adjoint: bfloat16 [8192, 2048], P('seq', 'head'), may hold values from -0.59765625 to 0.59765625
- basis_input: bfloat16 [4608, 4608], P('seq', 'head'), may hold values from -0.09375 to 0.09375
- basis_grad: bfloat16 [8, 128, 128], P('head'), may hold values from -0.5 to 0.5
- eigvals: bfloat16 [4608, 1024], P('head'), may hold values from 0.0019 to 30.5, as said below
- query_act: bfloat16 [64, 4608], P(None, 'head'), may hold values from -6 to 6
- query_adj: bfloat16 [64, 1024], P(None, 'head'), may hold values from -6 to 6
Outputs:
- influence: float32 [8192], P('seq')
Inputs may be any that keep to these rules, and one draw needn't show every extreme that they name: eigvals are positive.
All inputs are finite; a program needn't handle non-finite values.
Results may differ from a plain program's by a relative error of at most 0.018.
Values may be sent and summed in bfloat16 or wider, within the bound.
A program may use at most 192 MiB of HBM per device.

v0:
```python
import jax
import jax.numpy as jnp
from jax import lax
from jax.sharding import PartitionSpec as P

WINDOW = 4096


SCORE_SCALE = 1.0 / 12.0
SOFT_CAP = 50.0
DAMP_FACTOR = 0.1


def shifted(value, axis, by):
    size = lax.axis_size(axis)
    pairs = [(i, i + by) for i in range(size) if 0 <= i + by < size]
    return lax.ppermute(value, axis, pairs)


def attend(query_head, key_head, adjoint_head, seq_index, key_span):
    local_rows = query_head.shape[0]
    raw = (
        jnp.einsum("ad,otd->aot", query_head, key_head, preferred_element_type=jnp.float32)
        * SCORE_SCALE
    )
    capped = SOFT_CAP * jnp.tanh(raw / SOFT_CAP)
    query_pos = seq_index * local_rows + jnp.arange(local_rows, dtype=jnp.int32)
    offsets = jnp.arange(key_span + 1, dtype=jnp.int32)
    key_pos = (seq_index - offsets)[:, None] * local_rows + jnp.arange(local_rows, dtype=jnp.int32)[
        None, :
    ]
    gap_pos = query_pos[:, None, None] - key_pos[None, :, :]
    valid = (key_pos[None, :, :] >= 0) & (gap_pos >= 0) & (gap_pos < WINDOW)
    weights = jnp.where(valid, jnp.exp(capped), jnp.zeros_like(capped))
    totals = jnp.sum(weights, axis=(1, 2), keepdims=True)
    probs = (weights / totals).astype(jnp.bfloat16)
    return jnp.einsum("aot,ad->otd", probs, adjoint_head, preferred_element_type=jnp.float32)


def rotate_heads(matrix, basis_grad):
    row_count = matrix.shape[0]
    split_heads = matrix.reshape(row_count, basis_grad.shape[0], basis_grad.shape[1])
    turned = jnp.einsum("the,hef->thf", split_heads, basis_grad, preferred_element_type=jnp.float32)
    return turned.reshape(row_count, -1).astype(jnp.bfloat16)


def on_device(
    act, query_rows, key_rows, out_adjoint, basis_input, basis_grad, eigvals, query_act, query_adj
):
    local_rows = act.shape[0]
    heads_here = basis_grad.shape[0]
    head_width = basis_grad.shape[1]
    key_span = WINDOW // local_rows
    seq_index = lax.axis_index("seq")
    stacked = key_rows[None]
    for bit_pos in range(key_span.bit_length() - 1):
        moved = shifted(stacked, "seq", 1 << bit_pos)
        stacked = jnp.concatenate([stacked, moved], axis=0)
    farthest = shifted(key_rows, "seq", key_span)
    key_stack = jnp.concatenate([stacked, farthest[None]], axis=0)
    pieces = []
    for head_pos in range(heads_here):
        lower = head_pos * head_width
        key_head = key_stack[:, :, lower : lower + head_width]
        group_sum = None
        for member in range(2):
            q_lower = (2 * head_pos + member) * head_width
            q_upper = q_lower + head_width
            term = attend(
                query_rows[:, q_lower:q_upper],
                key_head,
                out_adjoint[:, q_lower:q_upper],
                seq_index,
                key_span,
            )
            group_sum = term if group_sum is None else group_sum + term
        pieces.append(group_sum.astype(jnp.bfloat16))
    partials = jnp.concatenate(pieces, axis=2)
    adjoint_sum = partials[0].astype(jnp.float32)
    for offset in range(1, key_span + 1):
        arrived = shifted(partials[offset], "seq", -offset)
        adjoint_sum = adjoint_sum + arrived.astype(jnp.float32)
    value_adjoint = adjoint_sum.astype(jnp.bfloat16)
    turned_tokens = rotate_heads(value_adjoint, basis_grad)
    turned_query = rotate_heads(query_adj, basis_grad)
    all_turned, all_query_turned = (
        lax.all_gather(turned_tokens, "head", axis=1, tiled=True),
        lax.all_gather(turned_query, "head", axis=1, tiled=True),
    )
    full_act, full_query_act = (
        lax.all_gather(act, "head", axis=1, tiled=True),
        lax.all_gather(query_act, "head", axis=1, tiled=True),
    )
    piece = lax.all_gather(basis_input, "seq", axis=0, tiled=True)
    rotated_tokens = jnp.dot(full_act, piece, preferred_element_type=jnp.float32)
    rotated_query = jnp.dot(full_query_act, piece, preferred_element_type=jnp.float32)
    rotated_tokens = rotated_tokens.astype(jnp.bfloat16)
    rotated_query = rotated_query.astype(jnp.bfloat16)
    query_grad = (
        jnp.dot(rotated_query.T, all_query_turned, preferred_element_type=jnp.float32)
        / query_act.shape[0]
    )
    local_total = jnp.sum(eigvals, dtype=jnp.float32)
    eigen_total = lax.psum(local_total, "head")
    damping = (
        DAMP_FACTOR * eigen_total / (eigvals.shape[0] * lax.axis_size("head") * eigvals.shape[1])
    )
    scaled = (query_grad / (eigvals.astype(jnp.float32) + damping)).astype(jnp.bfloat16)
    mapped = jnp.dot(rotated_tokens, scaled, preferred_element_type=jnp.float32)
    partial_score = jnp.sum(mapped * all_turned.astype(jnp.float32), axis=1)
    return lax.psum(partial_score, "head")


def solution(mesh):
    return jax.shard_map(
        on_device,
        mesh=mesh,
        in_specs=(
            P("seq", "head"),
            P("seq", "head"),
            P("seq", "head"),
            P("seq", "head"),
            P("seq", "head"),
            P("head", None, None),
            P("head", None),
            P(None, "head"),
            P(None, "head"),
        ),
        out_specs=P("seq"),
        check_vma=False,
    )
```

profile of v0, /device:TPU:5, one launch (start us, length us, event | category | flops | bytes accessed | tf_op | source)
XLA Modules:
  0.0 496.6 jit_solution(10714825756387201183)
XLA Ops:
  8.1 3.1 collective-permute-start
  11.2 12.7 %collective-permute-done = bf16[1,512,512]{2,1,0:T(8,128)(2,1)S(1)} collective-permute-done((bf16[1,512,512]{2,1,0:T(8,128)(2,1)}, bf16[1,512,512]{2,1,0:T(8,128)(2,1)S(1)}, u32[]{:S(2)}, u32[]{:S(2)}) %collective-permute-start) | collective-permute-done | bytes 524320 | tf_op jit(solution)/shard_map/ppermute | solution.py:17
  25.0 4.0 collective-permute-start.1
  29.1 31.2 %collective-permute-done.1 = bf16[2,512,512]{2,1,0:T(8,128)(2,1)S(1)} collective-permute-done((bf16[2,512,512]{2,1,0:T(8,128)(2,1)S(1)}, bf16[2,512,512]{2,1,0:T(8,128)(2,1)S(1)}, u32[]{:S(2)}, u32[]{:S(2)}) %collective-permute-start.1) | collective-permute-done | bytes 1048608 | tf_op jit(solution)/shard_map/ppermute | solution.py:17
  60.3 2.6 pad_maximum_fusion.1
  62.9 12.3 %collective-permute-start.2 = (bf16[4,512,512]{2,1,0:T(8,128)(2,1)}, bf16[4,512,512]{2,1,0:T(8,128)(2,1)}, u32[]{:S(2)}, u32[]{:S(2)}) collective-permute-start(bf16[4,512,512]{2,1,0:T(8,128)(2,1)} %pad_maximum_fusion.1), channel_id=1, source_target_pairs={{0,8},{2,10},{4,12},{6,14},{8,16},{10,18},{12,20},{14,22},{16,24},... | collective-permute-start | bytes 6291464 | tf_op jit(solution)/shard_map/ppermute | solution.py:17
  75.2 5.5 %collective-permute-start.3 = (bf16[512,512]{1,0:T(8,128)(2,1)S(1)}, bf16[512,512]{1,0:T(8,128)(2,1)}, u32[]{:S(2)}, u32[]{:S(2)}) collective-permute-start(bf16[512,512]{1,0:T(8,128)(2,1)S(1)} %copy-done.4), channel_id=1, source_target_pairs={{0,16},{2,18},{4,20},{6,22},{8,24},{10,26},{12,28},{14,30},{1,17},... | collective-permute-start | bytes 1572872 | tf_op jit(solution)/shard_map/ppermute | solution.py:17
  81.0 66.4 %collective-permute-done.2 = bf16[4,512,512]{2,1,0:T(8,128)(2,1)} collective-permute-done((bf16[4,512,512]{2,1,0:T(8,128)(2,1)}, bf16[4,512,512]{2,1,0:T(8,128)(2,1)}, u32[]{:S(2)}, u32[]{:S(2)}) %collective-permute-start.2) | collective-permute-done | bytes 2097184 | tf_op jit(solution)/shard_map/ppermute | solution.py:17
  147.4 1.7 constant_dynamic-update-slice_fusion
  149.1 20.6 %collective-permute-done.3 = bf16[512,512]{1,0:T(8,128)(2,1)} collective-permute-done((bf16[512,512]{1,0:T(8,128)(2,1)S(1)}, bf16[512,512]{1,0:T(8,128)(2,1)}, u32[]{:S(2)}, u32[]{:S(2)}) %collective-permute-start.3) | collective-permute-done | bytes 524320 | tf_op jit(solution)/shard_map/ppermute | solution.py:17
  170.8 1.4 fusion.30
  172.2 5.1 %fusion.32 = f32[9,512,512]{2,1,0:T(8,128)} fusion(bf16[9,512,512]{2,1,0:T(8,128)(2,1)S(1)} %bitcast_dynamic-update-slice_fusion, bf16[512,1024]{1,0:T(8,128)(2,1)S(1)} %copy-done.5), kind=kOutput, calls=%fused_computation.65 | convolution fusion | flops 603979776 | bytes 10747904 | tf_op jit(solution)/shard_map/ad,otd->aot/dot_general | solution.py:23
  177.3 1.4 fusion.34
  178.7 5.0 fusion.36
  183.7 5.0 fusion.38
  188.6 5.0 %fusion.40 = f32[9,512,512]{2,1,0:T(8,128)} fusion(bf16[9,512,512]{2,1,0:T(8,128)(2,1)S(1)} %bitcast_dynamic-update-slice_fusion, bf16[512,1024]{1,0:T(8,128)(2,1)S(1)} %copy-done.5), kind=kOutput, calls=%fused_computation.73 | convolution fusion | flops 603979776 | bytes 10747904 | tf_op jit(solution)/shard_map/ad,otd->aot/dot_general | solution.py:23
  193.6 5.0 %fusion.44 = f32[9,512,512]{2,1,0:T(8,128)} fusion(bf16[9,512,512]{2,1,0:T(8,128)(2,1)S(1)} %bitcast_dynamic-update-slice_fusion, bf16[512,1024]{1,0:T(8,128)(2,1)S(1)} %copy-done.5), kind=kOutput, calls=%fused_computation.77 | convolution fusion | flops 603979776 | bytes 10747904 | tf_op jit(solution)/shard_map/ad,otd->aot/dot_general | solution.py:23
  198.6 27.9 %fusion.5 = (f32[512]{0:T(512)S(1)}, f32[512]{0:T(512)S(1)}, f32[512]{0:T(512)S(1)}, f32[512]{0:T(512)S(1)}, f32[512]{0:T(512)S(1)}, /*index=5*/f32[512]{0:T(512...) fusion(s32[9,512]{1,0:T(8,128)S(1)} %iota_add_fusion, s32[512]{0:T(512)S(1)} %iota_add_fusion.1, ...), kind=kOutput, calls=%fused_computation.25 | convolution fusion | flops 691269632 | bytes 76867584 | tf_op jit(solution)/shard_map/ad,otd->aot/dot_general | solution.py:23
  226.6 10.4 %fusion.12 = f32[9,512,128]{1,2,0:T(8,128)} fusion(f32[9,512,512]{2,1,0:T(8,128)} %fusion.44, f32[512]{0:T(512)S(1)} %get-tuple-element.12, bf16[512,1024]{1,0:T(8,128)(2,1)} %param.12, s32[9,512]{1,0:T(8,128)S(1)} %iota_add_fusion, s32[512]{0:T(512)S(1)} %iota_add_fusion.1, pred[9,512]{1,0:T(8,128)(4,1)S(1)} %broadcast_compare_fusion), kind=kOutput, calls=%fused_computation.33 | convolution fusion | flops 627572736 | bytes 11954688 | tf_op jit(solution)/shard_map/aot,ad->otd/dot_general | solution.py:37
  237.0 5.5 %fusion.14 = f32[9,512,128]{1,2,0:T(8,128)S(1)} fusion(f32[9,512,512]{2,1,0:T(8,128)S(1)} %copy-done.3, f32[512]{0:T(512)S(1)} %get-tuple-element.6, bf16[512,1024]{1,0:T(8,128)(2,1)S(1)} %copy-done.7, s32[9,512]{1,0:T(8,128)S(1)} %iota_add_fusion, s32[512]{0:T(512)S(1)} %iota_add_fusion.1, pred[9,512]{1,0:T(8,128)(4,1)S(1)} %broadcast_compare_fusion), kind=kOutput, calls=%fused_computation.35 | convolution fusion | flops 627572736 | bytes 11972608 | tf_op jit(solution)/shard_map/aot,ad->otd/dot_general | solution.py:37
  242.5 11.1 %fusion.16 = f32[9,512,128]{1,2,0:T(8,128)S(1)} fusion(f32[9,512,512]{2,1,0:T(8,128)} %fusion.36, f32[512]{0:T(512)S(1)} %get-tuple-element.8, bf16[512,1024]{1,0:T(8,128)(2,1)S(1)} %copy-done.7, s32[9,512]{1,0:T(8,128)S(1)} %iota_add_fusion, s32[512]{0:T(512)S(1)} %iota_add_fusion.1, pred[9,512]{1,0:T(8,128)(4,1)S(1)} %broadcast_compare_fusion), kind=kOutput, calls=%fused_computation.37 | convolution fusion | flops 627572736 | bytes 11972608 | tf_op jit(solution)/shard_map/aot,ad->otd/dot_general | solution.py:37
  253.7 7.3 %fusion.18 = f32[9,512,128]{1,2,0:T(8,128)} fusion(f32[9,512,512]{2,1,0:T(8,128)S(1)} %bitcast.175, f32[512]{0:T(512)S(1)} %get-tuple-element.10, bf16[512,1024]{1,0:T(8,128)(2,1)S(1)} %copy-done.7, s32[9,512]{1,0:T(8,128)S(1)} %iota_add_fusion, s32[512]{0:T(512)S(1)} %iota_add_fusion.1, pred[9,512]{1,0:T(8,128)(4,1)S(1)} %broadcast_compare_fusion), kind=kOutput, calls=%fused_computation.39 | convolution fusion | flops 627572736 | bytes 11972608 | tf_op jit(solution)/shard_map/aot,ad->otd/dot_general | solution.py:37
  260.9 6.5 %add_convert_fusion.2 = bf16[9,512,128]{1,2,0:T(8,128)(2,1)S(1)} fusion(f32[9,512,128]{1,2,0:T(8,128)S(1)} %fusion.14, f32[9,512,512]{2,1,0:T(8,128)S(1)} %bitcast.177, f32[512]{0:T(512)S(1)} %get-tuple-element.7, bf16[512,1024]{1,0:T(8,128)(2,1)S(1)} %copy-done.7, s32[9,512]{1,0:T(8,128)S(1)} %iota_add_fusion, s32[512]{0:T(512)S(1)} %iota_add_fusion.1, ...), kind=kOutput, calls=%fused_computation.45 | convolution fusion | flops 628752384 | bytes 13152256 | tf_op jit(solution)/shard_map/aot,ad->otd/dot_general | solution.py:37
  267.5 6.7 %add_convert_fusion.1 = bf16[9,512,128]{1,2,0:T(8,128)(2,1)S(1)} fusion(f32[9,512,128]{1,2,0:T(8,128)S(1)} %fusion.16, f32[9,512,512]{2,1,0:T(8,128)S(1)} %fusion.34, f32[512]{0:T(512)S(1)} %get-tuple-element.9, bf16[512,1024]{1,0:T(8,128)(2,1)S(1)} %copy-done.7, s32[9,512]{1,0:T(8,128)S(1)} %iota_add_fusion, s32[512]{0:T(512)S(1)} %iota_add_fusion.1, ...), kind=kOutput, calls=%fused_computation.44 | convolution fusion | flops 628752384 | bytes 13152256 | tf_op jit(solution)/shard_map/aot,ad->otd/dot_general | solution.py:37
  274.2 6.5 %add_convert_fusion = bf16[9,512,128]{1,2,0:T(8,128)(2,1)S(1)} fusion(f32[9,512,128]{1,2,0:T(8,128)S(1)} %copy-done.9, f32[9,512,512]{2,1,0:T(8,128)S(1)} %fusion.30, f32[512]{0:T(512)S(1)} %get-tuple-element.11, bf16[512,1024]{1,0:T(8,128)(2,1)S(1)} %copy-done.7, s32[9,512]{1,0:T(8,128)S(1)} %iota_add_fusion, s32[512]{0:T(512)S(1)} %iota_add_fusion.1, ...), kind=kOutput, calls=%fused_computation.43 | convolution fusion | flops 628752384 | bytes 13152256 | tf_op jit(solution)/shard_map/aot,ad->otd/dot_general | solution.py:37
  280.7 6.5 %add_convert_fusion.3 = bf16[9,512,128]{1,2,0:T(8,128)(2,1)S(1)} fusion(f32[9,512,128]{1,2,0:T(8,128)S(1)} %copy-done.8, f32[9,512,512]{2,1,0:T(8,128)S(1)} %bitcast.187, f32[512]{0:T(512)S(1)} %get-tuple-element.5, bf16[512,1024]{1,0:T(8,128)(2,1)S(1)} %copy-done.7, s32[9,512]{1,0:T(8,128)S(1)} %iota_add_fusion, s32[512]{0:T(512)S(1)} %iota_add_fusion.1, ...), kind=kOutput, calls=%fused_computation.46 | convolution fusion | flops 628752384 | bytes 13152256 | tf_op jit(solution)/shard_map/aot,ad->otd/dot_general | solution.py:37
  287.6 2.2 copy-done.2
  289.7 1.4 slice_bitcast_fusion.7
  291.1 1.3 collective-permute-start.10
  292.4 1.3 collective-permute-start.11
  293.7 1.9 collective-permute-start.4
  295.7 1.9 collective-permute-start.5
  297.6 1.3 collective-permute-start.6
  298.9 26.8 %collective-permute-done.10 = bf16[512,512]{0,1:T(8,128)(2,1)S(1)} collective-permute-done((bf16[512,512]{0,1:T(8,128)(2,1)S(1)}, bf16[512,512]{0,1:T(8,128)(2,1)S(1)}, u32[]{:S(2)}, u32[]{:S(2)}) %collective-permute-start.10) | collective-permute-done | bytes 524320 | tf_op jit(solution)/shard_map/ppermute | solution.py:17
  325.7 1.3 collective-permute-start.7
  326.9 18.3 %collective-permute-done.11 = bf16[512,512]{0,1:T(8,128)(2,1)S(1)} collective-permute-done((bf16[512,512]{0,1:T(8,128)(2,1)S(1)}, bf16[512,512]{0,1:T(8,128)(2,1)S(1)}, u32[]{:S(2)}, u32[]{:S(2)}) %collective-permute-start.11) | collective-permute-done | bytes 524320 | tf_op jit(solution)/shard_map/ppermute | solution.py:17
  345.2 1.3 collective-permute-start.8
  346.5 1.3 collective-permute-start.9
  347.8 3.0 convert_reduce_fusion
  350.9 16.9 %psum.14 = f32[]{:T(128)} all-reduce(f32[]{:T(128)} %convert_reduce_fusion), channel_id=1, replica_groups=mesh['seq'=16,'head'=2] {'head'}, use_global_device_ids=true, to_apply=%region_1.2 | all-reduce | flops 1 | bytes 8 | tf_op jit(solution)/shard_map/psum | solution.py:104
  368.6 1.9 all_gather.18
  370.5 2.4 all_gather.17
  372.9 74.4 %collective-permute-done.9 = bf16[512,512]{0,1:T(8,128)(2,1)} collective-permute-done((bf16[512,512]{0,1:T(8,128)(2,1)S(1)}, bf16[512,512]{0,1:T(8,128)(2,1)}, u32[]{:S(2)}, u32[]{:S(2)}) %collective-permute-start.9) | collective-permute-done | bytes 524320 | tf_op jit(solution)/shard_map/ppermute | solution.py:17
  447.4 2.4 fusion.29
  451.3 17.9 %convolution_convert_fusion = bf16[512,2304]{1,0:T(8,128)(2,1)} fusion(bf16[512,4608]{1,0:T(8,128)(2,1)} %all-gather.4.cloned.1.call-done, bf16[4608,2304]{1,0:T(8,128)(2,1)} %all-gather.6.cloned.1.call-done), kind=kOutput, calls=%fused_computation.41 | convolution fusion | flops 10872815616 | bytes 28311552 | tf_op jit(solution)/shard_map/dot_general | solution.py:95
  469.2 3.8 convolution_convert_fusion.1
  473.0 7.3 %multiply_reduce_fusion = f32[512]{0:T(512)S(1)} fusion(bf16[512,1024]{1,0:T(8,128)(2,1)} %all-gather.8.cloned.1.call-done, bf16[512,2304]{1,0:T(8,128)(2,1)} %convolution_convert_fusion, bf16[2304,1024]{1,0:T(8,128)(2,1)} %param.15, bf16[64,2304]{1,0:T(8,128)(2,1)S(1)} %convolution_convert_fusion.1, bf16[64,1024]{1,0:T(8,128)(2,1)S(1)} %all_gather.18, ...), kind=kOutput, calls=%fused_computation.49 | convolution fusion | flops 2731277824 | bytes 8554500 | tf_op jit(solution)/shard_map/dot_general | solution.py:109
  480.4 9.2 %psum.15 = f32[512]{0:T(512)} all-reduce(f32[512]{0:T(512)S(1)} %multiply_reduce_fusion), channel_id=1, replica_groups=mesh['seq'=16,'head'=2] {'head'}, use_global_device_ids=true, to_apply=%region_11.12 | all-reduce | flops 512 | bytes 4096 | tf_op jit(solution)/shard_map/psum | solution.py:111
  (73 shorter events, 6.1 us)
Async XLA Ops:
  6.5 361.2 %copy-start = (bf16[4,128,128]{2,1,0:T(8,128)(2,1)S(1)}, bf16[4,128,128]{2,1,0:T(8,128)(2,1)}, u32[]{:S(2)}) copy-start(bf16[4,128,128]{2,1,0:T(8,128)(2,1)} %param.14) | copy-start | bytes 393220
  6.5 68.6 %copy-start.4 = (bf16[512,512]{1,0:T(8,128)(2,1)S(1)}, bf16[512,512]{1,0:T(8,128)(2,1)}, u32[]{:S(2)}) copy-start(bf16[512,512]{1,0:T(8,128)(2,1)} %param.11) | copy-start | bytes 1572868
  6.5 164.3 %copy-start.5 = (bf16[512,1024]{1,0:T(8,128)(2,1)S(1)}, bf16[512,1024]{1,0:T(8,128)(2,1)}, u32[]{:S(2)}) copy-start(bf16[512,1024]{1,0:T(8,128)(2,1)} %param.10) | copy-start | bytes 3145732
  6.5 444.7 %all-gather.4.cloned.1.call-start = ((), (), s32[]{:S(2)}) async-start(), calls=%async_computation | async-start | bytes 7077888 | tf_op jit(solution)/shard_map/all_gather | solution.py:91
  7.3 444.0 %all-gather.6.cloned.1.call-start = ((), (), s32[]{:S(2)}) async-start(), calls=%async_computation.1 | async-start | bytes 22560768 | tf_op jit(solution)/shard_map/all_gather | solution.py:94
  8.0 465.0 %all-gather.8.cloned.1.call-start = ((), (), s32[]{:S(2)}) async-start(), calls=%async_computation.2 | async-start | bytes 1572864 | tf_op jit(solution)/shard_map/all_gather | solution.py:87
  8.1 15.8 %collective-permute-start = (bf16[1,512,512]{2,1,0:T(8,128)(2,1)}, bf16[1,512,512]{2,1,0:T(8,128)(2,1)S(1)}, u32[]{:S(2)}, u32[]{:S(2)}) collective-permute-start(bf16[1,512,512]{2,1,0:T(8,128)(2,1)} %bitcast.180), channel_id=1, source_target_pairs={{0,2},{2,4},{4,6},{6,8},{8,10},{10,12},{12,14},{14,16},{16,18},{18... | collective-permute-start | bytes 1572872 | tf_op jit(solution)/shard_map/ppermute | solution.py:17
  25.0 35.3 %collective-permute-start.1 = (bf16[2,512,512]{2,1,0:T(8,128)(2,1)S(1)}, bf16[2,512,512]{2,1,0:T(8,128)(2,1)S(1)}, u32[]{:S(2)}, u32[]{:S(2)}) collective-permute-start(bf16[2,512,512]{2,1,0:T(8,128)(2,1)S(1)} %pad_maximum_fusion.2), channel_id=1, source_target_pairs={{0,4},{2,6},{4,8},{6,10},{8,12},{10,14},{12,16},{14,18},{16,20},{1... | collective-permute-start | bytes 3145736 | tf_op jit(solution)/shard_map/ppermute | solution.py:17
  62.9 84.5 %collective-permute-start.2 = (bf16[4,512,512]{2,1,0:T(8,128)(2,1)}, bf16[4,512,512]{2,1,0:T(8,128)(2,1)}, u32[]{:S(2)}, u32[]{:S(2)}) collective-permute-start(bf16[4,512,512]{2,1,0:T(8,128)(2,1)} %pad_maximum_fusion.1), channel_id=1, source_target_pairs={{0,8},{2,10},{4,12},{6,14},{8,16},{10,18},{12,20},{14,22},{16,24},... | collective-permute-start | bytes 6291464 | tf_op jit(solution)/shard_map/ppermute | solution.py:17
  75.2 94.6 %collective-permute-start.3 = (bf16[512,512]{1,0:T(8,128)(2,1)S(1)}, bf16[512,512]{1,0:T(8,128)(2,1)}, u32[]{:S(2)}, u32[]{:S(2)}) collective-permute-start(bf16[512,512]{1,0:T(8,128)(2,1)S(1)} %copy-done.4), channel_id=1, source_target_pairs={{0,16},{2,18},{4,20},{6,22},{8,24},{10,26},{12,28},{14,30},{1,17},... | collective-permute-start | bytes 1572872 | tf_op jit(solution)/shard_map/ppermute | solution.py:17
  226.6 10.4 %copy-start.3 = (f32[9,512,512]{2,1,0:T(8,128)S(1)}, f32[9,512,512]{2,1,0:T(8,128)}, u32[]{:S(2)}) copy-start(f32[9,512,512]{2,1,0:T(8,128)} %fusion.40) | copy-start | bytes 28311556
  226.6 10.4 %copy-start.7 = (bf16[512,1024]{1,0:T(8,128)(2,1)S(1)}, bf16[512,1024]{1,0:T(8,128)(2,1)}, u32[]{:S(2)}) copy-start(bf16[512,1024]{1,0:T(8,128)(2,1)} %param.12) | copy-start | bytes 3145732
  237.0 16.6 %slice-start = ((s8[9437184]{0:T(1024)(128)(4,1)}), s8[4194304]{0:T(1024)(128)(4,1)S(1)}, s32[]{:S(2)}) async-start(s8[9437184]{0:T(1024)(128)(4,1)} %bitcast.174), calls=%async_computation.3 | async-start | bytes 8388608
  237.0 16.6 %slice-start.1 = ((s8[9437184]{0:T(1024)(128)(4,1)}), s8[4194304]{0:T(1024)(128)(4,1)S(1)}, s32[]{:S(2)}) async-start(s8[9437184]{0:T(1024)(128)(4,1)} %bitcast.174), calls=%async_computation.4 | async-start | bytes 8388608
  242.5 11.1 %slice-start.2 = ((s8[9437184]{0:T(1024)(128)(4,1)}), s8[1048576]{0:T(1024)(128)(4,1)S(1)}, s32[]{:S(2)}) async-start(s8[9437184]{0:T(1024)(128)(4,1)} %bitcast.174), calls=%async_computation.5 | async-start | bytes 2097152
  242.5 18.4 %slice-start.3 = ((s8[9437184]{0:T(1024)(128)(4,1)}), s8[4194304]{0:T(1024)(128)(4,1)S(1)}, s32[]{:S(2)}) async-start(s8[9437184]{0:T(1024)(128)(4,1)} %bitcast.176), calls=%async_computation.6 | async-start | bytes 8388608
  242.5 18.4 %slice-start.4 = ((s8[9437184]{0:T(1024)(128)(4,1)}), s8[4194304]{0:T(1024)(128)(4,1)S(1)}, s32[]{:S(2)}) async-start(s8[9437184]{0:T(1024)(128)(4,1)} %bitcast.176), calls=%async_computation.7 | async-start | bytes 8388608
  253.6 7.3 %slice-start.5 = ((s8[9437184]{0:T(1024)(128)(4,1)}), s8[1048576]{0:T(1024)(128)(4,1)S(1)}, s32[]{:S(2)}) async-start(s8[9437184]{0:T(1024)(128)(4,1)} %bitcast.176), calls=%async_computation.8 | async-start | bytes 2097152
  267.4 6.7 %copy-start.9 = (f32[9,512,128]{1,2,0:T(8,128)S(1)}, f32[9,512,128]{1,2,0:T(8,128)}, u32[]{:S(2)}) copy-start(f32[9,512,128]{1,2,0:T(8,128)} %fusion.18) | copy-start | bytes 7077892
  267.4 13.2 %slice-start.8 = ((s8[9437184]{0:T(1024)(128)(4,1)}), s8[1048576]{0:T(1024)(128)(4,1)S(1)}, s32[]{:S(2)}) async-start(s8[9437184]{0:T(1024)(128)(4,1)} %bitcast.186), calls=%async_computation.11 | async-start | bytes 2097152
  267.4 13.2 %slice-start.9 = ((s8[9437184]{0:T(1024)(128)(4,1)}), s8[4194304]{0:T(1024)(128)(4,1)S(1)}, s32[]{:S(2)}) async-start(s8[9437184]{0:T(1024)(128)(4,1)} %bitcast.186), calls=%async_computation.12 | async-start | bytes 8388608
  274.2 6.5 %slice-start.10 = ((s8[9437184]{0:T(1024)(128)(4,1)}), s8[4194304]{0:T(1024)(128)(4,1)S(1)}, s32[]{:S(2)}) async-start(s8[9437184]{0:T(1024)(128)(4,1)} %bitcast.186), calls=%async_computation.13 | async-start | bytes 8388608
  274.2 6.5 %copy-start.8 = (f32[9,512,128]{1,2,0:T(8,128)S(1)}, f32[9,512,128]{1,2,0:T(8,128)}, u32[]{:S(2)}) copy-start(f32[9,512,128]{1,2,0:T(8,128)} %fusion.12) | copy-start | bytes 7077892
  274.2 73.6 %slice-start.6 = ((s8[4718592]{0:T(1024)(128)(4,1)}), s8[4194304]{0:T(1024)(128)(4,1)S(1)}, s32[]{:S(2)}) async-start(s8[4718592]{0:T(1024)(128)(4,1)} %bitcast.178), calls=%async_computation.9 | async-start | bytes 8388608
  280.7 67.1 %slice-start.7 = ((s8[4718592]{0:T(1024)(128)(4,1)}), s8[524288]{0:T(1024)(128)(4,1)S(1)}, s32[]{:S(2)}) async-start(s8[4718592]{0:T(1024)(128)(4,1)} %bitcast.178), calls=%async_computation.10 | async-start | bytes 1048576
  287.2 80.5 %copy-start.6 = (bf16[64,512]{1,0:T(8,128)(2,1)S(1)}, bf16[64,512]{1,0:T(8,128)(2,1)}, u32[]{:S(2)}) copy-start(bf16[64,512]{1,0:T(8,128)(2,1)} %param.17) | copy-start | bytes 196612
  287.6 2.2 copy-start.2
  291.1 34.5 %collective-permute-start.10 = (bf16[512,512]{0,1:T(8,128)(2,1)S(1)}, bf16[512,512]{0,1:T(8,128)(2,1)S(1)}, u32[]{:S(2)}, u32[]{:S(2)}) collective-permute-start(bf16[512,512]{0,1:T(8,128)(2,1)S(1)} %get-tuple-element.15), channel_id=1, source_target_pairs={{14,0},{16,2},{18,4},{20,6},{22,8},{24,10},{26,12},{28,14},{30,16}... | collective-permute-start | bytes 1572872 | tf_op jit(solution)/shard_map/ppermute | solution.py:17
  292.4 52.8 %collective-permute-start.11 = (bf16[512,512]{0,1:T(8,128)(2,1)S(1)}, bf16[512,512]{0,1:T(8,128)(2,1)S(1)}, u32[]{:S(2)}, u32[]{:S(2)}) collective-permute-start(bf16[512,512]{0,1:T(8,128)(2,1)S(1)} %get-tuple-element.14), channel_id=1, source_target_pairs={{16,0},{18,2},{20,4},{22,6},{24,8},{26,10},{28,12},{30,14},{17,1},... | collective-permute-start | bytes 1572872 | tf_op jit(solution)/shard_map/ppermute | solution.py:17
  293.7 52.8 %collective-permute-start.4 = (bf16[512,512]{0,1:T(8,128)(2,1)S(1)}, bf16[512,512]{0,1:T(8,128)(2,1)S(1)}, u32[]{:S(2)}, u32[]{:S(2)}) collective-permute-start(bf16[512,512]{0,1:T(8,128)(2,1)S(1)} %get-tuple-element.13), channel_id=1, source_target_pairs={{2,0},{4,2},{6,4},{8,6},{10,8},{12,10},{14,12},{16,14},{18,16},{20... | collective-permute-start | bytes 1572872 | tf_op jit(solution)/shard_map/ppermute | solution.py:17
  295.7 77.3 %collective-permute-start.5 = (bf16[512,512]{0,1:T(8,128)(2,1)}, bf16[512,512]{0,1:T(8,128)(2,1)}, u32[]{:S(2)}, u32[]{:S(2)}) collective-permute-start(bf16[512,512]{0,1:T(8,128)(2,1)} %get-tuple-element.20), channel_id=1, source_target_pairs={{4,0},{6,2},{8,4},{10,6},{12,8},{14,10},{16,12},{18,14},{20,16},{2... | collective-permute-start | bytes 1572872 | tf_op jit(solution)/shard_map/ppermute | solution.py:17
  297.6 75.3 %collective-permute-start.6 = (bf16[512,512]{0,1:T(8,128)(2,1)}, bf16[512,512]{0,1:T(8,128)(2,1)}, u32[]{:S(2)}, u32[]{:S(2)}) collective-permute-start(bf16[512,512]{0,1:T(8,128)(2,1)} %get-tuple-element.19), channel_id=1, source_target_pairs={{6,0},{8,2},{10,4},{12,6},{14,8},{16,10},{18,12},{20,14},{22,16},{... | collective-permute-start | bytes 1572872 | tf_op jit(solution)/shard_map/ppermute | solution.py:17
  325.7 47.3 %collective-permute-start.7 = (bf16[512,512]{0,1:T(8,128)(2,1)}, bf16[512,512]{0,1:T(8,128)(2,1)}, u32[]{:S(2)}, u32[]{:S(2)}) collective-permute-start(bf16[512,512]{0,1:T(8,128)(2,1)} %get-tuple-element.18), channel_id=1, source_target_pairs={{8,0},{10,2},{12,4},{14,6},{16,8},{18,10},{20,12},{22,14},{24,16},... | collective-permute-start | bytes 1572872 | tf_op jit(solution)/shard_map/ppermute | solution.py:17
  345.2 27.7 %collective-permute-start.8 = (bf16[512,512]{0,1:T(8,128)(2,1)S(1)}, bf16[512,512]{0,1:T(8,128)(2,1)}, u32[]{:S(2)}, u32[]{:S(2)}) collective-permute-start(bf16[512,512]{0,1:T(8,128)(2,1)S(1)} %get-tuple-element.17), channel_id=1, source_target_pairs={{10,0},{12,2},{14,4},{16,6},{18,8},{20,10},{22,12},{24,14},{26,16}... | collective-permute-start | bytes 1572872 | tf_op jit(solution)/shard_map/ppermute | solution.py:17
  346.5 100.9 %collective-permute-start.9 = (bf16[512,512]{0,1:T(8,128)(2,1)S(1)}, bf16[512,512]{0,1:T(8,128)(2,1)}, u32[]{:S(2)}, u32[]{:S(2)}) collective-permute-start(bf16[512,512]{0,1:T(8,128)(2,1)S(1)} %get-tuple-element.16), channel_id=1, source_target_pairs={{12,0},{14,2},{16,4},{18,6},{20,8},{22,10},{24,12},{26,14},{28,16}... | collective-permute-start | bytes 1572872 | tf_op jit(solution)/shard_map/ppermute | solution.py:17
  451.3 17.9 %copy-start.1 = (bf16[4608,2304]{1,0:T(8,128)(2,1)S(1)}, bf16[4608,2304]{1,0:T(8,128)(2,1)}, u32[]{:S(2)}) copy-start(bf16[4608,2304]{1,0:T(8,128)(2,1)} %all-gather.6.cloned.1.call-done) | copy-start | bytes 63700996
Sparse Core Ops, SparseCore 0:
  8.9 16.3 all-gather.3
  28.1 294.1 all-gather.5
  451.3 13.1 all-gather.7
where the time goes:
time: 505 us; the launch traced here: 497 us
  waiting for transfers between devices  252 us (50%)
  matrix products  146 us (29%)
  starting transfers between devices  36.6 us (7%)
  blocking collectives  30.4 us (6%)
  between operations  14.7 us (3%)
  other arithmetic  9.74 us (2%)
  local copies, waits for them, and re-layouts  7.66 us (2%)
    ppermute x12, waiting for transfers between devices, shifted(): return lax.ppermute(value, axis, pairs)  250 us
    dot_general x8, matrix products, attend(): jnp.einsum('aot,ad->otd', probs, adjoint_head, preferred_element_type=jnp...  60.3 us
    dot_general x8, matrix products, attend(): jnp.einsum('ad,otd->aot', query_head, key_head, preferred_element_type=jn...  55.7 us
    ppermute x12, starting transfers between devices, shifted(): return lax.ppermute(value, axis, pairs)  36.5 us
    dot_general x1, matrix products, on_device(): jnp.dot(full_act, piece, preferred_element_type=jnp.float32)  17.9 us
    psum x1, blocking collectives, on_device(): eigen_total = lax.psum(local_total, 'head')  16.9 us
  transfers between devices with their start and end apart: 15, of which 7 were waited for; matrix products, arithmetic and copies ran while one was open for 31% of the time, Pallas kernels for 0%

commit v1 on v0

v1 whole, which is shorter than its diff:
```python
import math

import jax
import jax.numpy as jnp
from jax import lax
from jax.experimental import pallas as pl
from jax.experimental.pallas import tpu as pltpu
from jax.sharding import PartitionSpec as P

WINDOW = 4096
SCORE_SCALE = 1.0 / 12.0
SOFT_CAP = 50.0
DAMP_FACTOR = 0.1
LOG2E = math.log2(math.e)


def shifted(value, by):
    size = lax.axis_size("seq")
    pairs = [(i, i + by) for i in range(size) if 0 <= i + by < size]
    return lax.ppermute(value, "seq", pairs)


def swapped(value, group, mask):
    size = lax.axis_size("seq")
    pairs = [(i, (i // group) * group + ((i % group) ^ mask)) for i in range(size)]
    return lax.ppermute(value, "seq", pairs)


def attend_kernel(key_span, place_ref, query_ref, adjoint_ref, key_ref, out_ref, weight_ref, sum_ref):
    block = pl.program_id(0)
    member = pl.program_id(1)
    depth, group, rows, width = key_ref.shape
    place = place_ref[0]
    first = place_ref[1]
    step_rows = min(rows, 256)

    @pl.when((block == 0) & (member == 0))
    def clear():
        sum_ref[...] = jnp.zeros_like(sum_ref)

    def where_is(offset):
        line = (depth - 1) * group + block - offset
        back = depth - 1 - line // group
        return back, (line % group) ^ place

    own_slot = block ^ place
    query = query_ref[own_slot]
    total_ref = weight_ref[1]
    weights = weight_ref[0]
    total_ref[...] = jnp.zeros_like(total_ref)
    for offset in range(key_span + 1):

        @pl.when(first + block >= offset)
        def score(offset=offset):
            back, slot = where_is(offset)
            for start in range(0, rows, step_rows):
                keys = key_ref[back, slot, pl.ds(start, step_rows), :]
                raw = lax.dot_general(
                    keys, query, (((1,), (1,)), ((), ())), preferred_element_type=jnp.float32
                )
                turned = jnp.tanh(raw * (SCORE_SCALE / SOFT_CAP))
                weight = jnp.exp2(turned * (SOFT_CAP * LOG2E))
                if offset == 0 or offset == key_span:
                    key_pos = start + lax.broadcasted_iota(jnp.int32, weight.shape, 0)
                    query_pos = lax.broadcasted_iota(jnp.int32, weight.shape, 1)
                    keep = key_pos <= query_pos if offset == 0 else key_pos > query_pos
                    weight = jnp.where(keep, weight, 0.0)
                total_ref[...] += jnp.sum(weight.reshape(-1, 8, rows), axis=0)
                weights[offset, pl.ds(start, step_rows), :] = weight.astype(jnp.bfloat16)

    total = jnp.sum(total_ref[...], axis=0, keepdims=True)
    inverse = jnp.broadcast_to(1.0 / total, (width, rows)).T
    scaled = (adjoint_ref[own_slot].astype(jnp.float32) * inverse).astype(jnp.bfloat16)
    for offset in range(key_span + 1):

        @pl.when(first + block >= offset)
        def spread(offset=offset):
            back, slot = where_is(offset)
            sum_ref[back, slot] += jnp.dot(
                weights[offset], scaled, preferred_element_type=jnp.float32
            )

    @pl.when((block == group - 1) & (member == 1))
    def finish():
        out_ref[...] = sum_ref[...].astype(out_ref.dtype)


def attend(place, query, adjoint, keys, key_span):
    depth, group, rows, width = keys.shape

    def body(place_ref, query_ref, adjoint_ref, key_ref, out_ref, weight_ref, total_ref, sum_ref):
        attend_kernel(
            key_span, place_ref, query_ref, adjoint_ref, key_ref, out_ref, (weight_ref, total_ref), sum_ref
        )

    tiles = 2 * group * (key_span + 1) * rows * rows
    whole = pl.BlockSpec((group, rows, width), lambda b, m: (0, 0, m))
    return pl.pallas_call(
        body,
        grid=(group, 2),
        in_specs=[
            pl.BlockSpec(memory_space=pltpu.SMEM),
            whole,
            whole,
            pl.BlockSpec((depth, group, rows, width), lambda b, m: (0, 0, 0, 0)),
        ],
        out_specs=pl.BlockSpec((depth, group, rows, width), lambda b, m: (0, 0, 0, 0)),
        out_shape=jax.ShapeDtypeStruct((depth, group, rows, width), jnp.bfloat16),
        scratch_shapes=[
            pltpu.VMEM((key_span + 1, rows, rows), jnp.bfloat16),
            pltpu.VMEM((8, rows), jnp.float32),
            pltpu.VMEM((depth, group, rows, width), jnp.float32),
        ],
        compiler_params=pltpu.CompilerParams(vmem_limit_bytes=48 * 1024 * 1024),
        cost_estimate=pl.CostEstimate(
            flops=4 * tiles * width, bytes_accessed=8 * keys.size, transcendentals=2 * tiles
        ),
    )(place, query, adjoint, keys)


def cut(value, place, width):
    return lax.dynamic_slice_in_dim(value, place * width, width, axis=1)


def on_device(
    act, query_rows, key_rows, out_adjoint, basis_input, basis_grad, eigvals, query_act, query_adj
):
    local_rows = act.shape[0]
    group = basis_grad.shape[0]
    width = basis_grad.shape[1]
    key_span = WINDOW // local_rows
    span = key_span // group
    seq_index = lax.axis_index("seq")
    place = seq_index % group

    with jax.named_scope("spread_heads"):
        key_parts, wide_parts = [], []
        for mask in range(group):
            part = cut(key_rows, place ^ mask, width)
            key_parts.append(part if mask == 0 else swapped(part, group, mask))
        for mask in range(group):
            part = jnp.concatenate(
                [
                    cut(query_rows, place ^ mask, 2 * width),
                    cut(out_adjoint, place ^ mask, 2 * width),
                ],
                axis=1,
            )
            wide_parts.append(part if mask == 0 else swapped(part, group, mask))
        own_keys = jnp.stack(key_parts)
        far_keys = [shifted(own_keys, back * group) for back in range(1, span + 1)]
        keys = jnp.stack([own_keys] + far_keys)
        wide = jnp.stack(wide_parts)

    with jax.named_scope("query_gradient"):
        row_count, column_count = basis_input.shape
        full_query_act = lax.all_gather(query_act, "head", axis=1, tiled=True)
        own_rows = lax.dynamic_slice_in_dim(
            full_query_act, seq_index * row_count, row_count, axis=1
        )
        rotated_part = jnp.dot(own_rows, basis_input, preferred_element_type=jnp.float32)
        rotated_query = lax.psum(rotated_part, "seq").astype(jnp.bfloat16)
        split_query = query_adj.reshape(query_adj.shape[0], group, width)
        turned_query = jnp.einsum(
            "the,hef->thf", split_query, basis_grad, preferred_element_type=jnp.float32
        )
        turned_query = turned_query.reshape(query_adj.shape).astype(jnp.bfloat16)
        all_turned_query = lax.all_gather(turned_query, "head", axis=1, tiled=True)
        query_grad = (
            jnp.dot(rotated_query.T, all_turned_query, preferred_element_type=jnp.float32)
            / query_act.shape[0]
        )
        eigen_total = lax.psum(jnp.sum(eigvals, dtype=jnp.float32), "head")
        damping = (
            DAMP_FACTOR * eigen_total / (eigvals.shape[0] * lax.axis_size("head") * eigvals.shape[1])
        )
        scaled = (query_grad / (eigvals.astype(jnp.float32) + damping)).astype(jnp.bfloat16)

    with jax.named_scope("token_map"):
        map_part = jnp.dot(basis_input, scaled, preferred_element_type=jnp.float32)
        map_rows = lax.psum_scatter(map_part, "head", scatter_dimension=1, tiled=True)
        token_map = lax.all_gather(map_rows.astype(jnp.bfloat16), "seq", axis=0, tiled=True)
        full_act = lax.all_gather(act, "head", axis=1, tiled=True)

    with jax.named_scope("attention"):
        spot = jnp.stack([place, seq_index - place]).astype(jnp.int32)
        partials = attend(
            spot, wide[:, :, : 2 * width], wide[:, :, 2 * width :], keys, key_span
        )
        adjoint_sum = partials[0].astype(jnp.float32)
        for back in range(1, span + 1):
            arrived = shifted(partials[back], -back * group)
            adjoint_sum = adjoint_sum + arrived.astype(jnp.float32)
        value_adjoint = adjoint_sum.astype(jnp.bfloat16)

    with jax.named_scope("gather_heads"):
        own_basis = lax.dynamic_index_in_dim(basis_grad, place, axis=0, keepdims=False)
        turned = jnp.einsum(
            "gte,ef->gtf", value_adjoint, own_basis, preferred_element_type=jnp.float32
        ).astype(jnp.bfloat16)
        parts = [turned[0]] + [swapped(turned[mask], group, mask) for mask in range(1, group)]
        stacked = jnp.stack(parts)
        turned_tokens = jnp.concatenate(
            [
                lax.dynamic_index_in_dim(stacked, place ^ head, axis=0, keepdims=False)
                for head in range(group)
            ],
            axis=1,
        )

    with jax.named_scope("influence"):
        mapped = jnp.dot(full_act, token_map, preferred_element_type=jnp.float32)
        score = jnp.sum(mapped * turned_tokens.astype(jnp.float32), axis=1)
        return lax.psum(score, "head")


def solution(mesh):
    return jax.shard_map(
        on_device,
        mesh=mesh,
        in_specs=(
            P("seq", "head"),
            P("seq", "head"),
            P("seq", "head"),
            P("seq", "head"),
            P("seq", "head"),
            P("head", None, None),
            P("head", None),
            P(None, "head"),
            P(None, "head"),
        ),
        out_specs=P("seq"),
        check_vma=False,
    )
```

time: 505 us -> 315 us (0.62)
  the two profiles are of different devices: /device:TPU:5 before, /device:TPU:11 now
where the time goes in v1:
time: 315 us; the launch traced here: 314 us
  waiting for transfers between devices  126 us (40%)
  blocking collectives  86.4 us (27%)
  Pallas kernels  41.8 us (13%)
  starting transfers between devices  18 us (6%)
  matrix products  14.8 us (5%)
  between operations  14 us (4%)
  other arithmetic  10.1 us (3%)
  local copies, waits for them, and re-layouts  3.22 us (1%)
    ppermute x4, waiting for transfers between devices, shifted(): return lax.ppermute(value, 'seq', pairs)  78.1 us
    psum x1, blocking collectives, on_device(): rotated_query = lax.psum(rotated_part, 'seq').astype(jnp.bfloat16)  60.4 us
    pallas_call x1, Pallas kernels, attend(): pl.pallas_call(body, grid=(group, 2), in_specs=[pl.BlockSpec(memory_space...  41.8 us
    ppermute x9, waiting for transfers between devices, swapped(): return lax.ppermute(value, 'seq', pairs)  30.9 us
    reduce_scatter x1, waiting for transfers between devices, on_device(): lax.psum_scatter(map_part, 'head', scatter_dimension=1, tiled=True)  16 us
    all_gather x1, blocking collectives, on_device(): all_turned_query = lax.all_gather(turned_query, 'head', axis=1, tiled=True)  14.2 us
    ppermute x9, starting transfers between devices, swapped(): return lax.ppermute(value, 'seq', pairs)  9.14 us
    ppermute x4, starting transfers between devices, shifted(): return lax.ppermute(value, 'seq', pairs)  8.75 us
  transfers between devices with their start and end apart: 16, of which 10 were waited for; matrix products, arithmetic and copies ran while one was open for 3% of the time, Pallas kernels for 13%

profile of v1, /device:TPU:11, one launch (start us, length us, event | category | flops | bytes accessed | tf_op | source)
XLA Modules:
  0.0 314.1 jit_solution(16903603228184074537)
XLA Ops:
  6.6 2.9 all_gather.12
  9.4 0.4 fusion.14
  9.9 60.4 %all-reduce.1 = bf16[64,2304]{1,0:T(8,128)(2,1)S(1)} all-reduce(f32[64,2304]{1,0:T(8,128)S(1)} %fusion.14), channel_id=1, replica_groups=mesh['seq'=16,'head'=2] {'seq'}, use_global_device_ids=true, to_apply=%region_0.1 | all-reduce | flops 147456 | bytes 884736 | tf_op jit(solution)/shard_map/query_gradient/psum | solution.py:162
  70.3 0.1 fusion.6
  70.5 5.4 %convert_reduce_fusion = f32[]{:T(128)} fusion(bf16[2304,1024]{1,0:T(8,128)(2,1)} %param.15), kind=kLoop, calls=%fused_computation.1 | loop fusion | flops 4718591 | bytes 4718596 | tf_op jit(solution)/shard_map/query_gradient/reduce_sum | solution.py:173
  75.9 14.2 %all_gather.13 = bf16[64,1024]{1,0:T(8,128)(2,1)S(1)} all-gather(bf16[64,512]{1,0:T(8,128)(2,1)S(1)} %bitcast.78), channel_id=1, replica_groups=mesh['seq'=16,'head'=2] {'head'}, dimensions={1}, use_global_device_ids=true | all-gather | bytes 196608 | tf_op jit(solution)/shard_map/query_gradient/all_gather | solution.py:168
  90.1 3.1 psum.22
  93.8 6.4 %fusion.3 = f32[288,1024]{1,0:T(8,128)} fusion(bf16[288,2304]{1,0:T(8,128)(2,1)S(1)} %copy-done, bf16[2304,1024]{1,0:T(8,128)(2,1)} %param.15, bf16[64,1024]{1,0:T(8,128)(2,1)S(1)} %all_gather.13, f32[]{:T(128)S(6)} %div.14, bf16[64,2304]{1,0:T(8,128)(2,1)S(1)} %all-reduce.1), kind=kOutput, calls=%fused_computation.7 | convolution fusion | flops 1672740864 | bytes 7651332 | tf_op jit(solution)/shard_map/token_map/dot_general | solution.py:180
  100.2 0.0 all-gather.5.cloned.1.call-start
  100.2 0.7 all-gather.5.cloned.1.call-update
  101.0 16.0 %reduce-scatter.2.cloned.1.call-done = f32[288,512]{1,0:T(8,128)} async-done(((f32[288,1024]{1,0:T(8,128)}), f32[288,512]{1,0:T(8,128)}) %reduce-scatter.2.cloned.1.call-update) | async-done | bytes 589840 | tf_op jit(solution)/shard_map/token_map/reduce_scatter | solution.py:181
  117.0 1.8 convert_element_type.49
  118.9 1.1 constant_dynamic-slice_fusion.9
  120.0 0.3 collective-permute-start
  120.4 1.3 collective-permute-start.1
  121.6 0.8 pad_maximum_fusion.4
  122.5 1.2 collective-permute-start.2
  123.6 0.8 dynamic-slice_bitcast_fusion.4
  124.4 0.3 collective-permute-start.3
  124.7 1.2 collective-permute-start.4
  125.9 21.5 %collective-permute-done.3 = bf16[512,128]{1,0:T(8,128)(2,1)S(1)} collective-permute-done((bf16[512,128]{1,0:T(8,128)(2,1)S(1)}, bf16[512,128]{1,0:T(8,128)(2,1)S(1)}, u32[]{:S(2)}, u32[]{:S(2)}) %collective-permute-start.3) | collective-permute-done | bytes 131104 | tf_op jit(solution)/shard_map/spread_heads/ppermute | solution.py:26
  147.4 1.3 collective-permute-start.5
  148.8 4.4 %collective-permute-done.5 = bf16[512,128]{1,0:T(8,128)(2,1)S(1)} collective-permute-done((bf16[512,128]{1,0:T(8,128)(2,1)}, bf16[512,128]{1,0:T(8,128)(2,1)S(1)}, u32[]{:S(2)}, u32[]{:S(2)}) %collective-permute-start.5) | collective-permute-done | bytes 131104 | tf_op jit(solution)/shard_map/spread_heads/ppermute | solution.py:26
  153.2 0.1 fusion.21
  153.3 3.1 collective-permute-start.6
  156.4 2.4 collective-permute-start.7
  158.8 0.1 pad_add_fusion.place_ref
  158.9 1.6 pad_maximum_fusion
  160.5 0.1 fusion.22
  160.7 7.2 %collective-permute-done.6 = bf16[4,512,128]{2,1,0:T(8,128)(2,1)S(1)} collective-permute-done((bf16[4,512,128]{2,1,0:T(8,128)(2,1)S(1)}, bf16[4,512,128]{2,1,0:T(8,128)(2,1)S(1)}, u32[]{:S(2)}, u32[]{:S(2)}) %collective-permute-start.6) | collective-permute-done | bytes 524320 | tf_op jit(solution)/shard_map/spread_heads/ppermute | solution.py:20
  167.9 34.1 %collective-permute-done.7 = bf16[4,512,128]{2,1,0:T(8,128)(2,1)S(1)} collective-permute-done((bf16[4,512,128]{2,1,0:T(8,128)(2,1)S(1)}, bf16[4,512,128]{2,1,0:T(8,128)(2,1)S(1)}, u32[]{:S(2)}, u32[]{:S(2)}) %collective-permute-start.7) | collective-permute-done | bytes 524320 | tf_op jit(solution)/shard_map/spread_heads/ppermute | solution.py:20
  202.0 0.2 pad_maximum_fusion.1.key_ref
  202.2 41.8 %attention.1 = bf16[3,4,512,128]{3,2,1,0:T(8,128)(2,1)S(1)} custom-call(s32[2]{0:T(128)S(1)} %pad_add_fusion.place_ref, bf16[4,512,256]{2,1,0:T(8,128)(2,1)S(1)} %get-tuple-element.6.query_ref, bf16[4,512,256]{2,1,0:T(8,128)(2,1)S(1)} %get-tuple-element.5.adjoint_ref, bf16[3,4,512,128]{3,2,1,0:T(8,128)(2,1)S(1)} %pad_maximum_fusion.1.key_ref), custom_call_target="tpu_custom_call" | custom-call | flops 9663676416 | bytes 6291456 | tf_op jit(solution)/shard_map/attention/pallas_call | solution.py:98
  244.0 1.1 slice_bitcast_fusion.1
  245.0 1.9 collective-permute-start.8
  246.9 1.3 collective-permute-start.9
  248.2 9.3 %collective-permute-done.8 = bf16[4,512,128]{2,1,0:T(8,128)(2,1)S(1)} collective-permute-done((bf16[4,512,128]{2,1,0:T(8,128)(2,1)}, bf16[4,512,128]{2,1,0:T(8,128)(2,1)S(1)}, u32[]{:S(2)}, u32[]{:S(2)}) %collective-permute-start.8) | collective-permute-done | bytes 524320 | tf_op jit(solution)/shard_map/attention/ppermute | solution.py:20
  257.6 27.4 %collective-permute-done.9 = bf16[4,512,128]{2,1,0:T(8,128)(2,1)} collective-permute-done((bf16[4,512,128]{2,1,0:T(8,128)(2,1)}, bf16[4,512,128]{2,1,0:T(8,128)(2,1)}, u32[]{:S(2)}, u32[]{:S(2)}) %collective-permute-start.9) | collective-permute-done | bytes 524320 | tf_op jit(solution)/shard_map/attention/ppermute | solution.py:20
  285.0 1.4 convolution_convert_fusion
  286.5 2.3 collective-permute-start.10
  288.8 0.4 collective-permute-start.11
  289.2 0.9 collective-permute-start.12
  290.1 1.1 collective-permute-done.10
  291.2 2.1 collective-permute-done.11
  293.3 1.7 collective-permute-done.12
  295.1 0.1 pad_maximum_fusion.6
  295.2 6.4 %fusion.5 = f32[512]{0:T(512)S(1)} fusion(bf16[4608,512]{1,0:T(8,128)(2,1)} %all-gather.3.cloned.1.call-done, bf16[512,4608]{1,0:T(8,128)(2,1)} %all-gather.5.cloned.1.call-done, bf16[512,128]{0,1:T(8,128)(2,1)S(1)} %get-tuple-element.18, bf16[512,128]{0,1:T(8,128)(2,1)S(1)} %get-tuple-element.19, bf16[512,128]{0,1:T(8,128)(2,1)S(1)} %get-tuple-element.20, ...), kind=kOutput, calls=%fused_computation.11 | convolution fusion | flops 2418540032 | bytes 9963520 | tf_op jit(solution)/shard_map/influence/dot_general | solution.py:212
  301.7 5.9 %psum.23 = f32[512]{0:T(512)} all-reduce(f32[512]{0:T(512)S(1)} %fusion.5), channel_id=1, replica_groups=mesh['seq'=16,'head'=2] {'head'}, use_global_device_ids=true, to_apply=%region_5.6 | all-reduce | flops 512 | bytes 4096 | tf_op jit(solution)/shard_map/influence/psum | solution.py:214
  (32 shorter events, 0.4 us)
Async XLA Ops:
  6.5 2.9 copy-start
  6.5 63.8 %copy-start.6 = (bf16[4,128,128]{2,1,0:T(8,128)(2,1)S(1)}, bf16[4,128,128]{2,1,0:T(8,128)(2,1)}, u32[]{:S(2)}) copy-start(bf16[4,128,128]{2,1,0:T(8,128)(2,1)} %param.14) | copy-start | bytes 393220
  6.5 63.8 %copy-start.7 = (bf16[64,512]{1,0:T(8,128)(2,1)S(1)}, bf16[64,512]{1,0:T(8,128)(2,1)}, u32[]{:S(2)}) copy-start(bf16[64,512]{1,0:T(8,128)(2,1)} %param.17) | copy-start | bytes 196612
  6.5 110.4 %reduce-scatter.2.cloned.1.call-start = ((), (), s32[]{:S(2)}) async-start(), calls=%async_computation.1 | async-start | bytes 1769472 | tf_op jit(solution)/shard_map/token_map/reduce_scatter | solution.py:181
  100.2 18.7 %copy-start.1 = (bf16[512,1024]{1,0:T(8,128)(2,1)S(1)}, bf16[512,1024]{1,0:T(8,128)(2,1)}, u32[]{:S(2)}) copy-start(bf16[512,1024]{1,0:T(8,128)(2,1)} %param.12) | copy-start | bytes 3145732
  100.2 18.7 %copy-start.2 = (bf16[512,1024]{1,0:T(8,128)(2,1)S(1)}, bf16[512,1024]{1,0:T(8,128)(2,1)}, u32[]{:S(2)}) copy-start(bf16[512,1024]{1,0:T(8,128)(2,1)} %param.10) | copy-start | bytes 3145732
  100.2 195.0 %all-gather.5.cloned.1.call-start = ((), (), s32[]{:S(2)}) async-start(), calls=%async_computation.3 | async-start | bytes 7077888 | tf_op jit(solution)/shard_map/token_map/all_gather | solution.py:183
  100.9 194.3 %all-gather.3.cloned.1.call-start = ((), (), s32[]{:S(2)}) async-start(), calls=%async_computation.2 | async-start | bytes 5013504 | tf_op jit(solution)/shard_map/token_map/all_gather | solution.py:182
  119.9 3.7 %copy-start.5 = (bf16[512,512]{1,0:T(8,128)(2,1)S(1)}, bf16[512,512]{1,0:T(8,128)(2,1)}, u32[]{:S(2)}) copy-start(bf16[512,512]{1,0:T(8,128)(2,1)} %param.11) | copy-start | bytes 1572868
  119.9 28.8 %copy-start.3 = (bf16[512,256]{1,0:T(8,128)(2,1)S(1)}, bf16[512,256]{1,0:T(8,128)(2,1)}, u32[]{:S(2)}) copy-start(bf16[512,256]{1,0:T(8,128)(2,1)} %get-tuple-element.13) | copy-start | bytes 786436
  119.9 28.8 %copy-start.4 = (bf16[512,256]{1,0:T(8,128)(2,1)S(1)}, bf16[512,256]{1,0:T(8,128)(2,1)}, u32[]{:S(2)}) copy-start(bf16[512,256]{1,0:T(8,128)(2,1)} %get-tuple-element.34) | copy-start | bytes 786436
  120.0 38.9 %collective-permute-start = (bf16[512,512]{1,0:T(8,128)(2,1)S(1)}, bf16[512,512]{1,0:T(8,128)(2,1)}, u32[]{:S(2)}, u32[]{:S(2)}) collective-permute-start(bf16[512,512]{1,0:T(8,128)(2,1)S(1)} %pad_maximum_fusion.2), channel_id=1, source_target_pairs={{0,2},{2,0},{4,6},{6,4},{8,10},{10,8},{12,14},{14,12},{16,18},{18,... | collective-permute-start | bytes 1572872 | tf_op jit(solution)/shard_map/spread_heads/ppermute | solution.py:26
  120.4 38.5 %collective-permute-start.1 = (bf16[512,512]{1,0:T(8,128)(2,1)S(1)}, bf16[512,512]{1,0:T(8,128)(2,1)}, u32[]{:S(2)}, u32[]{:S(2)}) collective-permute-start(bf16[512,512]{1,0:T(8,128)(2,1)S(1)} %pad_maximum_fusion.3), channel_id=1, source_target_pairs={{0,4},{2,6},{4,0},{6,2},{8,12},{10,14},{12,8},{14,10},{16,20},{18,... | collective-permute-start | bytes 1572872 | tf_op jit(solution)/shard_map/spread_heads/ppermute | solution.py:26
  122.5 36.5 %collective-permute-start.2 = (bf16[512,512]{1,0:T(8,128)(2,1)}, bf16[512,512]{1,0:T(8,128)(2,1)}, u32[]{:S(2)}, u32[]{:S(2)}) collective-permute-start(bf16[512,512]{1,0:T(8,128)(2,1)} %pad_maximum_fusion.4), channel_id=1, source_target_pairs={{0,6},{2,4},{4,2},{6,0},{8,14},{10,12},{12,10},{14,8},{16,22},{18,... | collective-permute-start | bytes 1572872 | tf_op jit(solution)/shard_map/spread_heads/ppermute | solution.py:26
  124.4 23.0 %collective-permute-start.3 = (bf16[512,128]{1,0:T(8,128)(2,1)S(1)}, bf16[512,128]{1,0:T(8,128)(2,1)S(1)}, u32[]{:S(2)}, u32[]{:S(2)}) collective-permute-start(bf16[512,128]{1,0:T(8,128)(2,1)S(1)} %get-tuple-element.28), channel_id=1, source_target_pairs={{0,2},{2,0},{4,6},{6,4},{8,10},{10,8},{12,14},{14,12},{16,18},{18,... | collective-permute-start | bytes 393224 | tf_op jit(solution)/shard_map/spread_heads/ppermute | solution.py:26
  124.7 24.1 %collective-permute-start.4 = (bf16[512,128]{1,0:T(8,128)(2,1)}, bf16[512,128]{1,0:T(8,128)(2,1)S(1)}, u32[]{:S(2)}, u32[]{:S(2)}) collective-permute-start(bf16[512,128]{1,0:T(8,128)(2,1)} %get-tuple-element.30), channel_id=1, source_target_pairs={{0,4},{2,6},{4,0},{6,2},{8,12},{10,14},{12,8},{14,10},{16,20},{18,... | collective-permute-start | bytes 393224 | tf_op jit(solution)/shard_map/spread_heads/ppermute | solution.py:26
  147.4 5.7 %collective-permute-start.5 = (bf16[512,128]{1,0:T(8,128)(2,1)}, bf16[512,128]{1,0:T(8,128)(2,1)S(1)}, u32[]{:S(2)}, u32[]{:S(2)}) collective-permute-start(bf16[512,128]{1,0:T(8,128)(2,1)} %get-tuple-element.29), channel_id=1, source_target_pairs={{0,6},{2,4},{4,2},{6,0},{8,14},{10,12},{12,10},{14,8},{16,22},{18,... | collective-permute-start | bytes 393224 | tf_op jit(solution)/shard_map/spread_heads/ppermute | solution.py:26
  153.3 14.7 %collective-permute-start.6 = (bf16[4,512,128]{2,1,0:T(8,128)(2,1)S(1)}, bf16[4,512,128]{2,1,0:T(8,128)(2,1)S(1)}, u32[]{:S(2)}, u32[]{:S(2)}) collective-permute-start(bf16[4,512,128]{2,1,0:T(8,128)(2,1)S(1)} %get-tuple-element.26), channel_id=1, source_target_pairs={{0,8},{2,10},{4,12},{6,14},{8,16},{10,18},{12,20},{14,22},{16,24},... | collective-permute-start | bytes 1572872 | tf_op jit(solution)/shard_map/spread_heads/ppermute | solution.py:20
  156.4 45.6 %collective-permute-start.7 = (bf16[4,512,128]{2,1,0:T(8,128)(2,1)S(1)}, bf16[4,512,128]{2,1,0:T(8,128)(2,1)S(1)}, u32[]{:S(2)}, u32[]{:S(2)}) collective-permute-start(bf16[4,512,128]{2,1,0:T(8,128)(2,1)S(1)} %get-tuple-element.26), channel_id=1, source_target_pairs={{0,16},{2,18},{4,20},{6,22},{8,24},{10,26},{12,28},{14,30},{1,17},... | collective-permute-start | bytes 1572872 | tf_op jit(solution)/shard_map/spread_heads/ppermute | solution.py:20
  245.0 12.6 %collective-permute-start.8 = (bf16[4,512,128]{2,1,0:T(8,128)(2,1)}, bf16[4,512,128]{2,1,0:T(8,128)(2,1)S(1)}, u32[]{:S(2)}, u32[]{:S(2)}) collective-permute-start(bf16[4,512,128]{2,1,0:T(8,128)(2,1)} %get-tuple-element.7), channel_id=1, source_target_pairs={{8,0},{10,2},{12,4},{14,6},{16,8},{18,10},{20,12},{22,14},{24,16},... | collective-permute-start | bytes 1572872 | tf_op jit(solution)/shard_map/attention/ppermute | solution.py:20
  246.9 38.1 %collective-permute-start.9 = (bf16[4,512,128]{2,1,0:T(8,128)(2,1)}, bf16[4,512,128]{2,1,0:T(8,128)(2,1)}, u32[]{:S(2)}, u32[]{:S(2)}) collective-permute-start(bf16[4,512,128]{2,1,0:T(8,128)(2,1)} %get-tuple-element.8), channel_id=1, source_target_pairs={{16,0},{18,2},{20,4},{22,6},{24,8},{26,10},{28,12},{30,14},{17,1},... | collective-permute-start | bytes 1572872 | tf_op jit(solution)/shard_map/attention/ppermute | solution.py:20
  286.5 4.7 %collective-permute-start.10 = (bf16[512,128]{0,1:T(8,128)(2,1)S(1)}, bf16[512,128]{0,1:T(8,128)(2,1)S(1)}, u32[]{:S(2)}, u32[]{:S(2)}) collective-permute-start(bf16[512,128]{0,1:T(8,128)(2,1)S(1)} %get-tuple-element.24), channel_id=1, source_target_pairs={{0,2},{2,0},{4,6},{6,4},{8,10},{10,8},{12,14},{14,12},{16,18},{18,... | collective-permute-start | bytes 393224 | tf_op jit(solution)/shard_map/gather_heads/ppermute | solution.py:26
  288.8 4.5 %collective-permute-start.11 = (bf16[512,128]{0,1:T(8,128)(2,1)S(1)}, bf16[512,128]{0,1:T(8,128)(2,1)S(1)}, u32[]{:S(2)}, u32[]{:S(2)}) collective-permute-start(bf16[512,128]{0,1:T(8,128)(2,1)S(1)} %get-tuple-element.23), channel_id=1, source_target_pairs={{0,4},{2,6},{4,0},{6,2},{8,12},{10,14},{12,8},{14,10},{16,20},{18,... | collective-permute-start | bytes 393224 | tf_op jit(solution)/shard_map/gather_heads/ppermute | solution.py:26
  289.2 5.9 %collective-permute-start.12 = (bf16[512,128]{0,1:T(8,128)(2,1)S(1)}, bf16[512,128]{0,1:T(8,128)(2,1)S(1)}, u32[]{:S(2)}, u32[]{:S(2)}) collective-permute-start(bf16[512,128]{0,1:T(8,128)(2,1)S(1)} %get-tuple-element.22), channel_id=1, source_target_pairs={{0,6},{2,4},{4,2},{6,0},{8,14},{10,12},{12,10},{14,8},{16,22},{18,... | collective-permute-start | bytes 393224 | tf_op jit(solution)/shard_map/gather_heads/ppermute | solution.py:26
Sparse Core Ops, SparseCore 0:
  100.3 16.6 reduce-scatter.1
  118.6 15.6 all-gather.4
  137.5 97.8 all-gather.2

commit v2 on v1

--- a/solution.py
+++ b/solution.py
@@ -12,6 +12,7 @@
 SOFT_CAP = 50.0
 DAMP_FACTOR = 0.1
 LOG2E = math.log2(math.e)
+MESH = pl.DeviceIdType.MESH
 
 
 def shifted(value, by):
@@ -118,8 +119,183 @@
     )(place, query, adjoint, keys)
 
 
-def cut(value, place, width):
-    return lax.dynamic_slice_in_dim(value, place * width, width, axis=1)
+def exchange_kernel(group, span, reduces, *refs):
+    if reduces:
+        part_ref, refs = refs[0], refs[1:]
+    query_ref, adjoint_ref, key_ref, query_out, adjoint_out, key_out = refs[:6]
+    refs = refs[6:]
+    if reduces:
+        rotated_out, refs = refs[0], refs[1:]
+    deal_send, deal_recv, far_send, far_recv = refs[:4]
+    if reduces:
+        got_ref, part_send, part_recv, sum_send, sum_recv = refs[4:]
+    me = lax.axis_index("seq")
+    size = lax.axis_size("seq")
+    place = me % group
+    base = me - place
+    width = key_ref.shape[1] // group
+
+    barrier = pltpu.get_barrier_semaphore()
+    for step in range(1, size):
+        pl.semaphore_signal(
+            barrier, inc=1, device_id={"seq": (me + step) % size}, device_id_type=MESH
+        )
+    pl.semaphore_wait(barrier, size - 1)
+
+    def deal(kind, mask):
+        source, target, columns = (
+            (key_ref, key_out.at[0], width),
+            (query_ref, query_out, 2 * width),
+            (adjoint_ref, adjoint_out, 2 * width),
+        )[kind]
+        other = place ^ mask
+        view = source.at[:, pl.ds(pl.multiple_of(other * columns, 128), columns)]
+        if mask == 0:
+            return pltpu.make_async_copy(view, target.at[0], deal_recv.at[kind, 0])
+        return pltpu.make_async_remote_copy(
+            src_ref=view,
+            dst_ref=target.at[mask],
+            send_sem=deal_send.at[kind, mask],
+            recv_sem=deal_recv.at[kind, mask],
+            device_id={"seq": base + other},
+            device_id_type=MESH,
+        )
+
+    def far(back):
+        return pltpu.make_async_remote_copy(
+            src_ref=key_out.at[0],
+            dst_ref=key_out.at[back],
+            send_sem=far_send.at[back],
+            recv_sem=far_recv.at[back],
+            device_id={"seq": jnp.minimum(me + back * group, size - 1)},
+            device_id_type=MESH,
+        )
+
+    def part(step):
+        peer = (me + step) % size
+        return pltpu.make_async_remote_copy(
+            src_ref=part_ref.at[peer],
+            dst_ref=got_ref.at[me],
+            send_sem=part_send.at[step],
+            recv_sem=part_recv.at[step],
+            device_id={"seq": peer},
+            device_id_type=MESH,
+        )
+
+    def part_arrival(step):
+        peer = (me + size - step) % size
+        return pltpu.make_async_remote_copy(
+            src_ref=part_ref.at[me],
+            dst_ref=got_ref.at[peer],
+            send_sem=part_send.at[step],
+            recv_sem=part_recv.at[step],
+            device_id={"seq": peer},
+            device_id_type=MESH,
+        )
+
+    def whole(step, source, peer):
+        return pltpu.make_async_remote_copy(
+            src_ref=rotated_out.at[source],
+            dst_ref=rotated_out.at[source],
+            send_sem=sum_send.at[step],
+            recv_sem=sum_recv.at[step],
+            device_id={"seq": peer},
+            device_id_type=MESH,
+        )
+
+    keys = [deal(0, mask) for mask in range(group)]
+    for copy in keys:
+        copy.start()
+    if reduces:
+        parts = [part(step) for step in range(1, size)]
+        for copy in parts:
+            copy.start()
+    wide = [deal(kind, mask) for kind in (1, 2) for mask in range(group)]
+    for mask in range(group):
+        for kind in (1, 2):
+            wide[(kind - 1) * group + mask].start()
+    keys[0].wait()
+    for copy in keys[1:]:
+        copy.wait_recv()
+    for back in range(1, span + 1):
+
+        @pl.when(me + back * group < size)
+        def send(back=back):
+            far(back).start()
+
+    if reduces:
+        got_ref[me] = part_ref[me]
+        for step in range(1, size):
+            part_arrival(step).wait_recv()
+        total = jnp.sum(got_ref[...].astype(jnp.float32), axis=0)
+        rotated_out[me] = total.astype(rotated_out.dtype)
+        sums = [whole(step, me, (me + step) % size) for step in range(1, size)]
+        for copy in sums:
+            copy.start()
+        for copy in parts:
+            copy.wait_send()
+        for step in range(1, size):
+            whole(step, (me + size - step) % size, (me + step) % size).wait_recv()
+        for copy in sums:
+            copy.wait_send()
+
+    for copy in keys[1:]:
+        copy.wait_send()
+    for place_in, copy in enumerate(wide):
+        if place_in % group == 0:
+            copy.wait()
+        else:
+            copy.wait_recv()
+            copy.wait_send()
+    for back in range(1, span + 1):
+
+        @pl.when(me + back * group < size)
+        def sent(back=back):
+            far(back).wait_send()
+
+        @pl.when(me >= back * group)
+        def arrived(back=back):
+            far(back).wait_recv()
+
+
+def exchange(query_rows, out_adjoint, key_rows, part, group, span):
+    rows, columns = key_rows.shape
+    width = columns // group
+    reduces = part is not None
+    anywhere = pl.BlockSpec(memory_space=pl.ANY)
+    in_vmem = pl.BlockSpec(memory_space=pltpu.VMEM)
+    wide = jax.ShapeDtypeStruct((group, rows, 2 * width), jnp.bfloat16)
+    outs = [wide, wide, jax.ShapeDtypeStruct((span + 1, group, rows, width), jnp.bfloat16)]
+    specs = [anywhere] * 3
+    dma = pltpu.SemaphoreType.DMA
+    scratch = [dma((3, group)), dma((3, group)), dma((span + 1,)), dma((span + 1,))]
+    args = (query_rows, out_adjoint, key_rows)
+    in_specs = [anywhere] * 3
+    if reduces:
+        args = (part,) + args
+        in_specs = [in_vmem] + in_specs
+        outs.append(jax.ShapeDtypeStruct(part.shape, part.dtype))
+        specs.append(in_vmem)
+        size = part.shape[0]
+        scratch = scratch + [pltpu.VMEM(part.shape, part.dtype)] + [dma((size,))] * 4
+
+    def body(*refs):
+        exchange_kernel(group, span, reduces, *refs)
+
+    got = pl.pallas_call(
+        body,
+        in_specs=in_specs,
+        out_specs=specs,
+        out_shape=outs,
+        scratch_shapes=scratch,
+        compiler_params=pltpu.CompilerParams(
+            collective_id=0, has_side_effects=True, vmem_limit_bytes=32 * 1024 * 1024
+        ),
+        cost_estimate=pl.CostEstimate(
+            flops=0, bytes_accessed=16 * key_rows.size, transcendentals=0
+        ),
+    )(*args)
+    return got if reduces else list(got) + [None]
 
 
 def on_device(
@@ -133,33 +309,31 @@
     seq_index = lax.axis_index("seq")
     place = seq_index % group
 
-    with jax.named_scope("spread_heads"):
-        key_parts, wide_parts = [], []
-        for mask in range(group):
-            part = cut(key_rows, place ^ mask, width)
-            key_parts.append(part if mask == 0 else swapped(part, group, mask))
-        for mask in range(group):
-            part = jnp.concatenate(
-                [
-                    cut(query_rows, place ^ mask, 2 * width),
-                    cut(out_adjoint, place ^ mask, 2 * width),
-                ],
-                axis=1,
-            )
-            wide_parts.append(part if mask == 0 else swapped(part, group, mask))
-        own_keys = jnp.stack(key_parts)
-        far_keys = [shifted(own_keys, back * group) for back in range(1, span + 1)]
-        keys = jnp.stack([own_keys] + far_keys)
-        wide = jnp.stack(wide_parts)
-
-    with jax.named_scope("query_gradient"):
+    with jax.named_scope("rotated_part"):
         row_count, column_count = basis_input.shape
+        query_count = query_act.shape[0]
+        size = lax.axis_size("seq")
         full_query_act = lax.all_gather(query_act, "head", axis=1, tiled=True)
         own_rows = lax.dynamic_slice_in_dim(
             full_query_act, seq_index * row_count, row_count, axis=1
         )
-        rotated_part = jnp.dot(own_rows, basis_input, preferred_element_type=jnp.float32)
-        rotated_query = lax.psum(rotated_part, "seq").astype(jnp.bfloat16)
+        part = lax.dot_general(
+            basis_input, own_rows, (((0,), (1,)), ((), ())), preferred_element_type=jnp.float32
+        )
+        reduces = column_count % (16 * size) == 0
+        if reduces:
+            part = part.astype(jnp.bfloat16).reshape(size, column_count // size, query_count)
+
+    with jax.named_scope("spread_heads"):
+        queries, adjoints, keys, rotated = exchange(
+            query_rows, out_adjoint, key_rows, part if reduces else None, group, span
+        )
+
+    with jax.named_scope("query_gradient"):
+        if reduces:
+            rotated_query = rotated.reshape(column_count, query_count)
+        else:
+            rotated_query = lax.psum(part, "seq").astype(jnp.bfloat16)
         split_query = query_adj.reshape(query_adj.shape[0], group, width)
         turned_query = jnp.einsum(
             "the,hef->thf", split_query, basis_grad, preferred_element_type=jnp.float32
@@ -167,7 +341,7 @@
         turned_query = turned_query.reshape(query_adj.shape).astype(jnp.bfloat16)
         all_turned_query = lax.all_gather(turned_query, "head", axis=1, tiled=True)
         query_grad = (
-            jnp.dot(rotated_query.T, all_turned_query, preferred_element_type=jnp.float32)
+            jnp.dot(rotated_query, all_turned_query, preferred_element_type=jnp.float32)
             / query_act.shape[0]
         )
         eigen_total = lax.psum(jnp.sum(eigvals, dtype=jnp.float32), "head")
@@ -185,7 +359,7 @@
     with jax.named_scope("attention"):
         spot = jnp.stack([place, seq_index - place]).astype(jnp.int32)
         partials = attend(
-            spot, wide[:, :, : 2 * width], wide[:, :, 2 * width :], keys, key_span
+            spot, queries, adjoints, keys, key_span
         )
         adjoint_sum = partials[0].astype(jnp.float32)
         for back in range(1, span + 1):

time: 315 us -> 268 us (0.85)
  the two profiles are of different devices: /device:TPU:11 before, /device:TPU:5 now
where the time goes in v2:
time: 268 us; the launch traced here: 266 us
  waiting for transfers between devices  129 us (48%)
  Pallas kernels  68.1 us (25%)
  matrix products  16.7 us (6%)
  between operations  13.9 us (5%)
  blocking collectives  13.7 us (5%)
  local copies, waits for them, and re-layouts  11.5 us (4%)
  other arithmetic  7.33 us (3%)
  starting transfers between devices  5.55 us (2%)
    ppermute x2, waiting for transfers between devices, shifted(): return lax.ppermute(value, 'seq', pairs)  99.3 us
    pallas_call x1, Pallas kernels, exchange(): pl.pallas_call(body, in_specs=in_specs, out_specs=specs, out_shape=outs,...  49.8 us
    reduce_scatter x1, waiting for transfers between devices, on_device(): lax.psum_scatter(map_part, 'head', scatter_dimension=1, tiled=True)  25.1 us
    pallas_call x1, Pallas kernels, attend(): pl.pallas_call(body, grid=(group, 2), in_specs=[pl.BlockSpec(memory_space...  18.3 us
    unnamed x22, local copies, waits for them, and re-layouts  9.04 us
    dot_general x1, matrix products, on_device(): map_part = jnp.dot(basis_input, scaled, preferred_element_type=jnp.float32)  6.57 us
    dot_general x1, matrix products, on_device(): mapped = jnp.dot(full_act, token_map, preferred_element_type=jnp.float32)  6.44 us
    psum x1, blocking collectives, on_device(): return lax.psum(score, 'head')  5.66 us
  transfers between devices with their start and end apart: 8, of which 6 were waited for; matrix products, arithmetic and copies ran while one was open for 2% of the time, Pallas kernels for 7%

profile of v2, /device:TPU:5, one launch (start us, length us, event | category | flops | bytes accessed | tf_op | source)
XLA Modules:
  0.0 266.1 jit_solution(3149853135090554252)
XLA Ops:
  6.5 0.0 copy-start
  6.5 0.0 reduce-scatter.2.cloned.1.call-start
  6.6 2.9 %all_gather.12 = bf16[64,4608]{1,0:T(8,128)(2,1)S(1)} all-gather(bf16[64,2304]{1,0:T(8,128)(2,1)} %param.16), channel_id=1, replica_groups=mesh['seq'=16,'head'=2] {'head'}, dimensions={1}, use_global_device_ids=true | all-gather | bytes 884736 | tf_op jit(solution)/shard_map/rotated_part/all_gather | solution.py:316
  9.4 1.1 fusion.7
  10.6 2.1 all_gather.13
  12.6 5.4 %convert_reduce_fusion = f32[]{:T(128)} fusion(bf16[2304,1024]{1,0:T(8,128)(2,1)} %param.15), kind=kLoop, calls=%fused_computation.1 | loop fusion | flops 4718591 | bytes 4718596 | tf_op jit(solution)/shard_map/query_gradient/reduce_sum | solution.py:347
  18.0 0.0 copy-done
  18.0 1.1 fusion.2
  19.1 1.3 copy.17
  20.4 3.1 %psum.14 = f32[]{:T(128)} all-reduce(f32[]{:T(128)} %convert_reduce_fusion), channel_id=1, replica_groups=mesh['seq'=16,'head'=2] {'head'}, use_global_device_ids=true, to_apply=%region_1.2 | all-reduce | flops 1 | bytes 8 | tf_op jit(solution)/shard_map/query_gradient/psum | solution.py:347
  24.2 0.0 copy-done.1
  24.2 0.0 copy-start.2
  24.2 1.2 copy-done.2
  25.4 49.8 %spread_heads.1 = (bf16[4,512,256]{2,1,0:T(8,128)(2,1)S(1)}, bf16[4,512,256]{2,1,0:T(8,128)(2,1)S(1)}, bf16[3,4,512,128]{3,2,1,0:T(8,128)(2,1)S(1)}, bf16[16,144,64]{2,1,0:T(8,128)(2,1)S(1)}) custom-call(bf16[16,144,64]{2,1,0:T(8,128)(2,1)S(1)} %bitcast.66, bf16[512,1024]{1,0:T(8,128)(2,1)S(1)} %copy-done.1, bf16[512,1024]{1,0:T(8,128)(2,1)S(1)} %copy-done.2, ...), custom_call_target="tpu_custom_call" | custom-call | bytes 4194304 | tf_op jit(solution)/shard_map/spread_heads/pallas_call | solution.py:285
  75.2 1.1 copy-done.4
  76.4 1.0 copy-done.6
  77.3 1.0 copy-done.8
  78.4 0.8 copy-done.10
  79.2 6.6 %fusion.4 = f32[288,1024]{1,0:T(8,128)} fusion(bf16[288,2304]{1,0:T(8,128)(2,1)S(1)} %copy-done, bf16[2304,1024]{1,0:T(8,128)(2,1)} %param.15, bf16[2304,64]{1,0:T(8,128)(2,1)} %bitcast.67, bf16[64,1024]{1,0:T(8,128)(2,1)} %all_gather.13, f32[]{:T(128)S(6)} %div.14), kind=kOutput, calls=%fused_computation.7 | convolution fusion | flops 1672740864 | bytes 7651332 | tf_op jit(solution)/shard_map/token_map/dot_general | solution.py:354
  85.8 0.0 reduce-scatter.2.cloned.1.call-update
  85.8 0.0 all-gather.5.cloned.1.call-start
  85.8 0.7 all-gather.5.cloned.1.call-update
  86.5 0.2 all-gather.3.cloned.1.call-start
  86.8 25.1 %reduce-scatter.2.cloned.1.call-done = f32[288,512]{1,0:T(8,128)} async-done(((f32[288,1024]{1,0:T(8,128)}), f32[288,512]{1,0:T(8,128)}) %reduce-scatter.2.cloned.1.call-update) | async-done | bytes 589840 | tf_op jit(solution)/shard_map/token_map/reduce_scatter | solution.py:355
  111.8 1.8 convert_element_type.53
  113.7 0.0 all-gather.3.cloned.1.call-update
  113.7 0.1 pad_add_fusion.place_ref
  113.8 1.4 copy-done.5
  115.2 1.2 copy-done.7
  116.4 1.2 copy-done.9
  117.6 18.3 %attention.1 = bf16[3,4,512,128]{3,2,1,0:T(8,128)(2,1)S(1)} custom-call(s32[2]{0:T(128)S(1)} %pad_add_fusion.place_ref, bf16[4,512,256]{2,1,0:T(8,128)(2,1)S(1)} %copy-done.7, bf16[4,512,256]{2,1,0:T(8,128)(2,1)S(1)} %copy-done.9, bf16[3,4,512,128]{3,2,1,0:T(8,128)(2,1)S(1)} %copy-done.5), custom_call_target="tpu_custom_call" | custom-call | flops 9663676416 | bytes 6291456 | tf_op jit(solution)/shard_map/attention/pallas_call | solution.py:99
  135.9 1.0 slice_bitcast_fusion.1
  136.9 1.3 collective-permute-start
  138.2 1.3 collective-permute-start.1
  139.5 46.5 %collective-permute-done = bf16[4,512,128]{2,1,0:T(8,128)(2,1)S(1)} collective-permute-done((bf16[4,512,128]{2,1,0:T(8,128)(2,1)}, bf16[4,512,128]{2,1,0:T(8,128)(2,1)S(1)}, u32[]{:S(2)}, u32[]{:S(2)}) %collective-permute-start) | collective-permute-done | bytes 524320 | tf_op jit(solution)/shard_map/attention/ppermute | solution.py:21
  186.0 52.8 %collective-permute-done.1 = bf16[4,512,128]{2,1,0:T(8,128)(2,1)} collective-permute-done((bf16[4,512,128]{2,1,0:T(8,128)(2,1)}, bf16[4,512,128]{2,1,0:T(8,128)(2,1)}, u32[]{:S(2)}, u32[]{:S(2)}) %collective-permute-start.1) | collective-permute-done | bytes 524320 | tf_op jit(solution)/shard_map/attention/ppermute | solution.py:21
  238.8 1.4 convolution_convert_fusion.1
  240.3 1.2 collective-permute-start.2
  241.5 0.2 collective-permute-start.3
  241.8 1.3 collective-permute-start.4
  243.0 1.7 collective-permute-done.2
  244.7 1.1 collective-permute-done.3
  245.9 1.4 collective-permute-done.4
  247.3 0.1 pad_maximum_fusion
  247.4 0.0 all-gather.5.cloned.1.call-done
  247.4 0.0 all-gather.3.cloned.1.call-done
  247.4 6.4 %fusion.6 = f32[512]{0:T(512)S(1)} fusion(bf16[4608,512]{1,0:T(8,128)(2,1)} %all-gather.3.cloned.1.call-done, bf16[512,4608]{1,0:T(8,128)(2,1)} %all-gather.5.cloned.1.call-done, bf16[512,128]{0,1:T(8,128)(2,1)S(1)} %get-tuple-element.16, bf16[512,128]{0,1:T(8,128)(2,1)S(1)} %get-tuple-element.17, bf16[512,128]{0,1:T(8,128)(2,1)S(1)} %get-tuple-element.18, ...), kind=kOutput, calls=%fused_computation.11 | convolution fusion | flops 2418540032 | bytes 9963520 | tf_op jit(solution)/shard_map/influence/dot_general | solution.py:386
  253.9 5.7 %psum.15 = f32[512]{0:T(512)} all-reduce(f32[512]{0:T(512)S(1)} %fusion.6), channel_id=1, replica_groups=mesh['seq'=16,'head'=2] {'head'}, use_global_device_ids=true, to_apply=%region_4.5 | all-reduce | flops 512 | bytes 4096 | tf_op jit(solution)/shard_map/influence/psum | solution.py:388
  (13 shorter events, 0.1 us)
Async XLA Ops:
  6.5 11.4 %copy-start = (bf16[288,2304]{1,0:T(8,128)(2,1)S(1)}, bf16[288,2304]{1,0:T(8,128)(2,1)}, u32[]{:S(2)}) copy-start(bf16[288,2304]{1,0:T(8,128)(2,1)} %param.13) | copy-start | bytes 3981316
  6.5 17.6 %copy-start.1 = (bf16[512,1024]{1,0:T(8,128)(2,1)S(1)}, bf16[512,1024]{1,0:T(8,128)(2,1)}, u32[]{:S(2)}) copy-start(bf16[512,1024]{1,0:T(8,128)(2,1)} %refs_1_.1) | copy-start | bytes 3145732
  6.5 17.6 %copy-start.3 = (bf16[512,512]{1,0:T(8,128)(2,1)S(1)}, bf16[512,512]{1,0:T(8,128)(2,1)}, u32[]{:S(2)}) copy-start(bf16[512,512]{1,0:T(8,128)(2,1)} %refs_3_.1) | copy-start | bytes 1572868
  6.5 105.3 %reduce-scatter.2.cloned.1.call-start = ((), (), s32[]{:S(2)}) async-start(), calls=%async_computation.1 | async-start | bytes 1769472 | tf_op jit(solution)/shard_map/token_map/reduce_scatter | solution.py:355
  24.2 1.2 copy-start.2
  75.2 1.1 copy-start.4
  76.4 1.0 copy-start.6
  77.3 1.0 copy-start.8
  78.4 0.8 copy-start.10
  85.8 161.6 %all-gather.5.cloned.1.call-start = ((), (), s32[]{:S(2)}) async-start(), calls=%async_computation.3 | async-start | bytes 7077888 | tf_op jit(solution)/shard_map/token_map/all_gather | solution.py:357
  86.5 160.9 %all-gather.3.cloned.1.call-start = ((), (), s32[]{:S(2)}) async-start(), calls=%async_computation.2 | async-start | bytes 5013504 | tf_op jit(solution)/shard_map/token_map/all_gather | solution.py:356
  113.8 1.4 copy-start.5
  115.2 1.2 copy-start.7
  116.4 1.2 copy-start.9
  136.9 49.1 %collective-permute-start = (bf16[4,512,128]{2,1,0:T(8,128)(2,1)}, bf16[4,512,128]{2,1,0:T(8,128)(2,1)S(1)}, u32[]{:S(2)}, u32[]{:S(2)}) collective-permute-start(bf16[4,512,128]{2,1,0:T(8,128)(2,1)} %get-tuple-element.13), channel_id=1, source_target_pairs={{8,0},{10,2},{12,4},{14,6},{16,8},{18,10},{20,12},{22,14},{24,16},... | collective-permute-start | bytes 1572872 | tf_op jit(solution)/shard_map/attention/ppermute | solution.py:21
  138.2 100.6 %collective-permute-start.1 = (bf16[4,512,128]{2,1,0:T(8,128)(2,1)}, bf16[4,512,128]{2,1,0:T(8,128)(2,1)}, u32[]{:S(2)}, u32[]{:S(2)}) collective-permute-start(bf16[4,512,128]{2,1,0:T(8,128)(2,1)} %get-tuple-element.14), channel_id=1, source_target_pairs={{16,0},{18,2},{20,4},{22,6},{24,8},{26,10},{28,12},{30,14},{17,1},... | collective-permute-start | bytes 1572872 | tf_op jit(solution)/shard_map/attention/ppermute | solution.py:21
  240.3 4.4 %collective-permute-start.2 = (bf16[512,128]{0,1:T(8,128)(2,1)S(1)}, bf16[512,128]{0,1:T(8,128)(2,1)S(1)}, u32[]{:S(2)}, u32[]{:S(2)}) collective-permute-start(bf16[512,128]{0,1:T(8,128)(2,1)S(1)} %get-tuple-element.22), channel_id=1, source_target_pairs={{0,2},{2,0},{4,6},{6,4},{8,10},{10,8},{12,14},{14,12},{16,18},{18,... | collective-permute-start | bytes 393224 | tf_op jit(solution)/shard_map/gather_heads/ppermute | solution.py:27
  241.5 4.4 %collective-permute-start.3 = (bf16[512,128]{0,1:T(8,128)(2,1)S(1)}, bf16[512,128]{0,1:T(8,128)(2,1)S(1)}, u32[]{:S(2)}, u32[]{:S(2)}) collective-permute-start(bf16[512,128]{0,1:T(8,128)(2,1)S(1)} %get-tuple-element.21), channel_id=1, source_target_pairs={{0,4},{2,6},{4,0},{6,2},{8,12},{10,14},{12,8},{14,10},{16,20},{18,... | collective-permute-start | bytes 393224 | tf_op jit(solution)/shard_map/gather_heads/ppermute | solution.py:27
  241.8 5.5 %collective-permute-start.4 = (bf16[512,128]{0,1:T(8,128)(2,1)S(1)}, bf16[512,128]{0,1:T(8,128)(2,1)S(1)}, u32[]{:S(2)}, u32[]{:S(2)}) collective-permute-start(bf16[512,128]{0,1:T(8,128)(2,1)S(1)} %get-tuple-element.20), channel_id=1, source_target_pairs={{0,6},{2,4},{4,2},{6,0},{8,14},{10,12},{12,10},{14,8},{16,22},{18,... | collective-permute-start | bytes 393224 | tf_op jit(solution)/shard_map/gather_heads/ppermute | solution.py:27
Sparse Core Ops, SparseCore 0:
  85.9 25.8 reduce-scatter.1
  113.5 15.6 all-gather.4
  132.3 104.3 all-gather.2

commit v3 on v2

--- a/solution.py
+++ b/solution.py
@@ -27,13 +27,53 @@
     return lax.ppermute(value, "seq", pairs)
 
 
-def attend_kernel(key_span, place_ref, query_ref, adjoint_ref, key_ref, out_ref, weight_ref, sum_ref):
+def attend_kernel(key_span, query_ref, adjoint_ref, key_ref, line_ref, out_ref, map_out, scratch):
+    weights, total_ref, sum_ref, spread_send, spread_recv = scratch
     block = pl.program_id(0)
     member = pl.program_id(1)
     depth, group, rows, width = key_ref.shape
-    place = place_ref[0]
-    first = place_ref[1]
+    me = lax.axis_index("seq")
+    place = me % group
+    first = me - place
     step_rows = min(rows, 256)
+
+    def spread_map(line, mask):
+        target = map_out.at[line * group + place]
+        if mask == 0:
+            return pltpu.make_async_copy(line_ref.at[line], target, spread_recv.at[line, 0])
+        return pltpu.make_async_remote_copy(
+            src_ref=line_ref.at[line],
+            dst_ref=target,
+            send_sem=spread_send.at[line, mask],
+            recv_sem=spread_recv.at[line, mask],
+            device_id={"seq": first + (place ^ mask)},
+            device_id_type=MESH,
+        )
+
+    def map_arrival(line, mask):
+        return pltpu.make_async_remote_copy(
+            src_ref=line_ref.at[line],
+            dst_ref=map_out.at[line * group + (place ^ mask)],
+            send_sem=spread_send.at[line, mask],
+            recv_sem=spread_recv.at[line, mask],
+            device_id={"seq": first + (place ^ mask)},
+            device_id_type=MESH,
+        )
+
+    if line_ref is not None:
+        lines = line_ref.shape[0]
+
+        @pl.when((block == 0) & (member == 0))
+        def start_map():
+            barrier = pltpu.get_barrier_semaphore()
+            for mask in range(1, group):
+                pl.semaphore_signal(
+                    barrier, inc=1, device_id={"seq": first + (place ^ mask)}, device_id_type=MESH
+                )
+            pl.semaphore_wait(barrier, group - 1)
+            for line in range(lines):
+                for mask in range(group):
+                    spread_map(line, mask).start()
 
     @pl.when((block == 0) & (member == 0))
     def clear():
@@ -46,8 +86,6 @@
 
     own_slot = block ^ place
     query = query_ref[own_slot]
-    total_ref = weight_ref[1]
-    weights = weight_ref[0]
     total_ref[...] = jnp.zeros_like(total_ref)
     for offset in range(key_span + 1):
 
@@ -84,51 +122,76 @@
     @pl.when((block == group - 1) & (member == 1))
     def finish():
         out_ref[...] = sum_ref[...].astype(out_ref.dtype)
-
-
-def attend(place, query, adjoint, keys, key_span):
+        if line_ref is not None:
+            for line in range(line_ref.shape[0]):
+                spread_map(line, 0).wait()
+                for mask in range(1, group):
+                    map_arrival(line, mask).wait_recv()
+                    spread_map(line, mask).wait_send()
+
+
+def attend(query, adjoint, keys, line_map, key_span):
     depth, group, rows, width = keys.shape
-
-    def body(place_ref, query_ref, adjoint_ref, key_ref, out_ref, weight_ref, total_ref, sum_ref):
-        attend_kernel(
-            key_span, place_ref, query_ref, adjoint_ref, key_ref, out_ref, (weight_ref, total_ref), sum_ref
-        )
+    spreads = line_map is not None
+
+    def body(*refs):
+        query_ref, adjoint_ref, key_ref = refs[:3]
+        if spreads:
+            line_ref, out_ref, map_out = refs[3:6]
+            scratch = refs[6:]
+        else:
+            line_ref, out_ref, map_out = None, refs[3], None
+            scratch = refs[4:] + (None, None)
+        attend_kernel(key_span, query_ref, adjoint_ref, key_ref, line_ref, out_ref, map_out, scratch)
 
     tiles = 2 * group * (key_span + 1) * rows * rows
     whole = pl.BlockSpec((group, rows, width), lambda b, m: (0, 0, m))
-    return pl.pallas_call(
+    every = pl.BlockSpec((depth, group, rows, width), lambda b, m: (0, 0, 0, 0))
+    anywhere = pl.BlockSpec(memory_space=pl.ANY)
+    args, in_specs = (query, adjoint, keys), [whole, whole, every]
+    outs = [jax.ShapeDtypeStruct((depth, group, rows, width), jnp.bfloat16)]
+    out_specs = [every]
+    scratch = [
+        pltpu.VMEM((key_span + 1, rows, rows), jnp.bfloat16),
+        pltpu.VMEM((8, rows), jnp.float32),
+        pltpu.VMEM((depth, group, rows, width), jnp.float32),
+    ]
+    params = {}
+    if spreads:
+        lines = line_map.shape[0]
+        args, in_specs = args + (line_map,), in_specs + [anywhere]
+        outs.append(jax.ShapeDtypeStruct((lines * group,) + line_map.shape[1:], line_map.dtype))
+        out_specs.append(anywhere)
+        scratch = scratch + [pltpu.SemaphoreType.DMA((lines, group))] * 2
+        params = {"collective_id": 1, "has_side_effects": True}
+    got = pl.pallas_call(
         body,
         grid=(group, 2),
-        in_specs=[
-            pl.BlockSpec(memory_space=pltpu.SMEM),
-            whole,
-            whole,
-            pl.BlockSpec((depth, group, rows, width), lambda b, m: (0, 0, 0, 0)),
-        ],
-        out_specs=pl.BlockSpec((depth, group, rows, width), lambda b, m: (0, 0, 0, 0)),
-        out_shape=jax.ShapeDtypeStruct((depth, group, rows, width), jnp.bfloat16),
-        scratch_shapes=[
-            pltpu.VMEM((key_span + 1, rows, rows), jnp.bfloat16),
-            pltpu.VMEM((8, rows), jnp.float32),
-            pltpu.VMEM((depth, group, rows, width), jnp.float32),
-        ],
-        compiler_params=pltpu.CompilerParams(vmem_limit_bytes=48 * 1024 * 1024),
+        in_specs=in_specs,
+        out_specs=out_specs,
+        out_shape=outs,
+        scratch_shapes=scratch,
+        compiler_params=pltpu.CompilerParams(vmem_limit_bytes=48 * 1024 * 1024, **params),
         cost_estimate=pl.CostEstimate(
             flops=4 * tiles * width, bytes_accessed=8 * keys.size, transcendentals=2 * tiles
         ),
-    )(place, query, adjoint, keys)
+    )(*args)
+    return got if spreads else list(got) + [None]
 
 
 def exchange_kernel(group, span, reduces, *refs):
     if reduces:
-        part_ref, refs = refs[0], refs[1:]
+        part_ref, basis_ref, eigen_ref, turned_ref = refs[:4]
+        refs = refs[4:]
     query_ref, adjoint_ref, key_ref, query_out, adjoint_out, key_out = refs[:6]
     refs = refs[6:]
     if reduces:
-        rotated_out, refs = refs[0], refs[1:]
+        line_out, refs = refs[0], refs[1:]
     deal_send, deal_recv, far_send, far_recv = refs[:4]
     if reduces:
-        got_ref, part_send, part_recv, sum_send, sum_recv = refs[4:]
+        got_ref, rotated_ref, eigen_sum, map_sum, map_got, map_rows = refs[4:10]
+        part_send, part_recv, sum_send, sum_recv = refs[10:14]
+        line_send, line_recv, pair_send, pair_recv = refs[14:]
     me = lax.axis_index("seq")
     size = lax.axis_size("seq")
     place = me % group
@@ -140,7 +203,14 @@
         pl.semaphore_signal(
             barrier, inc=1, device_id={"seq": (me + step) % size}, device_id_type=MESH
         )
-    pl.semaphore_wait(barrier, size - 1)
+    if reduces:
+        head = lax.axis_index("head")
+        pl.semaphore_signal(
+            barrier, inc=1, device_id={"head": 1 - head}, device_id_type=MESH
+        )
+        pl.semaphore_wait(barrier, size)
+    else:
+        pl.semaphore_wait(barrier, size - 1)
 
     def deal(kind, mask):
         source, target, columns = (
@@ -194,15 +264,39 @@
         )
 
     def whole(step, source, peer):
-        return pltpu.make_async_remote_copy(
-            src_ref=rotated_out.at[source],
-            dst_ref=rotated_out.at[source],
+        depth = part_ref.shape[1]
+        view = rotated_ref.at[pl.ds(pl.multiple_of(source * depth, 16), depth), :]
+        return pltpu.make_async_remote_copy(
+            src_ref=view,
+            dst_ref=view,
             send_sem=sum_send.at[step],
             recv_sem=sum_recv.at[step],
             device_id={"seq": peer},
             device_id_type=MESH,
         )
 
+    def pair(which, source, target):
+        return pltpu.make_async_remote_copy(
+            src_ref=source,
+            dst_ref=target,
+            send_sem=pair_send.at[which],
+            recv_sem=pair_recv.at[which],
+            device_id={"head": 1 - head},
+            device_id_type=MESH,
+        )
+
+    lines = size // group
+
+    def line(step, owner):
+        return pltpu.make_async_remote_copy(
+            src_ref=map_rows,
+            dst_ref=line_out.at[owner],
+            send_sem=line_send.at[step],
+            recv_sem=line_recv.at[step],
+            device_id={"seq": (me + step * group) % size},
+            device_id_type=MESH,
+        )
+
     keys = [deal(0, mask) for mask in range(group)]
     for copy in keys:
         copy.start()
@@ -210,25 +304,44 @@
         parts = [part(step) for step in range(1, size)]
         for copy in parts:
             copy.start()
+        features, outputs = eigen_ref.shape
+        chunk = 256 if features % 256 == 0 else 128
+
+        def add_eigen(index, total):
+            some = eigen_ref[pl.ds(pl.multiple_of(index * chunk, chunk), chunk), :]
+            return total + jnp.sum(some.astype(jnp.float32).reshape(-1, 8, outputs), axis=0)
+
+        eigen_part = lax.fori_loop(
+            0, features // chunk, add_eigen, jnp.zeros((8, outputs), jnp.float32)
+        )
+        eigen_part = jnp.sum(eigen_part, axis=0, keepdims=True)
+        eigen_part = jnp.sum(eigen_part, axis=1, keepdims=True)
+        eigen_sum[0] = jnp.broadcast_to(eigen_part, (8, 128))
+        eigen_copy = pair(0, eigen_sum.at[0], eigen_sum.at[1])
+        eigen_copy.start()
+    keys[0].wait()
+    for copy in keys[1:]:
+        copy.wait_recv()
+    for back in range(1, span + 1):
+
+        @pl.when(me + back * group < size)
+        def send(back=back):
+            far(back).start()
+
     wide = [deal(kind, mask) for kind in (1, 2) for mask in range(group)]
     for mask in range(group):
         for kind in (1, 2):
             wide[(kind - 1) * group + mask].start()
-    keys[0].wait()
-    for copy in keys[1:]:
-        copy.wait_recv()
-    for back in range(1, span + 1):
-
-        @pl.when(me + back * group < size)
-        def send(back=back):
-            far(back).start()
 
     if reduces:
         got_ref[me] = part_ref[me]
         for step in range(1, size):
             part_arrival(step).wait_recv()
         total = jnp.sum(got_ref[...].astype(jnp.float32), axis=0)
-        rotated_out[me] = total.astype(rotated_out.dtype)
+        depth = part_ref.shape[1]
+        rotated_ref[pl.ds(pl.multiple_of(me * depth, 16), depth), :] = total.astype(
+            rotated_ref.dtype
+        )
         sums = [whole(step, me, (me + step) % size) for step in range(1, size)]
         for copy in sums:
             copy.start()
@@ -238,6 +351,44 @@
             whole(step, (me + size - step) % size, (me + step) % size).wait_recv()
         for copy in sums:
             copy.wait_send()
+        eigen_copy.wait()
+        damping = (eigen_sum[0, 0:1, 0:1] + eigen_sum[1, 0:1, 0:1]) * (
+            DAMP_FACTOR / (2 * features * outputs)
+        )
+        map_sum[...] = jnp.zeros_like(map_sum)
+
+        def add_map(index, unused):
+            start = pl.multiple_of(index * chunk, chunk)
+            gradient = jnp.dot(
+                rotated_ref[pl.ds(start, chunk), :],
+                turned_ref[...],
+                preferred_element_type=jnp.float32,
+            )
+            spectrum = eigen_ref[pl.ds(start, chunk), :].astype(jnp.float32) + damping
+            scaled = (gradient * (1.0 / turned_ref.shape[0]) / spectrum).astype(jnp.bfloat16)
+            map_sum[...] += jnp.dot(
+                basis_ref[:, pl.ds(start, chunk)], scaled, preferred_element_type=jnp.float32
+            )
+            return unused
+
+        lax.fori_loop(0, features // chunk, add_map, 0)
+        half = outputs // 2
+        own = pl.ds(pl.multiple_of(head * half, 128), half)
+        other = pl.ds(pl.multiple_of((1 - head) * half, 128), half)
+        map_copy = pair(1, map_sum.at[:, other], map_got)
+        map_copy.start()
+        map_copy.wait()
+        map_rows[...] = (map_sum[:, own] + map_got[...]).astype(jnp.bfloat16)
+        here = pltpu.make_async_copy(map_rows, line_out.at[me // group], line_recv.at[0])
+        here.start()
+        line_copies = [line(step, me // group) for step in range(1, lines)]
+        for copy in line_copies:
+            copy.start()
+        here.wait()
+        for step in range(1, lines):
+            line(step, (me // group + lines - step) % lines).wait_recv()
+        for copy in line_copies:
+            copy.wait_send()
 
     for copy in keys[1:]:
         copy.wait_send()
@@ -258,26 +409,37 @@
             far(back).wait_recv()
 
 
-def exchange(query_rows, out_adjoint, key_rows, part, group, span):
+def exchange(query_rows, out_adjoint, key_rows, map_inputs, group, span):
     rows, columns = key_rows.shape
     width = columns // group
-    reduces = part is not None
+    reduces = map_inputs is not None
     anywhere = pl.BlockSpec(memory_space=pl.ANY)
     in_vmem = pl.BlockSpec(memory_space=pltpu.VMEM)
     wide = jax.ShapeDtypeStruct((group, rows, 2 * width), jnp.bfloat16)
     outs = [wide, wide, jax.ShapeDtypeStruct((span + 1, group, rows, width), jnp.bfloat16)]
-    specs = [anywhere] * 3
     dma = pltpu.SemaphoreType.DMA
     scratch = [dma((3, group)), dma((3, group)), dma((span + 1,)), dma((span + 1,))]
     args = (query_rows, out_adjoint, key_rows)
     in_specs = [anywhere] * 3
-    if reduces:
-        args = (part,) + args
-        in_specs = [in_vmem] + in_specs
-        outs.append(jax.ShapeDtypeStruct(part.shape, part.dtype))
-        specs.append(in_vmem)
-        size = part.shape[0]
-        scratch = scratch + [pltpu.VMEM(part.shape, part.dtype)] + [dma((size,))] * 4
+    flops = 0
+    if reduces:
+        part, basis, eigvals, turned = map_inputs
+        size, depth, count = part.shape
+        lines, outputs = size // group, eigvals.shape[1]
+        own_map = (basis.shape[0], outputs // 2)
+        args = tuple(map_inputs) + args
+        in_specs = [in_vmem] * 4 + in_specs
+        outs.append(jax.ShapeDtypeStruct((lines,) + own_map, jnp.bfloat16))
+        scratch = scratch + [
+            pltpu.VMEM(part.shape, part.dtype),
+            pltpu.VMEM((size * depth, count), part.dtype),
+            pltpu.VMEM((2, 8, 128), jnp.float32),
+            pltpu.VMEM((basis.shape[0], outputs), jnp.float32),
+            pltpu.VMEM(own_map, jnp.float32),
+            pltpu.VMEM(own_map, jnp.bfloat16),
+        ]
+        scratch = scratch + [dma((size,))] * 4 + [dma((lines,))] * 2 + [dma((2,))] * 2
+        flops = 2 * basis.size * outputs
 
     def body(*refs):
         exchange_kernel(group, span, reduces, *refs)
@@ -285,14 +447,14 @@
     got = pl.pallas_call(
         body,
         in_specs=in_specs,
-        out_specs=specs,
+        out_specs=[anywhere] * len(outs),
         out_shape=outs,
         scratch_shapes=scratch,
         compiler_params=pltpu.CompilerParams(
-            collective_id=0, has_side_effects=True, vmem_limit_bytes=32 * 1024 * 1024
+            collective_id=0, has_side_effects=True, vmem_limit_bytes=40 * 1024 * 1024
         ),
         cost_estimate=pl.CostEstimate(
-            flops=0, bytes_accessed=16 * key_rows.size, transcendentals=0
+            flops=flops, bytes_accessed=16 * key_rows.size, transcendentals=0
         ),
     )(*args)
     return got if reduces else list(got) + [None]
@@ -320,47 +482,46 @@
         part = lax.dot_general(
             basis_input, own_rows, (((0,), (1,)), ((), ())), preferred_element_type=jnp.float32
         )
-        reduces = column_count % (16 * size) == 0
+        reduces = column_count % (16 * size) == 0 and lax.axis_size("head") == 2 and group > 1
         if reduces:
             part = part.astype(jnp.bfloat16).reshape(size, column_count // size, query_count)
 
-    with jax.named_scope("spread_heads"):
-        queries, adjoints, keys, rotated = exchange(
-            query_rows, out_adjoint, key_rows, part if reduces else None, group, span
-        )
-
-    with jax.named_scope("query_gradient"):
-        if reduces:
-            rotated_query = rotated.reshape(column_count, query_count)
-        else:
-            rotated_query = lax.psum(part, "seq").astype(jnp.bfloat16)
-        split_query = query_adj.reshape(query_adj.shape[0], group, width)
+    with jax.named_scope("turned_query"):
+        split_query = query_adj.reshape(query_count, group, width)
         turned_query = jnp.einsum(
             "the,hef->thf", split_query, basis_grad, preferred_element_type=jnp.float32
         )
         turned_query = turned_query.reshape(query_adj.shape).astype(jnp.bfloat16)
         all_turned_query = lax.all_gather(turned_query, "head", axis=1, tiled=True)
-        query_grad = (
-            jnp.dot(rotated_query, all_turned_query, preferred_element_type=jnp.float32)
-            / query_act.shape[0]
-        )
-        eigen_total = lax.psum(jnp.sum(eigvals, dtype=jnp.float32), "head")
-        damping = (
-            DAMP_FACTOR * eigen_total / (eigvals.shape[0] * lax.axis_size("head") * eigvals.shape[1])
-        )
-        scaled = (query_grad / (eigvals.astype(jnp.float32) + damping)).astype(jnp.bfloat16)
-
-    with jax.named_scope("token_map"):
-        map_part = jnp.dot(basis_input, scaled, preferred_element_type=jnp.float32)
-        map_rows = lax.psum_scatter(map_part, "head", scatter_dimension=1, tiled=True)
-        token_map = lax.all_gather(map_rows.astype(jnp.bfloat16), "seq", axis=0, tiled=True)
+
+    with jax.named_scope("spread_heads"):
+        map_inputs = (part, basis_input, eigvals, all_turned_query) if reduces else None
+        queries, adjoints, keys, line_map = exchange(
+            query_rows, out_adjoint, key_rows, map_inputs, group, span
+        )
+
+    with jax.named_scope("attention"):
+        partials, token_map = attend(queries, adjoints, keys, line_map, key_span)
+        if reduces:
+            token_map = token_map.reshape(row_count * size, -1)
+
+    if not reduces:
+        with jax.named_scope("token_map"):
+            rotated_query = lax.psum(part, "seq").astype(jnp.bfloat16)
+            query_grad = (
+                jnp.dot(rotated_query, all_turned_query, preferred_element_type=jnp.float32)
+                / query_count
+            )
+            eigen_total = lax.psum(jnp.sum(eigvals, dtype=jnp.float32), "head")
+            eigen_count = eigvals.shape[0] * lax.axis_size("head") * eigvals.shape[1]
+            damping = DAMP_FACTOR * eigen_total / eigen_count
+            scaled = (query_grad / (eigvals.astype(jnp.float32) + damping)).astype(jnp.bfloat16)
+            map_part = jnp.dot(basis_input, scaled, preferred_element_type=jnp.float32)
+            map_rows = lax.psum_scatter(map_part, "head", scatter_dimension=1, tiled=True)
+            token_map = lax.all_gather(map_rows.astype(jnp.bfloat16), "seq", axis=0, tiled=True)
+
+    with jax.named_scope("value_adjoint"):
         full_act = lax.all_gather(act, "head", axis=1, tiled=True)
-
-    with jax.named_scope("attention"):
-        spot = jnp.stack([place, seq_index - place]).astype(jnp.int32)
-        partials = attend(
-            spot, queries, adjoints, keys, key_span
-        )
         adjoint_sum = partials[0].astype(jnp.float32)
         for back in range(1, span + 1):
             arrived = shifted(partials[back], -back * group)
@@ -384,6 +545,7 @@
 
     with jax.named_scope("influence"):
         mapped = jnp.dot(full_act, token_map, preferred_element_type=jnp.float32)
+        mapped = lax.optimization_barrier(mapped)
         score = jnp.sum(mapped * turned_tokens.astype(jnp.float32), axis=1)
         return lax.psum(score, "head")
 

time: 268 us -> 251 us (0.937)
  Pallas kernels: 68.1 us -> 150 us
  waiting for transfers between devices: 129 us -> 54.9 us
  matrix products: 16.7 us -> 7 us
  other arithmetic: 7.33 us -> 0.3 us
  local copies, waits for them, and re-layouts: 11.5 us -> 7.39 us
  blocking collectives: 13.7 us -> 9.87 us
    pallas_call x2, Pallas kernels: 68.1 us -> 150 us  [the longest x1 95.3 us: exchange(): pl.pallas_call(body, in_specs=in_specs, out_specs=[anywhere] * len(outs),...]
    ppermute x2, waiting for transfers between devices: 99.3 us -> 49.8 us  [shifted(): return lax.ppermute(value, 'seq', pairs)]
    reduce_scatter x1 -> x0, waiting for transfers between devices: 25.1 us -> none  [on_device(): lax.psum_scatter(map_part, 'head', scatter_dimension=1, tiled=True)]
    dot_general x1 -> x0, matrix products: 6.57 us -> none  [on_device(): map_part = jnp.dot(basis_input, scaled, preferred_element_type=jnp.float32)]
    reduce_sum x1, other arithmetic: 5.37 us -> 0.23 us  [on_device(): score = jnp.sum(mapped * turned_tokens.astype(jnp.float32), axis=1)]
    psum x1 -> x0, blocking collectives: 3.12 us -> none  [on_device(): eigen_total = lax.psum(jnp.sum(eigvals, dtype=jnp.float32), 'head')]
    unnamed x22 -> x18, local copies, waits for them, and re-layouts: 9.04 us -> 6.09 us
  transfers between devices with their start and end apart: 8 -> 6, of which waited for: 6 -> 5; matrix products, arithmetic and copies ran while one was open for 2% -> 1% of each run, Pallas kernels for 7% -> 60%
where the time goes in v3:
time: 251 us; the launch traced here: 249 us
  Pallas kernels  150 us (60%)
  waiting for transfers between devices  54.9 us (22%)
  between operations  13.6 us (5%)
  blocking collectives  9.87 us (4%)
  local copies, waits for them, and re-layouts  7.39 us (3%)
  matrix products  7 us (3%)
  starting transfers between devices  5.32 us (2%)
    pallas_call x1, Pallas kernels, exchange(): pl.pallas_call(body, in_specs=in_specs, out_specs=[anywhere] * len(outs),...  95.3 us
    pallas_call x1, Pallas kernels, attend(): pl.pallas_call(body, grid=(group, 2), in_specs=in_specs, out_specs=out_sp...  55.1 us
    ppermute x2, waiting for transfers between devices, shifted(): return lax.ppermute(value, 'seq', pairs)  49.8 us
    unnamed x18, local copies, waits for them, and re-layouts  6.09 us
    dot_general x1, matrix products, on_device(): mapped = jnp.dot(full_act, token_map, preferred_element_type=jnp.float32)  6.05 us
    psum x1, blocking collectives, on_device(): return lax.psum(score, 'head')  5.3 us
  transfers between devices with their start and end apart: 6, of which 5 were waited for; matrix products, arithmetic and copies ran while one was open for 1% of the time, Pallas kernels for 60%

profile of v3, /device:TPU:5, one launch (start us, length us, event | category | flops | bytes accessed | tf_op | source)
XLA Modules:
  0.0 248.8 jit_solution(2792339419682910446)
XLA Ops:
  6.5 0.0 copy-start
  6.5 0.0 copy-start.7
  6.5 0.0 copy-start.1
  6.5 0.0 copy-start.8
  6.5 0.0 all-gather.2.cloned.1.call-start
  6.6 0.7 all-gather.2.cloned.1.call-update
  7.3 0.0 copy-start.3
  7.3 0.2 copy-done.7
  7.5 2.6 %all_gather.9 = bf16[64,4608]{1,0:T(8,128)(2,1)S(1)} all-gather(bf16[64,2304]{1,0:T(8,128)(2,1)S(1)} %copy-done.7), channel_id=1, replica_groups=mesh['seq'=16,'head'=2] {'head'}, dimensions={1}, use_global_device_ids=true | all-gather | bytes 884736 | tf_op jit(solution)/shard_map/rotated_part/all_gather | solution.py:478
  10.2 0.0 copy-done.1
  10.2 0.4 fusion
  10.6 0.3 copy.10
  11.0 0.0 copy-done
  11.0 0.0 copy-done.8
  11.0 0.1 fusion.1
  11.2 1.9 all_gather.10.refs_3_
  13.1 0.0 copy-done.3
  13.1 0.0 copy-start.2
  13.1 2.3 copy-done.2
  15.4 0.0 copy-start.4
  15.4 1.3 copy-done.4
  16.7 0.0 copy-start.5
  16.7 1.1 copy-done.5
  17.8 95.3 %spread_heads.1 = (bf16[4,512,256]{2,1,0:T(8,128)(2,1)S(1)}, bf16[4,512,256]{2,1,0:T(8,128)(2,1)S(1)}, bf16[3,4,512,128]{3,2,1,0:T(8,128)(2,1)S(1)}, bf16[4,288,512]{2,1,0:T(8,128)(2,1)S(1)}) custom-call(bf16[16,144,64]{2,1,0:T(8,128)(2,1)S(1)} %bitcast.55, bf16[288,2304]{1,0:T(8,128)(2,1)S(1)} %copy-done.1, bf16[2304,1024]{1,0:T(8,128)(2,1)S(1)} %copy-done.2, ...), custom_call_target="tpu_custom_call" | custom-call | flops 1358954496 | bytes 4194304 | tf_op jit(solution)/shard_map/spread_heads/pallas_call | solution.py:447
  113.1 0.0 copy-start.6
  113.1 1.1 copy-done.6
  114.3 55.1 %attention.1 = (bf16[3,4,512,128]{3,2,1,0:T(8,128)(2,1)S(1)}, bf16[16,288,512]{2,1,0:T(8,128)(2,1)}) custom-call(bf16[4,512,256]{2,1,0:T(8,128)(2,1)S(1)} %get-tuple-element.11.refs_0_, bf16[4,512,256]{2,1,0:T(8,128)(2,1)S(1)} %get-tuple-element.12.refs_1_, bf16[3,4,512,128]{3,2,1,0:T(8,128)(2,1)} %copy-done.6, ...), custom_call_target="tpu_custom_call" | custom-call | flops 9663676416 | bytes 6291456 | tf_op jit(solution)/shard_map/attention/pallas_call | solution.py:167
  169.4 0.9 slice_bitcast_fusion.1
  170.3 1.3 collective-permute-start
  171.6 1.3 collective-permute-start.1
  172.9 16.4 %collective-permute-done = bf16[4,512,128]{2,1,0:T(8,128)(2,1)S(1)} collective-permute-done((bf16[4,512,128]{2,1,0:T(8,128)(2,1)}, bf16[4,512,128]{2,1,0:T(8,128)(2,1)S(1)}, u32[]{:S(2)}, u32[]{:S(2)}) %collective-permute-start) | collective-permute-done | bytes 524320 | tf_op jit(solution)/shard_map/value_adjoint/ppermute | solution.py:21
  189.3 33.4 %collective-permute-done.1 = bf16[4,512,128]{2,1,0:T(8,128)(2,1)S(1)} collective-permute-done((bf16[4,512,128]{2,1,0:T(8,128)(2,1)S(1)}, bf16[4,512,128]{2,1,0:T(8,128)(2,1)S(1)}, u32[]{:S(2)}, u32[]{:S(2)}) %collective-permute-start.1) | collective-permute-done | bytes 524320 | tf_op jit(solution)/shard_map/value_adjoint/ppermute | solution.py:21
  222.7 0.4 convolution_convert_fusion.1
  223.1 0.2 collective-permute-start.2
  223.3 1.3 collective-permute-start.3
  224.6 1.2 collective-permute-start.4
  225.8 1.2 collective-permute-done.2
  227.0 0.2 collective-permute-done.3
  227.1 3.1 %collective-permute-done.4 = bf16[512,128]{0,1:T(8,128)(2,1)S(1)} collective-permute-done((bf16[512,128]{0,1:T(8,128)(2,1)S(1)}, bf16[512,128]{0,1:T(8,128)(2,1)S(1)}, u32[]{:S(2)}, u32[]{:S(2)}) %collective-permute-start.4) | collective-permute-done | bytes 131104 | tf_op jit(solution)/shard_map/gather_heads/ppermute | solution.py:27
  230.2 0.1 pad_maximum_fusion
  230.4 0.0 all-gather.2.cloned.1.call-done
  230.4 6.0 %convolution_bitcast_fusion = f32[512,512]{0,1:T(8,128)S(1)} fusion(bf16[4608,512]{1,0:T(8,128)(2,1)} %bitcast.60, bf16[512,4608]{1,0:T(8,128)(2,1)} %all-gather.2.cloned.1.call-done), kind=kOutput, calls=%fused_computation.2 | convolution fusion | flops 2415919104 | bytes 10485760 | tf_op jit(solution)/shard_map/influence/dot_general | solution.py:547
  236.5 0.2 multiply_reduce_fusion
  236.7 5.3 %psum.7 = f32[512]{0:T(512)} all-reduce(f32[512]{0:T(512)S(1)} %multiply_reduce_fusion), channel_id=1, replica_groups=mesh['seq'=16,'head'=2] {'head'}, use_global_device_ids=true, to_apply=%region_1.2 | all-reduce | flops 512 | bytes 4096 | tf_op jit(solution)/shard_map/influence/psum | solution.py:550
  (3 shorter events, 0.1 us)
Async XLA Ops:
  6.5 4.4 %copy-start = (bf16[4,128,128]{2,1,0:T(8,128)(2,1)S(1)}, bf16[4,128,128]{2,1,0:T(8,128)(2,1)}, u32[]{:S(2)}) copy-start(bf16[4,128,128]{2,1,0:T(8,128)(2,1)} %param.14) | copy-start | bytes 393220
  6.5 1.0 copy-start.7
  6.5 3.6 %copy-start.1 = (bf16[288,2304]{1,0:T(8,128)(2,1)S(1)}, bf16[288,2304]{1,0:T(8,128)(2,1)}, u32[]{:S(2)}) copy-start(bf16[288,2304]{1,0:T(8,128)(2,1)} %refs_1_.1) | copy-start | bytes 3981316
  6.5 4.4 %copy-start.8 = (bf16[64,512]{1,0:T(8,128)(2,1)S(1)}, bf16[64,512]{1,0:T(8,128)(2,1)}, u32[]{:S(2)}) copy-start(bf16[64,512]{1,0:T(8,128)(2,1)} %param.17) | copy-start | bytes 196612
  6.5 223.9 %all-gather.2.cloned.1.call-start = ((), (), s32[]{:S(2)}) async-start(), calls=%async_computation | async-start | bytes 7077888 | tf_op jit(solution)/shard_map/value_adjoint/all_gather | solution.py:524
  7.3 5.8 %copy-start.3 = (bf16[512,1024]{1,0:T(8,128)(2,1)S(1)}, bf16[512,1024]{1,0:T(8,128)(2,1)}, u32[]{:S(2)}) copy-start(bf16[512,1024]{1,0:T(8,128)(2,1)} %refs_4_.1) | copy-start | bytes 3145732
  13.1 2.3 copy-start.2
  15.4 1.3 copy-start.4
  16.7 1.1 copy-start.5
  113.1 1.1 copy-start.6
  170.3 19.0 %collective-permute-start = (bf16[4,512,128]{2,1,0:T(8,128)(2,1)}, bf16[4,512,128]{2,1,0:T(8,128)(2,1)S(1)}, u32[]{:S(2)}, u32[]{:S(2)}) collective-permute-start(bf16[4,512,128]{2,1,0:T(8,128)(2,1)} %get-tuple-element.17), channel_id=1, source_target_pairs={{8,0},{10,2},{12,4},{14,6},{16,8},{18,10},{20,12},{22,14},{24,16},... | collective-permute-start | bytes 1572872 | tf_op jit(solution)/shard_map/value_adjoint/ppermute | solution.py:21
  171.6 51.1 %collective-permute-start.1 = (bf16[4,512,128]{2,1,0:T(8,128)(2,1)S(1)}, bf16[4,512,128]{2,1,0:T(8,128)(2,1)S(1)}, u32[]{:S(2)}, u32[]{:S(2)}) collective-permute-start(bf16[4,512,128]{2,1,0:T(8,128)(2,1)S(1)} %get-tuple-element.18), channel_id=1, source_target_pairs={{16,0},{18,2},{20,4},{22,6},{24,8},{26,10},{28,12},{30,14},{17,1},... | collective-permute-start | bytes 1572872 | tf_op jit(solution)/shard_map/value_adjoint/ppermute | solution.py:21
  223.1 3.9 %collective-permute-start.2 = (bf16[512,128]{0,1:T(8,128)(2,1)S(1)}, bf16[512,128]{0,1:T(8,128)(2,1)S(1)}, u32[]{:S(2)}, u32[]{:S(2)}) collective-permute-start(bf16[512,128]{0,1:T(8,128)(2,1)S(1)} %get-tuple-element.26), channel_id=1, source_target_pairs={{0,2},{2,0},{4,6},{6,4},{8,10},{10,8},{12,14},{14,12},{16,18},{18,... | collective-permute-start | bytes 393224 | tf_op jit(solution)/shard_map/gather_heads/ppermute | solution.py:27
  223.3 3.8 %collective-permute-start.3 = (bf16[512,128]{0,1:T(8,128)(2,1)S(1)}, bf16[512,128]{0,1:T(8,128)(2,1)S(1)}, u32[]{:S(2)}, u32[]{:S(2)}) collective-permute-start(bf16[512,128]{0,1:T(8,128)(2,1)S(1)} %get-tuple-element.25), channel_id=1, source_target_pairs={{0,4},{2,6},{4,0},{6,2},{8,12},{10,14},{12,8},{14,10},{16,20},{18,... | collective-permute-start | bytes 393224 | tf_op jit(solution)/shard_map/gather_heads/ppermute | solution.py:27
  224.6 5.6 %collective-permute-start.4 = (bf16[512,128]{0,1:T(8,128)(2,1)S(1)}, bf16[512,128]{0,1:T(8,128)(2,1)S(1)}, u32[]{:S(2)}, u32[]{:S(2)}) collective-permute-start(bf16[512,128]{0,1:T(8,128)(2,1)S(1)} %get-tuple-element.24), channel_id=1, source_target_pairs={{0,6},{2,4},{4,2},{6,0},{8,14},{10,12},{12,10},{14,8},{16,22},{18,... | collective-permute-start | bytes 393224 | tf_op jit(solution)/shard_map/gather_heads/ppermute | solution.py:27
Sparse Core Ops, SparseCore 0:
  8.9 16.3 all-gather.1

commit v4 on v3

--- a/solution.py
+++ b/solution.py
@@ -57,6 +57,18 @@
             send_sem=spread_send.at[line, mask],
             recv_sem=spread_recv.at[line, mask],
             device_id={"seq": first + (place ^ mask)},
+            device_id_type=MESH,
+        )
+
+    def forward(line):
+        came = 1 + line % 2
+        view = map_out.at[line * group + (place ^ came)]
+        return pltpu.make_async_remote_copy(
+            src_ref=view,
+            dst_ref=view,
+            send_sem=spread_send.at[line, 3],
+            recv_sem=spread_recv.at[line, 3],
+            device_id={"seq": first + (place ^ (3 - came))},
             device_id_type=MESH,
         )
 
@@ -73,7 +85,14 @@
             pl.semaphore_wait(barrier, group - 1)
             for line in range(lines):
                 for mask in range(group):
-                    spread_map(line, mask).start()
+                    if mask != 3:
+                        spread_map(line, mask).start()
+
+        @pl.when((block == group // 2) & (member == 0))
+        def forward_map():
+            for line in range(lines if group == 4 else 0):
+                map_arrival(line, 1 + line % 2).wait_recv()
+                forward(line).start()
 
     @pl.when((block == 0) & (member == 0))
     def clear():
@@ -126,8 +145,9 @@
             for line in range(line_ref.shape[0]):
                 spread_map(line, 0).wait()
                 for mask in range(1, group):
-                    map_arrival(line, mask).wait_recv()
-                    spread_map(line, mask).wait_send()
+                    if group != 4 or mask != 1 + line % 2:
+                        map_arrival(line, mask).wait_recv()
+                    (forward(line) if mask == 3 else spread_map(line, mask)).wait_send()
 
 
 def attend(query, adjoint, keys, line_map, key_span):
@@ -171,7 +191,7 @@
         out_specs=out_specs,
         out_shape=outs,
         scratch_shapes=scratch,
-        compiler_params=pltpu.CompilerParams(vmem_limit_bytes=48 * 1024 * 1024, **params),
+        compiler_params=pltpu.CompilerParams(vmem_limit_bytes=58 * 1024 * 1024, **params),
         cost_estimate=pl.CostEstimate(
             flops=4 * tiles * width, bytes_accessed=8 * keys.size, transcendentals=2 * tiles
         ),
@@ -181,7 +201,7 @@
 
 def exchange_kernel(group, span, reduces, *refs):
     if reduces:
-        part_ref, basis_ref, eigen_ref, turned_ref = refs[:4]
+        part_ref, basis_any, eigen_any, turned_ref = refs[:4]
         refs = refs[4:]
     query_ref, adjoint_ref, key_ref, query_out, adjoint_out, key_out = refs[:6]
     refs = refs[6:]
@@ -191,7 +211,8 @@
     if reduces:
         got_ref, rotated_ref, eigen_sum, map_sum, map_got, map_rows = refs[4:10]
         part_send, part_recv, sum_send, sum_recv = refs[10:14]
-        line_send, line_recv, pair_send, pair_recv = refs[14:]
+        line_send, line_recv, pair_send, pair_recv = refs[14:18]
+        load_sem, basis_ref, eigen_ref = refs[18:]
     me = lax.axis_index("seq")
     size = lax.axis_size("seq")
     place = me % group
@@ -306,34 +327,17 @@
             copy.start()
         features, outputs = eigen_ref.shape
         chunk = 256 if features % 256 == 0 else 128
+        loads = [
+            pltpu.make_async_copy(eigen_any, eigen_ref, load_sem.at[0]),
+            pltpu.make_async_copy(basis_any, basis_ref, load_sem.at[1]),
+        ]
+        for copy in loads:
+            copy.start()
 
         def add_eigen(index, total):
             some = eigen_ref[pl.ds(pl.multiple_of(index * chunk, chunk), chunk), :]
             return total + jnp.sum(some.astype(jnp.float32).reshape(-1, 8, outputs), axis=0)
 
-        eigen_part = lax.fori_loop(
-            0, features // chunk, add_eigen, jnp.zeros((8, outputs), jnp.float32)
-        )
-        eigen_part = jnp.sum(eigen_part, axis=0, keepdims=True)
-        eigen_part = jnp.sum(eigen_part, axis=1, keepdims=True)
-        eigen_sum[0] = jnp.broadcast_to(eigen_part, (8, 128))
-        eigen_copy = pair(0, eigen_sum.at[0], eigen_sum.at[1])
-        eigen_copy.start()
-    keys[0].wait()
-    for copy in keys[1:]:
-        copy.wait_recv()
-    for back in range(1, span + 1):
-
-        @pl.when(me + back * group < size)
-        def send(back=back):
-            far(back).start()
-
-    wide = [deal(kind, mask) for kind in (1, 2) for mask in range(group)]
-    for mask in range(group):
-        for kind in (1, 2):
-            wide[(kind - 1) * group + mask].start()
-
-    if reduces:
         got_ref[me] = part_ref[me]
         for step in range(1, size):
             part_arrival(step).wait_recv()
@@ -347,11 +351,37 @@
             copy.start()
         for copy in parts:
             copy.wait_send()
+        loads[0].wait()
+        eigen_part = lax.fori_loop(
+            0, features // chunk, add_eigen, jnp.zeros((8, outputs), jnp.float32)
+        )
+        eigen_part = jnp.sum(eigen_part, axis=0, keepdims=True)
+        eigen_part = jnp.sum(eigen_part, axis=1, keepdims=True)
+        eigen_sum[0] = jnp.broadcast_to(eigen_part, (8, 128))
+        eigen_copy = pair(0, eigen_sum.at[0], eigen_sum.at[1])
+        eigen_copy.start()
         for step in range(1, size):
             whole(step, (me + size - step) % size, (me + step) % size).wait_recv()
         for copy in sums:
             copy.wait_send()
+
+    keys[0].wait()
+    for copy in keys[1:]:
+        copy.wait_recv()
+    for back in range(1, span + 1):
+
+        @pl.when(me + back * group < size)
+        def send(back=back):
+            far(back).start()
+
+    wide = [deal(kind, mask) for kind in (1, 2) for mask in range(group)]
+    for mask in range(group):
+        for kind in (1, 2):
+            wide[(kind - 1) * group + mask].start()
+
+    if reduces:
         eigen_copy.wait()
+        loads[1].wait()
         damping = (eigen_sum[0, 0:1, 0:1] + eigen_sum[1, 0:1, 0:1]) * (
             DAMP_FACTOR / (2 * features * outputs)
         )
@@ -428,7 +458,7 @@
         lines, outputs = size // group, eigvals.shape[1]
         own_map = (basis.shape[0], outputs // 2)
         args = tuple(map_inputs) + args
-        in_specs = [in_vmem] * 4 + in_specs
+        in_specs = [in_vmem, anywhere, anywhere, in_vmem] + in_specs
         outs.append(jax.ShapeDtypeStruct((lines,) + own_map, jnp.bfloat16))
         scratch = scratch + [
             pltpu.VMEM(part.shape, part.dtype),
@@ -438,7 +468,8 @@
             pltpu.VMEM(own_map, jnp.float32),
             pltpu.VMEM(own_map, jnp.bfloat16),
         ]
-        scratch = scratch + [dma((size,))] * 4 + [dma((lines,))] * 2 + [dma((2,))] * 2
+        scratch = scratch + [dma((size,))] * 4 + [dma((lines,))] * 2 + [dma((2,))] * 3
+        scratch = scratch + [pltpu.VMEM(basis.shape, basis.dtype), pltpu.VMEM(eigvals.shape, eigvals.dtype)]
         flops = 2 * basis.size * outputs
 
     def body(*refs):
@@ -451,7 +482,7 @@
         out_shape=outs,
         scratch_shapes=scratch,
         compiler_params=pltpu.CompilerParams(
-            collective_id=0, has_side_effects=True, vmem_limit_bytes=40 * 1024 * 1024
+            collective_id=0, has_side_effects=True, vmem_limit_bytes=58 * 1024 * 1024
         ),
         cost_estimate=pl.CostEstimate(
             flops=flops, bytes_accessed=16 * key_rows.size, transcendentals=0
@@ -482,7 +513,7 @@
         part = lax.dot_general(
             basis_input, own_rows, (((0,), (1,)), ((), ())), preferred_element_type=jnp.float32
         )
-        reduces = column_count % (16 * size) == 0 and lax.axis_size("head") == 2 and group > 1
+        reduces = column_count % (16 * size) == 0 and lax.axis_size("head") == 2 and group in (2, 4)
         if reduces:
             part = part.astype(jnp.bfloat16).reshape(size, column_count // size, query_count)
 
@@ -522,7 +553,9 @@
 
     with jax.named_scope("value_adjoint"):
         full_act = lax.all_gather(act, "head", axis=1, tiled=True)
-        adjoint_sum = partials[0].astype(jnp.float32)
+        mapped = jnp.dot(full_act, token_map, preferred_element_type=jnp.float32)
+        mapped, own_partial = lax.optimization_barrier((mapped, partials[0]))
+        adjoint_sum = own_partial.astype(jnp.float32)
         for back in range(1, span + 1):
             arrived = shifted(partials[back], -back * group)
             adjoint_sum = adjoint_sum + arrived.astype(jnp.float32)
@@ -544,8 +577,6 @@
         )
 
     with jax.named_scope("influence"):
-        mapped = jnp.dot(full_act, token_map, preferred_element_type=jnp.float32)
-        mapped = lax.optimization_barrier(mapped)
         score = jnp.sum(mapped * turned_tokens.astype(jnp.float32), axis=1)
         return lax.psum(score, "head")
 

time: 251 us -> 223 us (0.89)
  Pallas kernels: 150 us -> 112 us
  blocking collectives: 9.87 us -> 22.5 us
  local copies, waits for them, and re-layouts: 7.39 us -> 3.44 us
    pallas_call x1, Pallas kernels: 95.3 us -> 69.7 us  [exchange(): pl.pallas_call(body, in_specs=in_specs, out_specs=[anywhere] * len(outs),...]
    pallas_call x1, Pallas kernels: 55.1 us -> 42.5 us  [attend(): pl.pallas_call(body, grid=(group, 2), in_specs=in_specs, out_specs=out_sp...]
    psum x1, blocking collectives: 5.3 us -> 17.7 us  [on_device(): return lax.psum(score, 'head')]
    unnamed x18 -> x4, local copies, waits for them, and re-layouts: 6.09 us -> 0.01 us
  transfers between devices with their start and end apart: 6 -> 6, of which waited for: 5 -> 4; matrix products, arithmetic and copies ran while one was open for 1% -> 5% of each run, Pallas kernels for 60% -> 51%
where the time goes in v4:
time: 223 us; the launch traced here: 222 us
  Pallas kernels  112 us (50%)
  waiting for transfers between devices  54.5 us (24%)
  blocking collectives  22.5 us (10%)
  between operations  13.5 us (6%)
  matrix products  8.32 us (4%)
  starting transfers between devices  7.13 us (3%)
  local copies, waits for them, and re-layouts  3.44 us (2%)
    pallas_call x1, Pallas kernels, exchange(): pl.pallas_call(body, in_specs=in_specs, out_specs=[anywhere] * len(outs),...  69.7 us
    ppermute x2, waiting for transfers between devices, shifted(): return lax.ppermute(value, 'seq', pairs)  49.4 us
    pallas_call x1, Pallas kernels, attend(): pl.pallas_call(body, grid=(group, 2), in_specs=in_specs, out_specs=out_sp...  42.5 us
    psum x1, blocking collectives, on_device(): return lax.psum(score, 'head')  17.7 us
    dot_general x1, matrix products, on_device(): mapped = jnp.dot(full_act, token_map, preferred_element_type=jnp.float32)  6.05 us
    ppermute x3, starting transfers between devices, swapped(): return lax.ppermute(value, 'seq', pairs)  4.56 us
    ppermute x3, waiting for transfers between devices, swapped(): return lax.ppermute(value, 'seq', pairs)  4.47 us
  transfers between devices with their start and end apart: 6, of which 4 were waited for; matrix products, arithmetic and copies ran while one was open for 5% of the time, Pallas kernels for 51%

profile of v4, /device:TPU:5, one launch (start us, length us, event | category | flops | bytes accessed | tf_op | source)
XLA Modules:
  0.0 221.9 jit_solution(14803055599379398434)
XLA Ops:
  6.5 0.0 copy-start
  6.5 0.0 copy-start.1
  6.5 0.0 all-gather.2.cloned.1.call-start
  6.5 0.7 all-gather.2.cloned.1.call-update
  7.3 2.7 %all_gather.9 = bf16[64,4608]{1,0:T(8,128)(2,1)S(1)} all-gather(bf16[64,2304]{1,0:T(8,128)(2,1)} %param.16), channel_id=1, replica_groups=mesh['seq'=16,'head'=2] {'head'}, dimensions={1}, use_global_device_ids=true | all-gather | bytes 884736 | tf_op jit(solution)/shard_map/rotated_part/all_gather | solution.py:509
  10.0 1.8 fusion
  11.8 1.1 copy.10
  12.8 0.0 copy-done
  12.8 0.0 copy-done.1
  12.8 0.1 fusion.1
  13.0 2.1 all_gather.10.refs_3_
  15.1 69.7 %spread_heads.1 = (bf16[4,512,256]{2,1,0:T(8,128)(2,1)}, bf16[4,512,256]{2,1,0:T(8,128)(2,1)}, bf16[3,4,512,128]{3,2,1,0:T(8,128)(2,1)}, bf16[4,288,512]{2,1,0:T(8,128)(2,1)}) custom-call(bf16[16,144,64]{2,1,0:T(8,128)(2,1)} %bitcast.51, bf16[288,2304]{1,0:T(8,128)(2,1)} %refs_1_.1, bf16[2304,1024]{1,0:T(8,128)(2,1)} %refs_2_.1, ...), custom_call_target="tpu_custom_call" | custom-call | flops 1358954496 | bytes 4194304 | tf_op jit(solution)/shard_map/spread_heads/pallas_call | solution.py:478
  84.8 42.5 %attention.1 = (bf16[3,4,512,128]{3,2,1,0:T(8,128)(2,1)}, bf16[16,288,512]{2,1,0:T(8,128)(2,1)}) custom-call(bf16[4,512,256]{2,1,0:T(8,128)(2,1)} %get-tuple-element.13.refs_0_, bf16[4,512,256]{2,1,0:T(8,128)(2,1)} %get-tuple-element.14.refs_1_, bf16[3,4,512,128]{3,2,1,0:T(8,128)(2,1)} %get-tuple-element.15.refs_2_, ...), custom_call_target="tpu_custom_call" | custom-call | flops 9663676416 | bytes 6291456 | tf_op jit(solution)/shard_map/attention/pallas_call | solution.py:187
  127.2 2.3 %slice_bitcast_fusion.1 = (bf16[4,512,128]{2,1,0:T(8,128)(2,1)}, bf16[4,512,128]{2,1,0:T(8,128)(2,1)S(1)}, bf16[4,512,128]{2,1,0:T(8,128)(2,1)S(1)}) fusion(bf16[3,4,512,128]{3,2,1,0:T(8,128)(2,1)} %get-tuple-element.18), kind=kLoop, calls=%fused_computation.10 | loop fusion | bytes 3145728 | tf_op jit(solution)/shard_map/value_adjoint/squeeze | solution.py:560
  129.5 1.3 collective-permute-start
  130.8 1.3 collective-permute-start.1
  132.1 0.0 all-gather.2.cloned.1.call-done
  132.1 6.0 %convolution_bitcast_fusion = f32[512,512]{0,1:T(8,128)S(1)} fusion(bf16[4608,512]{1,0:T(8,128)(2,1)} %bitcast.56, bf16[512,4608]{1,0:T(8,128)(2,1)} %all-gather.2.cloned.1.call-done), kind=kOutput, calls=%fused_computation.2 | convolution fusion | flops 2415919104 | bytes 10485760 | tf_op jit(solution)/shard_map/value_adjoint/dot_general | solution.py:556
  138.2 34.8 %collective-permute-done = bf16[4,512,128]{2,1,0:T(8,128)(2,1)S(1)} collective-permute-done((bf16[4,512,128]{2,1,0:T(8,128)(2,1)}, bf16[4,512,128]{2,1,0:T(8,128)(2,1)S(1)}, u32[]{:S(2)}, u32[]{:S(2)}) %collective-permute-start) | collective-permute-done | bytes 524320 | tf_op jit(solution)/shard_map/value_adjoint/ppermute | solution.py:21
  172.9 14.6 %collective-permute-done.1 = bf16[4,512,128]{2,1,0:T(8,128)(2,1)S(1)} collective-permute-done((bf16[4,512,128]{2,1,0:T(8,128)(2,1)S(1)}, bf16[4,512,128]{2,1,0:T(8,128)(2,1)S(1)}, u32[]{:S(2)}, u32[]{:S(2)}) %collective-permute-start.1) | collective-permute-done | bytes 524320 | tf_op jit(solution)/shard_map/value_adjoint/ppermute | solution.py:21
  187.5 0.4 convolution_convert_fusion.1
  188.0 0.1 collective-permute-start.2
  188.0 3.9 %collective-permute-start.3 = (bf16[512,128]{0,1:T(8,128)(2,1)S(1)}, bf16[512,128]{0,1:T(8,128)(2,1)S(1)}, u32[]{:S(2)}, u32[]{:S(2)}) collective-permute-start(bf16[512,128]{0,1:T(8,128)(2,1)S(1)} %get-tuple-element.30), channel_id=1, source_target_pairs={{0,4},{2,6},{4,0},{6,2},{8,12},{10,14},{12,8},{14,10},{16,20},{18,... | collective-permute-start | bytes 393224 | tf_op jit(solution)/shard_map/gather_heads/ppermute | solution.py:27
  192.0 0.5 collective-permute-start.4
  192.5 0.0 collective-permute-done.2
  192.5 2.8 %collective-permute-done.3 = bf16[512,128]{0,1:T(8,128)(2,1)S(1)} collective-permute-done((bf16[512,128]{0,1:T(8,128)(2,1)S(1)}, bf16[512,128]{0,1:T(8,128)(2,1)S(1)}, u32[]{:S(2)}, u32[]{:S(2)}) %collective-permute-start.3) | collective-permute-done | bytes 131104 | tf_op jit(solution)/shard_map/gather_heads/ppermute | solution.py:27
  195.3 1.7 collective-permute-done.4
  197.0 0.1 pad_maximum_fusion
  197.1 0.2 multiply_reduce_fusion
  197.3 17.7 %psum.7 = f32[512]{0:T(512)} all-reduce(f32[512]{0:T(512)S(1)} %multiply_reduce_fusion), channel_id=1, replica_groups=mesh['seq'=16,'head'=2] {'head'}, use_global_device_ids=true, to_apply=%region_1.2 | all-reduce | flops 512 | bytes 4096 | tf_op jit(solution)/shard_map/influence/psum | solution.py:581
  (3 shorter events, 0.1 us)
Async XLA Ops:
  6.5 6.3 %copy-start = (bf16[4,128,128]{2,1,0:T(8,128)(2,1)S(1)}, bf16[4,128,128]{2,1,0:T(8,128)(2,1)}, u32[]{:S(2)}) copy-start(bf16[4,128,128]{2,1,0:T(8,128)(2,1)} %param.14) | copy-start | bytes 393220
  6.5 6.3 %copy-start.1 = (bf16[64,512]{1,0:T(8,128)(2,1)S(1)}, bf16[64,512]{1,0:T(8,128)(2,1)}, u32[]{:S(2)}) copy-start(bf16[64,512]{1,0:T(8,128)(2,1)} %param.17) | copy-start | bytes 196612
  6.5 125.6 %all-gather.2.cloned.1.call-start = ((), (), s32[]{:S(2)}) async-start(), calls=%async_computation | async-start | bytes 7077888 | tf_op jit(solution)/shard_map/value_adjoint/all_gather | solution.py:555
  129.5 43.5 %collective-permute-start = (bf16[4,512,128]{2,1,0:T(8,128)(2,1)}, bf16[4,512,128]{2,1,0:T(8,128)(2,1)S(1)}, u32[]{:S(2)}, u32[]{:S(2)}) collective-permute-start(bf16[4,512,128]{2,1,0:T(8,128)(2,1)} %get-tuple-element.21), channel_id=1, source_target_pairs={{8,0},{10,2},{12,4},{14,6},{16,8},{18,10},{20,12},{22,14},{24,16},... | collective-permute-start | bytes 1572872 | tf_op jit(solution)/shard_map/value_adjoint/ppermute | solution.py:21
  130.8 56.8 %collective-permute-start.1 = (bf16[4,512,128]{2,1,0:T(8,128)(2,1)S(1)}, bf16[4,512,128]{2,1,0:T(8,128)(2,1)S(1)}, u32[]{:S(2)}, u32[]{:S(2)}) collective-permute-start(bf16[4,512,128]{2,1,0:T(8,128)(2,1)S(1)} %get-tuple-element.22), channel_id=1, source_target_pairs={{16,0},{18,2},{20,4},{22,6},{24,8},{26,10},{28,12},{30,14},{17,1},... | collective-permute-start | bytes 1572872 | tf_op jit(solution)/shard_map/value_adjoint/ppermute | solution.py:21
  188.0 4.6 %collective-permute-start.2 = (bf16[512,128]{0,1:T(8,128)(2,1)S(1)}, bf16[512,128]{0,1:T(8,128)(2,1)S(1)}, u32[]{:S(2)}, u32[]{:S(2)}) collective-permute-start(bf16[512,128]{0,1:T(8,128)(2,1)S(1)} %get-tuple-element.31), channel_id=1, source_target_pairs={{0,2},{2,0},{4,6},{6,4},{8,10},{10,8},{12,14},{14,12},{16,18},{18,... | collective-permute-start | bytes 393224 | tf_op jit(solution)/shard_map/gather_heads/ppermute | solution.py:27
  188.0 7.3 %collective-permute-start.3 = (bf16[512,128]{0,1:T(8,128)(2,1)S(1)}, bf16[512,128]{0,1:T(8,128)(2,1)S(1)}, u32[]{:S(2)}, u32[]{:S(2)}) collective-permute-start(bf16[512,128]{0,1:T(8,128)(2,1)S(1)} %get-tuple-element.30), channel_id=1, source_target_pairs={{0,4},{2,6},{4,0},{6,2},{8,12},{10,14},{12,8},{14,10},{16,20},{18,... | collective-permute-start | bytes 393224 | tf_op jit(solution)/shard_map/gather_heads/ppermute | solution.py:27
  192.0 5.0 %collective-permute-start.4 = (bf16[512,128]{0,1:T(8,128)(2,1)S(1)}, bf16[512,128]{0,1:T(8,128)(2,1)S(1)}, u32[]{:S(2)}, u32[]{:S(2)}) collective-permute-start(bf16[512,128]{0,1:T(8,128)(2,1)S(1)} %get-tuple-element.29), channel_id=1, source_target_pairs={{0,6},{2,4},{4,2},{6,0},{8,14},{10,12},{12,10},{14,8},{16,22},{18,... | collective-permute-start | bytes 393224 | tf_op jit(solution)/shard_map/gather_heads/ppermute | solution.py:27
Sparse Core Ops, SparseCore 0:
  8.9 16.3 all-gather.1

commit v5 on v4

--- a/solution.py
+++ b/solution.py
@@ -27,8 +27,8 @@
     return lax.ppermute(value, "seq", pairs)
 
 
-def attend_kernel(key_span, query_ref, adjoint_ref, key_ref, line_ref, out_ref, map_out, scratch):
-    weights, total_ref, sum_ref, spread_send, spread_recv = scratch
+def attend_kernel(key_span, query_ref, adjoint_ref, key_ref, rows_ref, out_ref, map_out, scratch):
+    weights, total_ref, sum_ref, line_send, line_recv, spread_send, spread_recv = scratch
     block = pl.program_id(0)
     member = pl.program_id(1)
     depth, group, rows, width = key_ref.shape
@@ -37,62 +37,120 @@
     first = me - place
     step_rows = min(rows, 256)
 
-    def spread_map(line, mask):
-        target = map_out.at[line * group + place]
-        if mask == 0:
-            return pltpu.make_async_copy(line_ref.at[line], target, spread_recv.at[line, 0])
-        return pltpu.make_async_remote_copy(
-            src_ref=line_ref.at[line],
-            dst_ref=target,
-            send_sem=spread_send.at[line, mask],
-            recv_sem=spread_recv.at[line, mask],
-            device_id={"seq": first + (place ^ mask)},
-            device_id_type=MESH,
-        )
-
-    def map_arrival(line, mask):
-        return pltpu.make_async_remote_copy(
-            src_ref=line_ref.at[line],
-            dst_ref=map_out.at[line * group + (place ^ mask)],
-            send_sem=spread_send.at[line, mask],
-            recv_sem=spread_recv.at[line, mask],
-            device_id={"seq": first + (place ^ mask)},
-            device_id_type=MESH,
-        )
-
-    def forward(line):
-        came = 1 + line % 2
-        view = map_out.at[line * group + (place ^ came)]
+    line = me // group
+    turn = 2 * block + member
+
+    def block_copy(index, seq, send_sem, recv_sem):
+        view = map_out.at[index]
         return pltpu.make_async_remote_copy(
             src_ref=view,
             dst_ref=view,
-            send_sem=spread_send.at[line, 3],
-            recv_sem=spread_recv.at[line, 3],
-            device_id={"seq": first + (place ^ (3 - came))},
+            send_sem=send_sem,
+            recv_sem=recv_sem,
+            device_id={"seq": seq},
             device_id_type=MESH,
         )
 
-    if line_ref is not None:
-        lines = line_ref.shape[0]
-
-        @pl.when((block == 0) & (member == 0))
+    def along(stage, way, index):
+        other = (line + (1 if way == 0 else lines - 1)) % lines
+        return block_copy(
+            index * group + place,
+            other * group + place,
+            line_send.at[way, stage],
+            line_recv.at[way, stage],
+        )
+
+    def hop(stage, way):
+        if way == 0:
+            going, coming = line - stage, line - stage - 1
+            return (going >= 0) & (line + 1 < lines), going, coming >= 0, coming
+        going, coming = line + stage, line + stage + 1
+        return (going < lines) & (line >= 1), going, coming < lines, coming
+
+    def beside(owner, mask):
+        return block_copy(
+            owner * group + place,
+            first + (place ^ mask),
+            spread_send.at[owner, mask],
+            spread_recv.at[owner, mask],
+        )
+
+    def arrival(owner, mask):
+        return block_copy(
+            owner * group + (place ^ mask),
+            first + (place ^ mask),
+            spread_send.at[owner, mask],
+            spread_recv.at[owner, mask],
+        )
+
+    def forward(owner):
+        came = 1 + owner % 2
+        return block_copy(
+            owner * group + (place ^ came),
+            first + (place ^ (3 - came)),
+            spread_send.at[owner, 3],
+            spread_recv.at[owner, 3],
+        )
+
+    if rows_ref is not None:
+        lines = map_out.shape[0] // group
+
+        def start_hops(stage):
+            for way in (0, 1):
+                sends, going, unused, unused_too = hop(stage, way)
+
+                @pl.when(sends)
+                def start(way=way, going=going):
+                    along(stage, way, going).start()
+
+        def await_hops(stage):
+            for way in (0, 1):
+                unused, unused_too, receives, coming = hop(stage, way)
+
+                @pl.when(receives)
+                def wait(way=way, coming=coming):
+                    along(stage, way, coming).wait_recv()
+
+        @pl.when(turn == 0)
         def start_map():
             barrier = pltpu.get_barrier_semaphore()
             for mask in range(1, group):
                 pl.semaphore_signal(
                     barrier, inc=1, device_id={"seq": first + (place ^ mask)}, device_id_type=MESH
                 )
-            pl.semaphore_wait(barrier, group - 1)
-            for line in range(lines):
-                for mask in range(group):
-                    if mask != 3:
-                        spread_map(line, mask).start()
-
-        @pl.when((block == group // 2) & (member == 0))
-        def forward_map():
-            for line in range(lines if group == 4 else 0):
-                map_arrival(line, 1 + line % 2).wait_recv()
-                forward(line).start()
+            for step in (1, lines - 1):
+                pl.semaphore_signal(
+                    barrier,
+                    inc=1,
+                    device_id={"seq": ((line + step) % lines) * group + place},
+                    device_id_type=MESH,
+                )
+            here = pltpu.make_async_copy(rows_ref, map_out.at[me], line_recv.at[0, lines - 1])
+            here.start()
+            here.wait()
+            pl.semaphore_wait(barrier, group + 1)
+            start_hops(0)
+
+        for stage in range(1, lines):
+
+            @pl.when(turn == stage)
+            def next_hop(stage=stage):
+                await_hops(stage - 1)
+                if stage < lines - 1:
+                    start_hops(stage)
+                else:
+                    for owner in range(lines):
+                        for mask in range(1, group):
+                            if mask != 3:
+                                beside(owner, mask).start()
+
+        if group == 4:
+
+            @pl.when(turn == lines + 2)
+            def forward_map():
+                for owner in range(lines):
+                    arrival(owner, 1 + owner % 2).wait_recv()
+                    forward(owner).start()
 
     @pl.when((block == 0) & (member == 0))
     def clear():
@@ -141,28 +199,35 @@
     @pl.when((block == group - 1) & (member == 1))
     def finish():
         out_ref[...] = sum_ref[...].astype(out_ref.dtype)
-        if line_ref is not None:
-            for line in range(line_ref.shape[0]):
-                spread_map(line, 0).wait()
+        if rows_ref is not None:
+            for stage in range(lines - 1):
+                for way in (0, 1):
+                    sends, going, unused, unused_too = hop(stage, way)
+
+                    @pl.when(sends)
+                    def sent(stage=stage, way=way, going=going):
+                        along(stage, way, going).wait_send()
+
+            for owner in range(lines):
                 for mask in range(1, group):
-                    if group != 4 or mask != 1 + line % 2:
-                        map_arrival(line, mask).wait_recv()
-                    (forward(line) if mask == 3 else spread_map(line, mask)).wait_send()
-
-
-def attend(query, adjoint, keys, line_map, key_span):
+                    if group != 4 or mask != 1 + owner % 2:
+                        arrival(owner, mask).wait_recv()
+                    (forward(owner) if mask == 3 else beside(owner, mask)).wait_send()
+
+
+def attend(query, adjoint, keys, map_rows, size, key_span):
     depth, group, rows, width = keys.shape
-    spreads = line_map is not None
+    spreads = map_rows is not None
 
     def body(*refs):
         query_ref, adjoint_ref, key_ref = refs[:3]
         if spreads:
-            line_ref, out_ref, map_out = refs[3:6]
+            rows_ref, out_ref, map_out = refs[3:6]
             scratch = refs[6:]
         else:
-            line_ref, out_ref, map_out = None, refs[3], None
-            scratch = refs[4:] + (None, None)
-        attend_kernel(key_span, query_ref, adjoint_ref, key_ref, line_ref, out_ref, map_out, scratch)
+            rows_ref, out_ref, map_out = None, refs[3], None
+            scratch = refs[4:] + (None,) * 4
+        attend_kernel(key_span, query_ref, adjoint_ref, key_ref, rows_ref, out_ref, map_out, scratch)
 
     tiles = 2 * group * (key_span + 1) * rows * rows
     whole = pl.BlockSpec((group, rows, width), lambda b, m: (0, 0, m))
@@ -178,10 +243,11 @@
     ]
     params = {}
     if spreads:
-        lines = line_map.shape[0]
-        args, in_specs = args + (line_map,), in_specs + [anywhere]
-        outs.append(jax.ShapeDtypeStruct((lines * group,) + line_map.shape[1:], line_map.dtype))
+        lines = size // group
+        args, in_specs = args + (map_rows,), in_specs + [anywhere]
+        outs.append(jax.ShapeDtypeStruct((size,) + map_rows.shape, map_rows.dtype))
         out_specs.append(anywhere)
+        scratch = scratch + [pltpu.SemaphoreType.DMA((2, lines))] * 2
         scratch = scratch + [pltpu.SemaphoreType.DMA((lines, group))] * 2
         params = {"collective_id": 1, "has_side_effects": True}
     got = pl.pallas_call(
@@ -206,13 +272,12 @@
     query_ref, adjoint_ref, key_ref, query_out, adjoint_out, key_out = refs[:6]
     refs = refs[6:]
     if reduces:
-        line_out, refs = refs[0], refs[1:]
+        map_rows, refs = refs[0], refs[1:]
     deal_send, deal_recv, far_send, far_recv = refs[:4]
     if reduces:
-        got_ref, rotated_ref, eigen_sum, map_sum, map_got, map_rows = refs[4:10]
-        part_send, part_recv, sum_send, sum_recv = refs[10:14]
-        line_send, line_recv, pair_send, pair_recv = refs[14:18]
-        load_sem, basis_ref, eigen_ref = refs[18:]
+        got_ref, rotated_ref, eigen_sum, map_sum, map_got = refs[4:9]
+        part_send, part_recv, sum_send, sum_recv = refs[9:13]
+        pair_send, pair_recv, load_sem, basis_ref, eigen_ref = refs[13:]
     me = lax.axis_index("seq")
     size = lax.axis_size("seq")
     place = me % group
@@ -254,13 +319,16 @@
 
     def far(back):
         return pltpu.make_async_remote_copy(
-            src_ref=key_out.at[0],
+            src_ref=key_out.at[back - 1],
             dst_ref=key_out.at[back],
             send_sem=far_send.at[back],
             recv_sem=far_recv.at[back],
-            device_id={"seq": jnp.minimum(me + back * group, size - 1)},
+            device_id={"seq": (me + group) % size},
             device_id_type=MESH,
         )
+
+    def sends(back):
+        return (me + group < size) & (me >= (back - 1) * group)
 
     def part(step):
         peer = (me + step) % size
@@ -303,18 +371,6 @@
             send_sem=pair_send.at[which],
             recv_sem=pair_recv.at[which],
             device_id={"head": 1 - head},
-            device_id_type=MESH,
-        )
-
-    lines = size // group
-
-    def line(step, owner):
-        return pltpu.make_async_remote_copy(
-            src_ref=map_rows,
-            dst_ref=line_out.at[owner],
-            send_sem=line_send.at[step],
-            recv_sem=line_recv.at[step],
-            device_id={"seq": (me + step * group) % size},
             device_id_type=MESH,
         )
 
@@ -368,11 +424,9 @@
     keys[0].wait()
     for copy in keys[1:]:
         copy.wait_recv()
-    for back in range(1, span + 1):
-
-        @pl.when(me + back * group < size)
-        def send(back=back):
-            far(back).start()
+    @pl.when(sends(1))
+    def send():
+        far(1).start()
 
     wide = [deal(kind, mask) for kind in (1, 2) for mask in range(group)]
     for mask in range(group):
@@ -409,16 +463,24 @@
         map_copy.start()
         map_copy.wait()
         map_rows[...] = (map_sum[:, own] + map_got[...]).astype(jnp.bfloat16)
-        here = pltpu.make_async_copy(map_rows, line_out.at[me // group], line_recv.at[0])
-        here.start()
-        line_copies = [line(step, me // group) for step in range(1, lines)]
-        for copy in line_copies:
-            copy.start()
-        here.wait()
-        for step in range(1, lines):
-            line(step, (me // group + lines - step) % lines).wait_recv()
-        for copy in line_copies:
-            copy.wait_send()
+
+    for back in range(1, span + 1):
+
+        @pl.when(me >= back * group)
+        def arrived(back=back):
+            far(back).wait_recv()
+
+        if back < span:
+
+            @pl.when(sends(back + 1))
+            def pass_on(back=back):
+                far(back + 1).start()
+
+    for back in range(1, span + 1):
+
+        @pl.when(sends(back))
+        def sent(back=back):
+            far(back).wait_send()
 
     for copy in keys[1:]:
         copy.wait_send()
@@ -428,15 +490,6 @@
         else:
             copy.wait_recv()
             copy.wait_send()
-    for back in range(1, span + 1):
-
-        @pl.when(me + back * group < size)
-        def sent(back=back):
-            far(back).wait_send()
-
-        @pl.when(me >= back * group)
-        def arrived(back=back):
-            far(back).wait_recv()
 
 
 def exchange(query_rows, out_adjoint, key_rows, map_inputs, group, span):
@@ -455,20 +508,19 @@
     if reduces:
         part, basis, eigvals, turned = map_inputs
         size, depth, count = part.shape
-        lines, outputs = size // group, eigvals.shape[1]
+        outputs = eigvals.shape[1]
         own_map = (basis.shape[0], outputs // 2)
         args = tuple(map_inputs) + args
         in_specs = [in_vmem, anywhere, anywhere, in_vmem] + in_specs
-        outs.append(jax.ShapeDtypeStruct((lines,) + own_map, jnp.bfloat16))
+        outs.append(jax.ShapeDtypeStruct(own_map, jnp.bfloat16))
         scratch = scratch + [
             pltpu.VMEM(part.shape, part.dtype),
             pltpu.VMEM((size * depth, count), part.dtype),
             pltpu.VMEM((2, 8, 128), jnp.float32),
             pltpu.VMEM((basis.shape[0], outputs), jnp.float32),
             pltpu.VMEM(own_map, jnp.float32),
-            pltpu.VMEM(own_map, jnp.bfloat16),
         ]
-        scratch = scratch + [dma((size,))] * 4 + [dma((lines,))] * 2 + [dma((2,))] * 3
+        scratch = scratch + [dma((size,))] * 4 + [dma((2,))] * 3
         scratch = scratch + [pltpu.VMEM(basis.shape, basis.dtype), pltpu.VMEM(eigvals.shape, eigvals.dtype)]
         flops = 2 * basis.size * outputs
 
@@ -478,7 +530,7 @@
     got = pl.pallas_call(
         body,
         in_specs=in_specs,
-        out_specs=[anywhere] * len(outs),
+        out_specs=[anywhere] * 3 + [in_vmem] * (len(outs) - 3),
         out_shape=outs,
         scratch_shapes=scratch,
         compiler_params=pltpu.CompilerParams(
@@ -514,6 +566,7 @@
             basis_input, own_rows, (((0,), (1,)), ((), ())), preferred_element_type=jnp.float32
         )
         reduces = column_count % (16 * size) == 0 and lax.axis_size("head") == 2 and group in (2, 4)
+        reduces = reduces and size // group + 2 < 2 * group
         if reduces:
             part = part.astype(jnp.bfloat16).reshape(size, column_count // size, query_count)
 
@@ -527,12 +580,12 @@
 
     with jax.named_scope("spread_heads"):
         map_inputs = (part, basis_input, eigvals, all_turned_query) if reduces else None
-        queries, adjoints, keys, line_map = exchange(
+        queries, adjoints, keys, map_rows = exchange(
             query_rows, out_adjoint, key_rows, map_inputs, group, span
         )
 
     with jax.named_scope("attention"):
-        partials, token_map = attend(queries, adjoints, keys, line_map, key_span)
+        partials, token_map = attend(queries, adjoints, keys, map_rows, size, key_span)
         if reduces:
             token_map = token_map.reshape(row_count * size, -1)
 
@@ -555,10 +608,11 @@
         full_act = lax.all_gather(act, "head", axis=1, tiled=True)
         mapped = jnp.dot(full_act, token_map, preferred_element_type=jnp.float32)
         mapped, own_partial = lax.optimization_barrier((mapped, partials[0]))
-        adjoint_sum = own_partial.astype(jnp.float32)
-        for back in range(1, span + 1):
-            arrived = shifted(partials[back], -back * group)
-            adjoint_sum = adjoint_sum + arrived.astype(jnp.float32)
+        carried = shifted(partials[span], -group)
+        for back in range(span - 1, 0, -1):
+            passed = partials[back].astype(jnp.float32) + carried.astype(jnp.float32)
+            carried = shifted(passed.astype(jnp.bfloat16), -group)
+        adjoint_sum = own_partial.astype(jnp.float32) + carried.astype(jnp.float32)
         value_adjoint = adjoint_sum.astype(jnp.bfloat16)
 
     with jax.named_scope("gather_heads"):

time: 223 us -> 200 us (0.90)
  waiting for transfers between devices: 54.5 us -> 19.1 us
  Pallas kernels: 112 us -> 127 us
  blocking collectives: 22.5 us -> 20.2 us
    ppermute x2, waiting for transfers between devices: 49.4 us -> 13.7 us  [shifted(): return lax.ppermute(value, 'seq', pairs)]
    pallas_call x1, Pallas kernels: 42.5 us -> 75.4 us  [attend(): pl.pallas_call(body, grid=(group, 2), in_specs=in_specs, out_specs=out_sp...]
    pallas_call x1, Pallas kernels: 69.7 us -> 52 us  [exchange(): pl.pallas_call(body, in_specs=in_specs, out_specs=[anywhere] * 3 + [in_vm...]
    psum x1, blocking collectives: 17.7 us -> 15.4 us  [on_device(): return lax.psum(score, 'head')]
  transfers between devices with their start and end apart: 6 -> 6, of which waited for: 4 -> 5; matrix products, arithmetic and copies ran while one was open for 5% -> 6% of each run, Pallas kernels for 51% -> 64%
where the time goes in v5:
time: 200 us; the launch traced here: 198 us
  Pallas kernels  127 us (64%)
  blocking collectives  20.2 us (10%)
  waiting for transfers between devices  19.1 us (10%)
  between operations  13.5 us (7%)
  matrix products  8.3 us (4%)
  starting transfers between devices  5.29 us (3%)
  local copies, waits for them, and re-layouts  2.45 us (1%)
    pallas_call x1, Pallas kernels, attend(): pl.pallas_call(body, grid=(group, 2), in_specs=in_specs, out_specs=out_sp...  75.4 us
    pallas_call x1, Pallas kernels, exchange(): pl.pallas_call(body, in_specs=in_specs, out_specs=[anywhere] * 3 + [in_vm...  52 us
    psum x1, blocking collectives, on_device(): return lax.psum(score, 'head')  15.4 us
    ppermute x2, waiting for transfers between devices, shifted(): return lax.ppermute(value, 'seq', pairs)  13.7 us
    dot_general x1, matrix products, on_device(): mapped = jnp.dot(full_act, token_map, preferred_element_type=jnp.float32)  6.05 us
    ppermute x3, waiting for transfers between devices, swapped(): return lax.ppermute(value, 'seq', pairs)  4.63 us
  transfers between devices with their start and end apart: 6, of which 5 were waited for; matrix products, arithmetic and copies ran while one was open for 6% of the time, Pallas kernels for 64%

profile of v5, /device:TPU:5, one launch (start us, length us, event | category | flops | bytes accessed | tf_op | source)
XLA Modules:
  0.0 197.8 jit_solution(10143296354042717716)
XLA Ops:
  6.5 0.0 copy-start
  6.5 0.0 copy-start.1
  6.5 0.0 all-gather.2.cloned.1.call-start
  6.5 0.7 all-gather.2.cloned.1.call-update
  7.3 2.7 %all_gather.9 = bf16[64,4608]{1,0:T(8,128)(2,1)S(1)} all-gather(bf16[64,2304]{1,0:T(8,128)(2,1)} %param.16), channel_id=1, replica_groups=mesh['seq'=16,'head'=2] {'head'}, dimensions={1}, use_global_device_ids=true | all-gather | bytes 884736 | tf_op jit(solution)/shard_map/rotated_part/all_gather | solution.py:561
  10.0 1.8 fusion
  11.8 1.1 copy.10
  12.8 0.0 copy-done
  12.8 0.0 copy-done.1
  12.8 0.1 fusion.1
  13.0 2.1 %all_gather.10.refs_3_ = bf16[64,1024]{1,0:T(8,128)(2,1)} all-gather(bf16[64,512]{1,0:T(8,128)(2,1)S(1)} %bitcast.53), channel_id=1, replica_groups=mesh['seq'=16,'head'=2] {'head'}, dimensions={1}, use_global_device_ids=true | all-gather | bytes 196608 | tf_op jit(solution)/shard_map/turned_query/all_gather | solution.py:579
  15.1 52.0 %spread_heads.1 = (bf16[4,512,256]{2,1,0:T(8,128)(2,1)}, bf16[4,512,256]{2,1,0:T(8,128)(2,1)}, bf16[3,4,512,128]{3,2,1,0:T(8,128)(2,1)}, bf16[288,512]{1,0:T(8,128)(2,1)}) custom-call(bf16[16,144,64]{2,1,0:T(8,128)(2,1)} %bitcast.52, bf16[288,2304]{1,0:T(8,128)(2,1)} %refs_1_.1, bf16[2304,1024]{1,0:T(8,128)(2,1)} %refs_2_.1, ...), custom_call_target="tpu_custom_call" | custom-call | flops 1358954496 | bytes 4194304 | tf_op jit(solution)/shard_map/spread_heads/pallas_call | solution.py:530
  67.1 75.4 %attention.1 = (bf16[3,4,512,128]{3,2,1,0:T(8,128)(2,1)}, bf16[16,288,512]{2,1,0:T(8,128)(2,1)}) custom-call(bf16[4,512,256]{2,1,0:T(8,128)(2,1)} %get-tuple-element.13.refs_0_, bf16[4,512,256]{2,1,0:T(8,128)(2,1)} %get-tuple-element.14.refs_1_, bf16[3,4,512,128]{3,2,1,0:T(8,128)(2,1)} %get-tuple-element.15.refs_2_, bf16[288,512]{1,0:T(8,128)(2,1)} %get-tuple-element.16.refs_3_), custom_call_target="tpu_custom_call" | custom-call | flops 9663676416 | bytes 6291456 | tf_op jit(solution)/shard_map/attention/pallas_call | solution.py:253
  142.6 1.3 slice_bitcast_fusion
  143.8 1.3 collective-permute-start
  145.2 8.6 %collective-permute-done = bf16[4,512,128]{2,1,0:T(8,128)(2,1)S(1)} collective-permute-done((bf16[4,512,128]{2,1,0:T(8,128)(2,1)S(1)}, bf16[4,512,128]{2,1,0:T(8,128)(2,1)S(1)}, u32[]{:S(2)}, u32[]{:S(2)}) %collective-permute-start) | collective-permute-done | bytes 524320 | tf_op jit(solution)/shard_map/value_adjoint/ppermute | solution.py:21
  153.8 1.2 fusion.2
  155.0 1.3 collective-permute-start.1
  156.3 0.0 all-gather.2.cloned.1.call-done
  156.3 6.0 %convolution_bitcast_fusion = f32[512,512]{0,1:T(8,128)S(1)} fusion(bf16[4608,512]{1,0:T(8,128)(2,1)} %bitcast.57, bf16[512,4608]{1,0:T(8,128)(2,1)} %all-gather.2.cloned.1.call-done), kind=kOutput, calls=%fused_computation.2 | convolution fusion | flops 2415919104 | bytes 10485760 | tf_op jit(solution)/shard_map/value_adjoint/dot_general | solution.py:609
  162.3 5.1 %collective-permute-done.1 = bf16[4,512,128]{2,1,0:T(8,128)(2,1)S(1)} collective-permute-done((bf16[4,512,128]{2,1,0:T(8,128)(2,1)S(1)}, bf16[4,512,128]{2,1,0:T(8,128)(2,1)S(1)}, u32[]{:S(2)}, u32[]{:S(2)}) %collective-permute-start.1) | collective-permute-done | bytes 524320 | tf_op jit(solution)/shard_map/value_adjoint/ppermute | solution.py:21
  167.4 0.3 convolution_convert_fusion.1
  167.8 0.1 collective-permute-start.2
  167.9 2.5 %collective-permute-start.3 = (bf16[512,128]{0,1:T(8,128)(2,1)S(1)}, bf16[512,128]{0,1:T(8,128)(2,1)S(1)}, u32[]{:S(2)}, u32[]{:S(2)}) collective-permute-start(bf16[512,128]{0,1:T(8,128)(2,1)S(1)} %get-tuple-element.29), channel_id=1, source_target_pairs={{0,4},{2,6},{4,0},{6,2},{8,12},{10,14},{12,8},{14,10},{16,20},{18,... | collective-permute-start | bytes 393224 | tf_op jit(solution)/shard_map/gather_heads/ppermute | solution.py:27
  170.5 0.1 collective-permute-start.4
  170.5 1.2 collective-permute-done.2
  171.7 2.1 %collective-permute-done.3 = bf16[512,128]{0,1:T(8,128)(2,1)S(1)} collective-permute-done((bf16[512,128]{0,1:T(8,128)(2,1)S(1)}, bf16[512,128]{0,1:T(8,128)(2,1)S(1)}, u32[]{:S(2)}, u32[]{:S(2)}) %collective-permute-start.3) | collective-permute-done | bytes 131104 | tf_op jit(solution)/shard_map/gather_heads/ppermute | solution.py:27
  173.8 1.4 collective-permute-done.4
  175.2 0.1 pad_maximum_fusion
  175.3 0.2 multiply_reduce_fusion
  175.5 15.4 %psum.7 = f32[512]{0:T(512)} all-reduce(f32[512]{0:T(512)S(1)} %multiply_reduce_fusion), channel_id=1, replica_groups=mesh['seq'=16,'head'=2] {'head'}, use_global_device_ids=true, to_apply=%region_1.2 | all-reduce | flops 512 | bytes 4096 | tf_op jit(solution)/shard_map/influence/psum | solution.py:635
  (3 shorter events, 0.1 us)
Async XLA Ops:
  6.5 6.3 %copy-start = (bf16[4,128,128]{2,1,0:T(8,128)(2,1)S(1)}, bf16[4,128,128]{2,1,0:T(8,128)(2,1)}, u32[]{:S(2)}) copy-start(bf16[4,128,128]{2,1,0:T(8,128)(2,1)} %param.14) | copy-start | bytes 393220
  6.5 6.3 %copy-start.1 = (bf16[64,512]{1,0:T(8,128)(2,1)S(1)}, bf16[64,512]{1,0:T(8,128)(2,1)}, u32[]{:S(2)}) copy-start(bf16[64,512]{1,0:T(8,128)(2,1)} %param.17) | copy-start | bytes 196612
  6.5 149.7 %all-gather.2.cloned.1.call-start = ((), (), s32[]{:S(2)}) async-start(), calls=%async_computation | async-start | bytes 7077888 | tf_op jit(solution)/shard_map/value_adjoint/all_gather | solution.py:608
  143.8 9.9 %collective-permute-start = (bf16[4,512,128]{2,1,0:T(8,128)(2,1)S(1)}, bf16[4,512,128]{2,1,0:T(8,128)(2,1)S(1)}, u32[]{:S(2)}, u32[]{:S(2)}) collective-permute-start(bf16[4,512,128]{2,1,0:T(8,128)(2,1)S(1)} %get-tuple-element.21), channel_id=1, source_target_pairs={{8,0},{10,2},{12,4},{14,6},{16,8},{18,10},{20,12},{22,14},{24,16},... | collective-permute-start | bytes 1572872 | tf_op jit(solution)/shard_map/value_adjoint/ppermute | solution.py:21
  155.0 12.5 %collective-permute-start.1 = (bf16[4,512,128]{2,1,0:T(8,128)(2,1)S(1)}, bf16[4,512,128]{2,1,0:T(8,128)(2,1)S(1)}, u32[]{:S(2)}, u32[]{:S(2)}) collective-permute-start(bf16[4,512,128]{2,1,0:T(8,128)(2,1)S(1)} %fusion.2), channel_id=1, source_target_pairs={{8,0},{10,2},{12,4},{14,6},{16,8},{18,10},{20,12},{22,14},{24,16},... | collective-permute-start | bytes 1572872 | tf_op jit(solution)/shard_map/value_adjoint/ppermute | solution.py:21
  167.8 3.9 %collective-permute-start.2 = (bf16[512,128]{0,1:T(8,128)(2,1)S(1)}, bf16[512,128]{0,1:T(8,128)(2,1)S(1)}, u32[]{:S(2)}, u32[]{:S(2)}) collective-permute-start(bf16[512,128]{0,1:T(8,128)(2,1)S(1)} %get-tuple-element.30), channel_id=1, source_target_pairs={{0,2},{2,0},{4,6},{6,4},{8,10},{10,8},{12,14},{14,12},{16,18},{18,... | collective-permute-start | bytes 393224 | tf_op jit(solution)/shard_map/gather_heads/ppermute | solution.py:27
  167.9 5.9 %collective-permute-start.3 = (bf16[512,128]{0,1:T(8,128)(2,1)S(1)}, bf16[512,128]{0,1:T(8,128)(2,1)S(1)}, u32[]{:S(2)}, u32[]{:S(2)}) collective-permute-start(bf16[512,128]{0,1:T(8,128)(2,1)S(1)} %get-tuple-element.29), channel_id=1, source_target_pairs={{0,4},{2,6},{4,0},{6,2},{8,12},{10,14},{12,8},{14,10},{16,20},{18,... | collective-permute-start | bytes 393224 | tf_op jit(solution)/shard_map/gather_heads/ppermute | solution.py:27
  170.5 4.7 %collective-permute-start.4 = (bf16[512,128]{0,1:T(8,128)(2,1)S(1)}, bf16[512,128]{0,1:T(8,128)(2,1)S(1)}, u32[]{:S(2)}, u32[]{:S(2)}) collective-permute-start(bf16[512,128]{0,1:T(8,128)(2,1)S(1)} %get-tuple-element.28), channel_id=1, source_target_pairs={{0,6},{2,4},{4,2},{6,0},{8,14},{10,12},{12,10},{14,8},{16,22},{18,... | collective-permute-start | bytes 393224 | tf_op jit(solution)/shard_map/gather_heads/ppermute | solution.py:27
Sparse Core Ops, SparseCore 0:
  8.9 16.3 all-gather.1

commit v6 on v5

--- a/solution.py
+++ b/solution.py
@@ -27,8 +27,11 @@
     return lax.ppermute(value, "seq", pairs)
 
 
-def attend_kernel(key_span, query_ref, adjoint_ref, key_ref, rows_ref, out_ref, map_out, scratch):
-    weights, total_ref, sum_ref, line_send, line_recv, spread_send, spread_recv = scratch
+def attend_kernel(key_span, query_ref, adjoint_ref, key_ref, rows_ref, basis_ref, out_ref, map_out, scratch):
+    weights, total_ref, sum_ref = scratch[:3]
+    if rows_ref is not None:
+        leave_ref, come_ref, turned_ref, line_send, line_recv, spread_send, spread_recv = scratch[3:10]
+        back_send, back_recv, turn_send, turn_recv = scratch[10:]
     block = pl.program_id(0)
     member = pl.program_id(1)
     depth, group, rows, width = key_ref.shape
@@ -198,8 +201,66 @@
 
     @pl.when((block == group - 1) & (member == 1))
     def finish():
-        out_ref[...] = sum_ref[...].astype(out_ref.dtype)
-        if rows_ref is not None:
+        if rows_ref is None:
+            out_ref[...] = sum_ref[...].astype(out_ref.dtype)
+        else:
+            span = depth - 1
+            size = map_out.shape[0]
+
+            def returned(back):
+                return pltpu.make_async_remote_copy(
+                    src_ref=leave_ref.at[back - 1],
+                    dst_ref=come_ref.at[back - 1],
+                    send_sem=back_send.at[back],
+                    recv_sem=back_recv.at[back],
+                    device_id={"seq": (me + size - group) % size},
+                    device_id_type=MESH,
+                )
+
+            def absorb(back):
+                @pl.when((me + group < size) & (me >= (back - 1) * group))
+                def add():
+                    returned(back).wait_recv()
+                    sum_ref[back - 1] += come_ref[back - 1].astype(jnp.float32)
+
+            for back in range(span, 0, -1):
+                if back < span:
+                    absorb(back + 1)
+                leave_ref[back - 1] = sum_ref[back].astype(leave_ref.dtype)
+
+                @pl.when(me >= back * group)
+                def leave(back=back):
+                    returned(back).start()
+
+            absorb(1)
+            value = sum_ref[0].astype(jnp.bfloat16).reshape(group * rows, width)
+            turned = jnp.dot(value, basis_ref[place], preferred_element_type=jnp.float32)
+            turned_ref[...] = turned.astype(jnp.bfloat16).reshape(group, rows, width)
+
+            def dealt(mask, head):
+                return pltpu.make_async_remote_copy(
+                    src_ref=turned_ref.at[mask],
+                    dst_ref=out_ref.at[head],
+                    send_sem=turn_send.at[mask],
+                    recv_sem=turn_recv.at[mask],
+                    device_id={"seq": first + (place ^ mask)},
+                    device_id_type=MESH,
+                )
+
+            own = pltpu.make_async_copy(turned_ref.at[0], out_ref.at[place], turn_recv.at[0])
+            own.start()
+            for mask in range(1, group):
+                dealt(mask, place).start()
+            own.wait()
+            for mask in range(1, group):
+                dealt(mask, place ^ mask).wait_recv()
+                dealt(mask, place).wait_send()
+            for back in range(span, 0, -1):
+
+                @pl.when(me >= back * group)
+                def left(back=back):
+                    returned(back).wait_send()
+
             for stage in range(lines - 1):
                 for way in (0, 1):
                     sends, going, unused, unused_too = hop(stage, way)
@@ -215,19 +276,21 @@
                     (forward(owner) if mask == 3 else beside(owner, mask)).wait_send()
 
 
-def attend(query, adjoint, keys, map_rows, size, key_span):
+def attend(query, adjoint, keys, map_rows, basis_grad, size, key_span):
     depth, group, rows, width = keys.shape
     spreads = map_rows is not None
 
     def body(*refs):
         query_ref, adjoint_ref, key_ref = refs[:3]
         if spreads:
-            rows_ref, out_ref, map_out = refs[3:6]
-            scratch = refs[6:]
+            rows_ref, basis_ref, out_ref, map_out = refs[3:7]
+            scratch = refs[7:]
         else:
-            rows_ref, out_ref, map_out = None, refs[3], None
-            scratch = refs[4:] + (None,) * 4
-        attend_kernel(key_span, query_ref, adjoint_ref, key_ref, rows_ref, out_ref, map_out, scratch)
+            rows_ref, basis_ref, out_ref, map_out = None, None, refs[3], None
+            scratch = refs[4:]
+        attend_kernel(
+            key_span, query_ref, adjoint_ref, key_ref, rows_ref, basis_ref, out_ref, map_out, scratch
+        )
 
     tiles = 2 * group * (key_span + 1) * rows * rows
     whole = pl.BlockSpec((group, rows, width), lambda b, m: (0, 0, m))
@@ -244,11 +307,18 @@
     params = {}
     if spreads:
         lines = size // group
-        args, in_specs = args + (map_rows,), in_specs + [anywhere]
+        args = args + (map_rows, basis_grad)
+        in_specs = in_specs + [anywhere, pl.BlockSpec(basis_grad.shape, lambda b, m: (0, 0, 0))]
+        outs = [jax.ShapeDtypeStruct((group, rows, width), jnp.bfloat16)]
+        out_specs = [anywhere]
+        passing = pltpu.VMEM((depth - 1, group, rows, width), jnp.bfloat16)
+        scratch = scratch + [passing, passing, pltpu.VMEM((group, rows, width), jnp.bfloat16)]
         outs.append(jax.ShapeDtypeStruct((size,) + map_rows.shape, map_rows.dtype))
         out_specs.append(anywhere)
         scratch = scratch + [pltpu.SemaphoreType.DMA((2, lines))] * 2
         scratch = scratch + [pltpu.SemaphoreType.DMA((lines, group))] * 2
+        scratch = scratch + [pltpu.SemaphoreType.DMA((depth,))] * 2
+        scratch = scratch + [pltpu.SemaphoreType.DMA((group,))] * 2
         params = {"collective_id": 1, "has_side_effects": True}
     got = pl.pallas_call(
         body,
@@ -585,7 +655,9 @@
         )
 
     with jax.named_scope("attention"):
-        partials, token_map = attend(queries, adjoints, keys, map_rows, size, key_span)
+        attended, token_map = attend(
+            queries, adjoints, keys, map_rows, basis_grad, size, key_span
+        )
         if reduces:
             token_map = token_map.reshape(row_count * size, -1)
 
@@ -604,34 +676,38 @@
             map_rows = lax.psum_scatter(map_part, "head", scatter_dimension=1, tiled=True)
             token_map = lax.all_gather(map_rows.astype(jnp.bfloat16), "seq", axis=0, tiled=True)
 
-    with jax.named_scope("value_adjoint"):
+    with jax.named_scope("mapped"):
         full_act = lax.all_gather(act, "head", axis=1, tiled=True)
         mapped = jnp.dot(full_act, token_map, preferred_element_type=jnp.float32)
-        mapped, own_partial = lax.optimization_barrier((mapped, partials[0]))
-        carried = shifted(partials[span], -group)
-        for back in range(span - 1, 0, -1):
-            passed = partials[back].astype(jnp.float32) + carried.astype(jnp.float32)
-            carried = shifted(passed.astype(jnp.bfloat16), -group)
-        adjoint_sum = own_partial.astype(jnp.float32) + carried.astype(jnp.float32)
-        value_adjoint = adjoint_sum.astype(jnp.bfloat16)
-
-    with jax.named_scope("gather_heads"):
-        own_basis = lax.dynamic_index_in_dim(basis_grad, place, axis=0, keepdims=False)
-        turned = jnp.einsum(
-            "gte,ef->gtf", value_adjoint, own_basis, preferred_element_type=jnp.float32
-        ).astype(jnp.bfloat16)
-        parts = [turned[0]] + [swapped(turned[mask], group, mask) for mask in range(1, group)]
-        stacked = jnp.stack(parts)
-        turned_tokens = jnp.concatenate(
-            [
+
+    if reduces:
+        heads = [attended[head] for head in range(group)]
+    else:
+        with jax.named_scope("value_adjoint"):
+            carried = shifted(attended[span], -group)
+            for back in range(span - 1, 0, -1):
+                passed = attended[back].astype(jnp.float32) + carried.astype(jnp.float32)
+                carried = shifted(passed.astype(jnp.bfloat16), -group)
+            adjoint_sum = attended[0].astype(jnp.float32) + carried.astype(jnp.float32)
+            value_adjoint = adjoint_sum.astype(jnp.bfloat16)
+
+        with jax.named_scope("gather_heads"):
+            own_basis = lax.dynamic_index_in_dim(basis_grad, place, axis=0, keepdims=False)
+            turned = jnp.einsum(
+                "gte,ef->gtf", value_adjoint, own_basis, preferred_element_type=jnp.float32
+            ).astype(jnp.bfloat16)
+            parts = [turned[0]] + [swapped(turned[mask], group, mask) for mask in range(1, group)]
+            stacked = jnp.stack(parts)
+            heads = [
                 lax.dynamic_index_in_dim(stacked, place ^ head, axis=0, keepdims=False)
                 for head in range(group)
-            ],
-            axis=1,
-        )
+            ]
 
     with jax.named_scope("influence"):
-        score = jnp.sum(mapped * turned_tokens.astype(jnp.float32), axis=1)
+        score = jnp.zeros((local_rows,), jnp.float32)
+        for head in range(group):
+            own_map = mapped[:, head * width : (head + 1) * width]
+            score = score + jnp.sum(own_map * heads[head].astype(jnp.float32), axis=1)
         return lax.psum(score, "head")
 
 

time: 200 us -> 199 us (level)
  Pallas kernels: 127 us -> 152 us
  waiting for transfers between devices: 19.1 us -> 0.73 us
  starting transfers between devices: 5.29 us -> 0.01 us
    pallas_call x1, Pallas kernels: 75.4 us -> 99.5 us  [attend(): pl.pallas_call(body, grid=(group, 2), in_specs=in_specs, out_specs=out_sp...]
    ppermute x5 -> x0, waiting for transfers between devices: 18.3 us -> none  [the longest x2 13.7 us: shifted(): return lax.ppermute(value, 'seq', pairs)]
    ppermute x5 -> x0, starting transfers between devices: 5.29 us -> none  [the longest x3 2.71 us: swapped(): return lax.ppermute(value, 'seq', pairs)]
  transfers between devices with their start and end apart: 6 -> 1, of which waited for: 5 -> 0; matrix products, arithmetic and copies ran while one was open for 6% -> 2% of each run, Pallas kernels for 64% -> 77%
where the time goes in v6:
time: 199 us; the launch traced here: 196 us
  Pallas kernels  152 us (76%)
  blocking collectives  21.2 us (11%)
  between operations  13.5 us (7%)
  matrix products  7.9 us (4%)
    pallas_call x1, Pallas kernels, attend(): pl.pallas_call(body, grid=(group, 2), in_specs=in_specs, out_specs=out_sp...  99.5 us
    pallas_call x1, Pallas kernels, exchange(): pl.pallas_call(body, in_specs=in_specs, out_specs=[anywhere] * 3 + [in_vm...  52 us
    psum x1, blocking collectives, on_device(): return lax.psum(score, 'head')  16.4 us
    dot_general x1, matrix products, on_device(): mapped = jnp.dot(full_act, token_map, preferred_element_type=jnp.float32)  6 us
  transfers between devices with their start and end apart: 1, of which 0 were waited for; matrix products, arithmetic and copies ran while one was open for 2% of the time, Pallas kernels for 77%

profile of v6, /device:TPU:5, one launch (start us, length us, event | category | flops | bytes accessed | tf_op | source)
XLA Modules:
  0.0 196.3 jit_solution(13760569085592726617)
XLA Ops:
  6.5 0.0 copy-start
  6.5 0.0 copy-start.2
  6.5 0.0 all-gather.2.cloned.1.call-start
  6.5 0.7 all-gather.2.cloned.1.call-update
  7.3 2.7 %all_gather.9 = bf16[64,4608]{1,0:T(8,128)(2,1)S(1)} all-gather(bf16[64,2304]{1,0:T(8,128)(2,1)} %param.16), channel_id=1, replica_groups=mesh['seq'=16,'head'=2] {'head'}, dimensions={1}, use_global_device_ids=true | all-gather | bytes 884736 | tf_op jit(solution)/shard_map/rotated_part/all_gather | solution.py:631
  10.0 1.8 fusion
  11.8 1.1 copy.10
  12.9 0.0 copy-done
  12.9 0.0 copy-done.2
  12.9 0.1 fusion.1
  13.0 2.1 %all_gather.10.refs_3_ = bf16[64,1024]{1,0:T(8,128)(2,1)} all-gather(bf16[64,512]{1,0:T(8,128)(2,1)S(1)} %bitcast.36), channel_id=1, replica_groups=mesh['seq'=16,'head'=2] {'head'}, dimensions={1}, use_global_device_ids=true | all-gather | bytes 196608 | tf_op jit(solution)/shard_map/turned_query/all_gather | solution.py:649
  15.1 52.0 %spread_heads.1 = (bf16[4,512,256]{2,1,0:T(8,128)(2,1)}, bf16[4,512,256]{2,1,0:T(8,128)(2,1)}, bf16[3,4,512,128]{3,2,1,0:T(8,128)(2,1)}, bf16[288,512]{1,0:T(8,128)(2,1)}) custom-call(bf16[16,144,64]{2,1,0:T(8,128)(2,1)} %bitcast.35, bf16[288,2304]{1,0:T(8,128)(2,1)} %refs_1_.1, bf16[2304,1024]{1,0:T(8,128)(2,1)} %refs_2_.1, ...), custom_call_target="tpu_custom_call" | custom-call | flops 1358954496 | bytes 4194304 | tf_op jit(solution)/shard_map/spread_heads/pallas_call | solution.py:600
  67.1 99.5 %attention.1 = (bf16[4,512,128]{2,1,0:T(8,128)(2,1)}, bf16[16,288,512]{2,1,0:T(8,128)(2,1)}) custom-call(bf16[4,512,256]{2,1,0:T(8,128)(2,1)} %get-tuple-element.11.refs_0_, bf16[4,512,256]{2,1,0:T(8,128)(2,1)} %get-tuple-element.12.refs_1_, bf16[3,4,512,128]{3,2,1,0:T(8,128)(2,1)} %get-tuple-element.13.refs_2_, bf16[288,512]{1,0:T(8,128)(2,1)} %get-tuple-element.14.refs_3_, ...), custom_call_target="tpu_custom_call" | custom-call | flops 9663676416 | bytes 6291456 | tf_op jit(solution)/shard_map/attention/pallas_call | solution.py:323
  166.6 0.0 all-gather.2.cloned.1.call-done
  166.7 0.0 copy-start.1
  166.7 6.0 %convolution_bitcast_fusion = f32[512,512]{1,0:T(8,128)S(1)} fusion(bf16[512,4608]{1,0:T(8,128)(2,1)} %all-gather.2.cloned.1.call-done, bf16[4608,512]{1,0:T(8,128)(2,1)} %bitcast.37), kind=kOutput, calls=%fused_computation.2 | convolution fusion | flops 2415919104 | bytes 10485760 | tf_op jit(solution)/shard_map/mapped/dot_general | solution.py:681
  172.7 0.0 copy-done.1
  172.7 0.4 fusion.4
  173.1 16.4 %psum.7 = f32[512]{0:T(512)} all-reduce(f32[512]{0:T(512)S(1)} %add_add_fusion), channel_id=1, replica_groups=mesh['seq'=16,'head'=2] {'head'}, use_global_device_ids=true, to_apply=%region_4.0 | all-reduce | flops 512 | bytes 4096 | tf_op jit(solution)/shard_map/influence/psum | solution.py:711
  (2 shorter events, 0.0 us)
Async XLA Ops:
  6.5 6.3 %copy-start = (bf16[64,512]{1,0:T(8,128)(2,1)S(1)}, bf16[64,512]{1,0:T(8,128)(2,1)}, u32[]{:S(2)}) copy-start(bf16[64,512]{1,0:T(8,128)(2,1)} %param.17) | copy-start | bytes 196612
  6.5 6.3 %copy-start.2 = (bf16[4,128,128]{2,1,0:T(8,128)(2,1)S(1)}, bf16[4,128,128]{2,1,0:T(8,128)(2,1)}, u32[]{:S(2)}) copy-start(bf16[4,128,128]{2,1,0:T(8,128)(2,1)} %refs_4_.3) | copy-start | bytes 393220
  6.5 160.1 %all-gather.2.cloned.1.call-start = ((), (), s32[]{:S(2)}) async-start(), calls=%async_computation | async-start | bytes 7077888 | tf_op jit(solution)/shard_map/mapped/all_gather | solution.py:680
  166.7 6.0 %copy-start.1 = (bf16[4,512,128]{2,1,0:T(8,128)(2,1)S(1)}, bf16[4,512,128]{2,1,0:T(8,128)(2,1)}, u32[]{:S(2)}) copy-start(bf16[4,512,128]{2,1,0:T(8,128)(2,1)} %get-tuple-element.16) | copy-start | bytes 1572868
Sparse Core Ops, SparseCore 0:
  8.9 16.3 all-gather.1
